TPU v7x, 32 devices: a whole 2x2x4 slice. The times are simulated.
32 devices in a mesh: dp: 8 (over z, x), mp: 4 (over y, core).
Axes of the slice: x: 2, y: 2, z: 4, core: 2. Of those that a mesh axis runs over, the one named last changes fastest.
Arguments:
- text_in: bfloat16 [8704, 768], P(('dp', 'mp')), may hold values from -6 to 6
- segment_ids: int32 [136, 64], P('dp'), may hold values from 0 to 3, never falling along the last dimension, each value on 1 to 40 neighbouring positions
- valid_lengths: int32 [136], P('dp'), may hold values from 40 to 64
- text_grad: bfloat16 [8704, 768], P(('dp', 'mp')), may hold values from -6 to 6
- attn_gain: bfloat16 [768], replicated, may hold values from 0.5 to 1.5
- attn_shift: bfloat16 [768], replicated, may hold values from -3 to 3
- qkv_weight: bfloat16 [768, 3, 768], P(None, None, 'mp'), may hold values from -0.21875 to 0.21875
- qv_bias: bfloat16 [2, 768], P(None, 'mp'), may hold values from -3 to 3
- out_weight: bfloat16 [768, 768], P('mp'), may hold values from -0.875 to 0.875
- out_bias: bfloat16 [768], replicated, may hold values from -3 to 3
- mlp_gain: bfloat16 [768], replicated, may hold values from 0.5 to 1.5
- mlp_shift: bfloat16 [768], replicated, may hold values from -3 to 3
- fc1_weight: bfloat16 [768, 3072], P(None, 'mp'), may hold values from -0.21875 to 0.21875
- fc1_bias: bfloat16 [3072], P('mp'), may hold values from -3 to 3
- fc2_weight: bfloat16 [3072, 768], P('mp'), may hold values from -0.21875 to 0.21875
- fc2_bias: bfloat16 [768], replicated, may hold values from -3 to 3
- images: bfloat16 [12800, 768], P(('dp', 'mp')), may hold values from -6 to 6
- img_attn_gain: bfloat16 [768], replicated, may hold values from 0.5 to 1.5
- img_attn_shift: bfloat16 [768], replicated, may hold values from -3 to 3
- img_qkv_weight: bfloat16 [768, 3, 768], P(None, None, 'mp'), may hold values from -0.21875 to 0.21875
- img_qv_bias: bfloat16 [2, 768], P(None, 'mp'), may hold values from -3 to 3
- img_out_weight: bfloat16 [768, 768], P('mp'), may hold values from -1.25 to 1.25
- img_out_bias: bfloat16 [768], replicated, may hold values from -3 to 3
- img_mlp_gain: bfloat16 [768], replicated, may hold values from 0.5 to 1.5
- img_mlp_shift: bfloat16 [768], replicated, may hold values from -3 to 3
- img_fc1_weight: bfloat16 [768, 3072], P(None, 'mp'), may hold values from -0.21875 to 0.21875
- img_fc1_bias: bfloat16 [3072], P('mp'), may hold values from -3 to 3
- img_fc2_weight: bfloat16 [3072, 768], P('mp'), may hold values from -0.21875 to 0.21875
- img_fc2_bias: bfloat16 [768], replicated, may hold values from -3 to 3
Outputs:
- text_out: bfloat16 [8704, 768], P(('dp', 'mp'))
- image_out: bfloat16 [12800, 768], P(('dp', 'mp'))
- text_in_grad: bfloat16 [8704, 768], P(('dp', 'mp'))
- grad_attn_gain: float32 [768], replicated
- grad_attn_shift: float32 [768], replicated
- grad_qkv_weight: float32 [768, 3, 768], P(None, None, 'mp')
- grad_qv_bias: float32 [2, 768], P(None, 'mp')
- grad_out_weight: float32 [768, 768], P('mp')
- grad_out_bias: float32 [768], replicated
- grad_mlp_gain: float32 [768], replicated
- grad_mlp_shift: float32 [768], replicated
- grad_fc1_weight: float32 [768, 3072], P(None, 'mp')
- grad_fc1_bias: float32 [3072], P('mp')
- grad_fc2_weight: float32 [3072, 768], P('mp')
- grad_fc2_bias: float32 [768], replicated
Inputs may be any that keep to these rules, and one draw needn't show every extreme that they name: `segment_ids`: along each row the number never falls. `valid_lengths`: positions at or past it in a row are padding.
All inputs are finite; a program needn't handle non-finite values.
Results may differ from a plain program's by a relative error of at most 0.015.
Values may be sent and summed in bfloat16 or wider, within the bound.
No kernel may reach another device: no remote copies, remote signals or barrier semaphores. Data moves between devices by JAX's collectives and lax.ppermute only.
A program may use at most 128 MiB of HBM per device.

v0:
```python
import functools

import jax
import jax.numpy as jnp
from jax import lax
from jax.experimental import pallas as pl
from jax.experimental.pallas import tpu as pltpu
from jax.sharding import PartitionSpec as P

HEAD = 64
IMG_SEQ = 50
EPS = 1e-05
BF = jnp.bfloat16
F32 = jnp.float32
SCALE = HEAD ** (-0.5)
NEG = -1000000000.0
ROOT = 0.7978845608028654
CUBE = 0.044715

NN = (((1,), (0,)), ((), ()))
NT = (((1,), (1,)), ((), ()))
TN = (((0,), (0,)), ((), ()))


def dot(a, b, dims=NN):
    return lax.dot_general(a, b, dims, preferred_element_type=F32)


def shape(*dims, dtype=BF):
    return jax.ShapeDtypeStruct(dims, dtype)


class Line:
    def __init__(self):
        self.token = None

    def __call__(self, body, outs, args, scratch=(), vmem=16, untouched=(), scalars=(), after=(),
                 same=None, outside=False):
        args = list(args)
        real = len(args)
        args += list(after) + ([] if self.token is None else [self.token])
        given = len(args)

        def in_space(i):
            if i >= real or i in untouched:
                return pl.ANY
            return pltpu.SMEM if i in scalars else pltpu.VMEM

        def run(*refs):
            body(*refs[:real], *refs[given : given + len(outs)], *refs[given + len(outs) + 1 :])

        out_space = pl.ANY if outside or same is not None else pltpu.VMEM
        results = pl.pallas_call(
            run,
            out_shape=(*outs, shape(8, 128, dtype=F32)),
            in_specs=[pl.BlockSpec(memory_space=in_space(i)) for i in range(given)],
            out_specs=tuple(
                pl.BlockSpec(memory_space=space) for space in [out_space] * len(outs) + [pl.ANY]
            ),
            scratch_shapes=list(scratch),
            input_output_aliases={} if same is None else {same: 0},
            compiler_params=pltpu.CompilerParams(vmem_limit_bytes=vmem * 1024 * 1024),
            cost_estimate=pl.CostEstimate(flops=1, bytes_accessed=1, transcendentals=0),
        )(*args)
        self.token = results[-1]
        return results[:-1] if len(outs) > 1 else results[0]

    def hold(self, value):
        return self(lambda *refs: None, [shape(*value.shape, dtype=value.dtype)], [value],
                    untouched=(0,), same=0)


def norm(x):
    centred = x - jnp.mean(x, axis=-1, keepdims=True)
    inverse = lax.rsqrt(jnp.mean(centred * centred, axis=-1, keepdims=True) + EPS)
    return centred * inverse, inverse


def norm_back(upstream, gain, normed, inverse):
    scaled = upstream * gain
    first = jnp.mean(scaled, axis=-1, keepdims=True)
    second = jnp.mean(scaled * normed, axis=-1, keepdims=True)
    return inverse * (scaled - first - normed * second)


def head_marks(width, dtype):
    lane = lax.broadcasted_iota(jnp.int32, (1, width), 1) // HEAD
    return [jnp.where(lane == h, 1.0, 0.0).astype(dtype) for h in range(width // HEAD)]


def stack_heads(rows, marks):
    return jnp.concatenate([rows * mark for mark in marks], axis=0)


def fold_heads(stacked, count, marks):
    total = stacked[:count] * marks[0]
    for h in range(1, len(marks)):
        total += stacked[h * count : (h + 1) * count] * marks[h]
    return total


def masked_scores(q_stack, k, mask):
    raw = dot(q_stack, k, NT)
    heads = raw.shape[0] // mask.shape[0]
    raw = raw.reshape(heads, mask.shape[0], mask.shape[1])
    return jnp.where(mask[None] > 0, raw * SCALE, NEG)


def softmax_parts(scores):
    peak = jnp.max(scores, axis=-1, keepdims=True)
    weights = jnp.exp(scores - peak)
    return weights, jnp.sum(weights, axis=-1, keepdims=True)


def attend(q, k, v, mask):
    count = q.shape[0]
    scores = masked_scores(stack_heads(q, head_marks(q.shape[1], BF)), k, mask)
    weights, total = softmax_parts(scores)
    probs = (weights / total).astype(BF).reshape(-1, mask.shape[1])
    return fold_heads(dot(probs, v), count, head_marks(q.shape[1], F32)).astype(BF)


def attend_back(q, k, v, grad, mask):
    count = q.shape[0]
    low = head_marks(q.shape[1], BF)
    q_stack = stack_heads(q, low)
    g_stack = stack_heads(grad, low)
    weights, total = softmax_parts(masked_scores(q_stack, k, mask))
    probs = weights / total
    prob_grad = dot(g_stack, v, NT).reshape(probs.shape)
    centre = jnp.sum(prob_grad * probs, axis=-1, keepdims=True)
    score_grad = (probs * (prob_grad - centre)).astype(BF).reshape(-1, mask.shape[1])
    probs_low = probs.astype(BF).reshape(-1, mask.shape[1])
    v_grad = dot(probs_low, g_stack, TN)
    q_grad = fold_heads(dot(score_grad, k), count, head_marks(q.shape[1], F32)) * SCALE
    k_grad = dot(score_grad, q_stack, TN) * SCALE
    return q_grad.astype(BF), k_grad.astype(BF), v_grad.astype(BF)


def gelu_parts(v):
    square = v * v
    t = jnp.tanh(ROOT * (v + CUBE * (square * v)))
    half = 0.5 * (1.0 + t)
    slope = half + 0.5 * v * (1.0 - t * t) * (ROOT * (1.0 + 3.0 * CUBE * square))
    return v * half, slope


def repeat(count, body):
    def step(i, carry):
        body(i)
        return carry

    lax.fori_loop(0, count, step, 0)


def lanes(index, size):
    return pl.ds(pl.multiple_of(index * size, 128), size)


def chunk_start(index, size):
    return pl.ds(pl.multiple_of(index * size, 16), size)


def row_blocks(count, length, first):
    blocks = []
    for low, high in ((0, first), (first, count)):
        row = low
        if (high - low) % 2:
            blocks.append((row * length, length))
            row += 1
        while row < high:
            blocks.append((row * length, 2 * length))
            row += 2
    return blocks


def mask_kernel(blocks, segments, lengths, mask):
    length = segments.shape[1]
    square = (length, length)
    key = lax.broadcasted_iota(jnp.int32, square, 1)
    diagonal = key == lax.broadcasted_iota(jnp.int32, square, 0)
    mask[...] = jnp.zeros(mask.shape, F32)
    for start, count in blocks:
        for place in range(count // length):
            row = start // length + place
            along = jnp.broadcast_to(segments[row : row + 1, :].astype(F32), square)
            seen = (along == along.T) & ((key < lengths[row]) | diagonal)
            low = start + place * length
            mask[low : low + length, place * length : (place + 1) * length] = jnp.where(
                seen, 1.0, 0.0
            )


def bundle_kernel(w_t, out_w, qv, bundle, held, sems):
    width = qv.shape[1]
    held[...] = jnp.zeros(held.shape, held.dtype)
    held[0:2, :width] = qv[...]
    start, copies = 0, []
    for k, piece in enumerate((w_t, out_w, held)):
        rows = piece.shape[0]
        copies.append(pltpu.make_async_copy(piece, bundle.at[start : start + rows], sems.at[k]))
        copies[-1].start()
        start += rows
    for copy in copies:
        copy.wait()


ATTN_GAIN, ATTN_SHIFT, OUT_BIAS, MLP_GAIN, MLP_SHIFT, FC2_BIAS, FC1_BIAS = range(7)


def vectors_kernel(*refs):
    *items, text, image = refs
    for out, own in ((text, items[: len(items) // 2]), (image, items[len(items) // 2 :])):
        out[...] = jnp.zeros(out.shape, F32)
        for k, item in enumerate(own):
            out[k : k + 1, :] = item[...].astype(F32).reshape(1, -1)


def vector(vectors, index):
    return vectors[index : index + 1, :]


def project(x_pair, vectors, w_t, bias, rows, qkv, bias_rows, at):
    size = x_pair.shape[1]
    width = bias.shape[1]
    gain, shift = vector(vectors, ATTN_GAIN), vector(vectors, ATTN_SHIFT)
    bias_rows[...] = jnp.zeros(bias_rows.shape, F32)
    bias_rows[0:1, :] = bias[...].astype(F32)[0:1]
    bias_rows[2:3, :] = bias[...].astype(F32)[1:2]

    def normalize(i):
        normed, _ = norm(x_pair[i].astype(F32))
        rows[chunk_start(i, size), :] = (normed * gain + shift).astype(BF)

    def part(i):
        value = dot(rows[...], w_t[chunk_start(i, width), :], NT) + bias_rows[pl.ds(i, 1), :]
        qkv[i, at, :] = value.astype(BF)

    repeat(2, normalize)
    repeat(3, part)


def own_rows_kernel(x0, x1, vectors, w_t, bias, rows_out, qkv, x_pair, bias_rows):
    core = lax.axis_index("mp") % 2
    x_pair[core] = x0[...]
    x_pair[1 - core] = x1[...]
    project(x_pair, vectors, w_t, bias, rows_out, qkv, bias_rows, slice(None))


def far_operands_kernel(grad, bundle, packed, sem):
    size = grad.shape[0]
    part = packed.shape[0] - size
    copy = pltpu.make_async_copy(
        bundle.at[chunk_start(lax.axis_index("dp"), part)], packed.at[size:], sem
    )
    copy.start()
    packed[:size] = grad[...]
    copy.wait()


def unpack_kernel(packed, grad, part):
    size = grad.shape[0]
    grad[...] = packed[:size]
    part[...] = packed[size:]


def block_loop(blocks, body, unroll=False):
    if unroll:
        for start, tokens in blocks:
            body(pl.ds(start, tokens), tokens)
        return
    singles = [b for b in blocks if b[1] != blocks[-1][1]]
    pairs = [b[0] for b in blocks if b[1] == blocks[-1][1]]
    count = blocks[-1][1]
    for start, tokens in singles:
        body(pl.ds(start, tokens), tokens)

    def pair(i):
        start = pairs[0] + i * count
        for k in range(1, len(pairs)):
            gap = pairs[k] - pairs[k - 1] - count
            if gap:
                start = start + jnp.where(i >= k, gap, 0)
        body(pl.ds(pl.multiple_of(start, 16), count), count)

    repeat(len(pairs), pair)


def attn_forward_kernel(blocks, x2, x3, qkv_own, vectors, w_t, bias, out_w, mask,
                        rows_out, qkv, ctx, keep0, keep1, send0, send1, x_pair, bias_rows):
    me = lax.axis_index("mp")
    core, side = me % 2, me // 2
    size, dim = x2.shape
    x_pair[core] = x2[...]
    x_pair[1 - core] = x3[...]
    far = chunk_start(1 - side, 2 * size)
    project(x_pair, vectors, w_t, bias, rows_out, qkv, bias_rows, far)
    own = chunk_start(side, 2 * size)
    for part in range(3):
        qkv[part, own, :] = qkv_own[part]

    def block(at, count):
        ctx[at, :] = attend(qkv[0, at, :], qkv[1, at, :], qkv[2, at, :], mask[at, :count])

    block_loop(blocks, block, unroll=True)

    def columns(i):
        cols = lanes(i, 256)
        weight = out_w[:, cols]
        for half, (keep, send) in enumerate(((keep0, send0), (keep1, send1))):
            theirs = ctx[chunk_start(2 * half + 1 - core, size), :]
            send[:, cols] = dot(theirs, weight).astype(BF)
            mine = ctx[chunk_start(2 * half + core, size), :]
            keep[:, cols] = dot(mine, weight).astype(BF)

    repeat(dim // 256, columns)


def add_kernel(a, b, out):
    out[...] = (a[...].astype(F32) + b[...].astype(F32)).astype(BF)


def add_pair_kernel(a0, b0, a1, b1, out0, out1):
    for a, b, out in ((a0, b0, out0), (a1, b1, out1)):
        out[...] = (a[...].astype(F32) + b[...].astype(F32)).astype(BF)


def add_split_kernel(a, b, keep, send):
    half = keep.shape[0]
    keep[...] = (a[:half].astype(F32) + b[:half].astype(F32)).astype(BF)
    send[...] = (a[half:].astype(F32) + b[half:].astype(F32)).astype(BF)


def join_kernel(a, b, out):
    half = a.shape[0]
    out[:half] = a[...]
    out[half:] = b[...]


def chosen(half, own, far):
    return jnp.where(lax.axis_index("mp") // 2 == half, own[...], far[...])


def after_attn_kernel(half, x0, x2, mine, theirs, vectors, after_out, rows):
    total = mine[...].astype(F32) + theirs[...].astype(F32)
    stream = chosen(half, x0, x2).astype(F32) + (total + vector(vectors, OUT_BIAS))
    after_out[...] = stream
    normed, _ = norm(stream)
    rows[...] = (normed * vector(vectors, MLP_GAIN) + vector(vectors, MLP_SHIFT)).astype(BF)


def mlp_kernel(half, rows0, rows1, t0, t1, t2, t3, w1, vectors, w2,
               act, hid_grad, br_keep, br_send, mg_keep, mg_send, rows, grad):
    size, dim = rows0.shape
    rows[:size, :] = rows0[...]
    rows[size:, :] = rows1[...]
    grad[:size, :] = chosen(half, t0, t2)
    grad[size:, :] = chosen(half, t1, t3)

    def units(i):
        cols = lanes(i, 256)
        hidden = dot(rows[...], w1[:, cols]) + vectors[FC1_BIAS : FC1_BIAS + 1, cols]
        active, slope = gelu_parts(hidden)
        act[:, cols] = active.astype(BF)
        active_grad = dot(grad[...], w2[cols, :], NT)
        hid_grad[:, cols] = (active_grad * slope).astype(BF)

    def columns(i):
        cols = lanes(i, 256)
        value = dot(hid_grad[...], w1[cols, :], NT).astype(BF)
        mg_keep[:, cols] = value[:size]
        mg_send[:, cols] = value[size:]
        value = dot(act[...], w2[:, cols]).astype(BF)
        br_keep[:, cols] = value[:size]
        br_send[:, cols] = value[size:]

    repeat(w1.shape[1] // 256, units)
    repeat(dim // 256, columns)


def mlp_back_kernel(half, after, mine, theirs, t0, t2, vectors, after_grad, out_grad, sums):
    normed, inverse = norm(after[...])
    rows_grad = mine[...].astype(F32) + theirs[...].astype(F32)
    sums[...] = jnp.concatenate(
        [
            jnp.sum(rows_grad * normed, axis=0, keepdims=True),
            jnp.sum(rows_grad, axis=0, keepdims=True),
        ],
        axis=0,
    )
    value = chosen(half, t0, t2).astype(F32) + norm_back(
        rows_grad, vector(vectors, MLP_GAIN), normed, inverse
    )
    after_grad[...] = value
    out_grad[...] = value.astype(BF)


def attn_back_first_kernel(blocks, og_mine, og_other, qkv, mask, out_w, og, cg, pg):
    core = lax.axis_index("mp") % 2
    size = og_mine.shape[0]
    og[chunk_start(core, size), :] = og_mine[...]
    og[chunk_start(1 - core, size), :] = og_other[...]
    cg[...] = dot(og[...], out_w[...], NT).astype(BF)

    def block(at, count):
        grads = attend_back(
            qkv[0, at, :], qkv[1, at, :], qkv[2, at, :], cg[at, :], mask[at, :count]
        )
        for part in range(3):
            pg[part, at, :] = grads[part]

    block_loop(blocks, block)


def attn_back_second_kernel(blocks, og_mine, og_other, cg_first, pg_first, qkv, mask, out_w, w_t,
                            og, pg, p0, p1, p2, p3, cg):
    me = lax.axis_index("mp")
    core = me % 2
    size, dim = og_mine.shape
    width = out_w.shape[0]
    half = 2 * size
    done = pg_first.shape[1]
    og[chunk_start(core, size), :] = og_mine[...]
    og[chunk_start(1 - core, size), :] = og_other[...]
    cg[half:, :] = dot(og[...], out_w[...], NT).astype(BF)
    cg[:half, :] = cg_first[...]
    for part in range(3):
        pg[part, :done, :] = pg_first[part]

    def block(at, count):
        grads = attend_back(
            qkv[0, at, :], qkv[1, at, :], qkv[2, at, :], cg[at, :], mask[at, :count]
        )
        for part in range(3):
            pg[part, at, :] = grads[part]

    block_loop(blocks, block, unroll=True)

    def columns(i):
        cols = lanes(i, 256)
        for j, out in ((3, p3), (1, p1), (2, p2), (0, p0)):
            at = chunk_start(me ^ j, size)
            total = dot(pg[0, at, :], w_t[:width, cols])
            for part in range(1, 3):
                total += dot(pg[part, at, :], w_t[part * width : (part + 1) * width, cols])
            out[:, cols] = total.astype(BF)

    repeat(dim // 256, columns)


def place_in(relative, order):
    place = 0
    for k, bit in enumerate(order):
        place = place + ((relative // bit) % 2) * 2 ** (len(order) - 1 - k)
    return place


def place_of(relative, orders):
    core = lax.axis_index("mp") % 2
    return jnp.where(core == 0, place_in(relative, orders[0]), place_in(relative, orders[1]))


def emit(full, outs, orders):
    if orders is None:
        outs[0][...] = full[...]
        return
    keep, send = outs
    blocks = 2 ** len(orders[0])
    size = full.shape[0] // blocks
    here = lax.axis_index("dp")

    def block(b):
        place = place_of(here ^ b, orders)
        value = full[chunk_start(b, size), :].astype(BF)

        @pl.when(place < blocks // 2)
        def _():
            keep[chunk_start(place, size), :] = value

        @pl.when(place >= blocks // 2)
        def _():
            send[chunk_start(place - blocks // 2, size), :] = value

    repeat(blocks, block)


def weight_product(left, right, full):
    def block(i):
        at = pl.ds(pl.multiple_of(i * 256, 256), 256)
        full[at, :] = dot(left[:, lanes(i, 256)], right[...], TN)

    repeat(left.shape[1] // 256, block)


def row_sum(ref):
    return jnp.sum(ref[...].astype(F32), axis=0, keepdims=True)


def fc2_weight_kernel(orders, act0, act1, t0, t1, t2, t3, *rest):
    *outs, sums, full, left, right = rest
    size = t0.shape[0]
    side = lax.axis_index("mp") // 2
    left[chunk_start(side, 2 * size), :] = act0[...]
    left[chunk_start(1 - side, 2 * size), :] = act1[...]
    for k, t in enumerate((t0, t1, t2, t3)):
        right[k * size : (k + 1) * size, :] = t[...]
    weight_product(left, right, full)
    emit(full, outs, orders)
    sums[...] = row_sum(right)


def fc1_weight_kernel(orders, rows00, rows01, rows10, rows11, hg0, hg1, *rest):
    *outs, sums, full, left, right = rest
    size = rows00.shape[0]
    for k, rows in enumerate((rows00, rows01, rows10, rows11)):
        left[k * size : (k + 1) * size, :] = rows[...]
    right[: 2 * size, :] = hg0[...]
    right[2 * size :, :] = hg1[...]
    weight_product(left, right, full)
    emit(full, outs, orders)
    sums[...] = row_sum(right)


def attn_weights_kernel(orders, ctx, og0, og1, rows_own, rows_far, pg, *rest):
    *outs, out_sum, qv_sum, full, rows, og = rest
    half = og0.shape[0]
    side = lax.axis_index("mp") // 2
    width = ctx.shape[1]
    rows[chunk_start(side, half), :] = rows_own[...]
    rows[chunk_start(1 - side, half), :] = rows_far[...]
    og[:half, :] = og0[...]
    og[half:, :] = og1[...]

    def part(i):
        full[chunk_start(i, width), :] = dot(pg[i], rows[...], TN)

    repeat(3, part)
    full[3 * width :, :] = dot(ctx[...], og[...], TN)
    emit(full, outs, orders)
    out_sum[...] = row_sum(og)
    qv_sum[...] = jnp.concatenate(
        [jnp.sum(pg[part].astype(F32), axis=0, keepdims=True) for part in (0, 2)], axis=0
    )


def gather_blocks_kernel(orders, low_half, high_half, out):
    blocks = 2 ** len(orders[0])
    size = 2 * low_half.shape[0] // blocks
    here = lax.axis_index("dp")

    def block(b):
        place = place_of(here ^ b, orders)
        at = chunk_start(place % (blocks // 2), size)
        value = jnp.where(place < blocks // 2, low_half[at, :], high_half[at, :])
        out[chunk_start(b, size), :] = value.astype(F32)

    repeat(blocks, block)


def gather_attn_kernel(orders, low_half, high_half, qkv, out_w, full):
    gather_blocks_kernel(orders, low_half, high_half, full)
    rows = qkv.shape[0]
    qkv[...] = full[:rows, :]
    out_w[...] = full[rows:, :]


def input_grad_kernel(x, mine, theirs, after_grad0, after_grad1, vectors, grad, sums):
    side = lax.axis_index("mp") // 2
    normed, inverse = norm(x[...].astype(F32))
    rows_grad = mine[...].astype(F32) + theirs[...].astype(F32)
    sums[...] = jnp.concatenate(
        [
            jnp.sum(rows_grad * normed, axis=0, keepdims=True),
            jnp.sum(rows_grad, axis=0, keepdims=True),
        ],
        axis=0,
    )
    after_grad = jnp.where(side == 0, after_grad0[...], after_grad1[...])
    value = after_grad + norm_back(
        rows_grad, vector(vectors, ATTN_GAIN), normed, inverse
    )
    grad[...] = value.astype(BF)


def text_out_kernel(mine0, mine1, theirs, after0, after1, vectors, out):
    side = lax.axis_index("mp") // 2
    after = jnp.where(side == 0, after0[...], after1[...])
    mine = jnp.where(side == 0, mine0[...], mine1[...])
    branch = mine.astype(F32) + theirs[...].astype(F32)
    out[...] = (after + (branch + vector(vectors, FC2_BIAS))).astype(BF)


def far_branch_kernel(br0, br1, far):
    far[...] = jnp.where(lax.axis_index("mp") // 2 == 0, br1[...], br0[...])


def add_rows_kernel(a, b, out):
    out[...] = a[...] + b[...]


def norm_sums_kernel(mlp0, mlp1, attn, out):
    out[0:2, :] = mlp0[...] + mlp1[...]
    out[2:4, :] = attn[...]


def small_kernel(sums, far, fc2, fc1, out_b, qv, out):
    width = qv.shape[1]
    out[0:2, :] = sums[0:2, :]
    out[2:4, :] = sums[2:4, :] + far[2:4, :]
    out[4:5, :] = fc2[...]
    out[5:6, :] = fc1[...]
    out[6:7, :] = out_b[...]
    out[7:8, :] = jnp.zeros((1, out.shape[1]), F32)
    out[7:8, :width] = qv[0:1, :]
    out[7:8, 2 * width : 3 * width] = qv[1:2, :]


def image_windows(count, images):
    windows = []
    per = 4
    for low in range(0, images, per):
        start = (low * IMG_SEQ + 15) // 16 * 16 if low else 0
        end = min(count, ((low + per) * IMG_SEQ + 15) // 16 * 16)
        if low + per >= images:
            end = count
        key_start = start // IMG_SEQ * IMG_SEQ // 16 * 16
        key_end = min(count, ((end - 1) // IMG_SEQ * IMG_SEQ + IMG_SEQ + 15) // 16 * 16)
        windows.append((start, end, key_start, key_end))
    return windows


def image_attn_kernel(first, last, shards, x, vectors, *rest):
    rest = list(rest)
    before = None if first else rest.pop(0)
    sources, rest = rest[:shards], rest[shards:]
    *outs, total, rows, context, bundle, sems = rest
    count, dim = x.shape
    images = count // IMG_SEQ
    width = dim // 4
    copies = [
        pltpu.make_async_copy(source.at[0 : 4 * width + 16], bundle.at[s], sems.at[s])
        for s, source in enumerate(sources)
    ]
    for copy in copies:
        copy.start()
    normed, _ = norm(x[...].astype(F32))
    rows[...] = (normed * vector(vectors, ATTN_GAIN) + vector(vectors, ATTN_SHIFT)).astype(BF)
    total[...] = jnp.zeros((count, dim), F32) if first else before[...]
    windows = image_windows(count, images)

    def shard(s):
        for k in range(shards):

            @pl.when(s == k)
            def _():
                copies[k].wait()

        weights = bundle.at[s]
        bias = weights[4 * width : 4 * width + 16, :].astype(F32)
        q = (dot(rows[...], weights[:width, :], NT) + bias[0:1, :width]).astype(BF)
        k = dot(rows[...], weights[width : 2 * width, :], NT).astype(BF)
        v = (dot(rows[...], weights[2 * width : 3 * width, :], NT) + bias[1:2, :width]).astype(BF)
        for q_low, q_high, k_low, k_high in windows:
            extent = (q_high - q_low, k_high - k_low)
            q_image = (lax.broadcasted_iota(jnp.int32, extent, 0) + q_low) // IMG_SEQ
            k_image = (lax.broadcasted_iota(jnp.int32, extent, 1) + k_low) // IMG_SEQ
            mask = jnp.where(q_image == k_image, 1.0, 0.0)
            context[q_low:q_high, :] = attend(
                q[q_low:q_high], k[k_low:k_high], v[k_low:k_high], mask
            )

        def columns(i):
            cols = lanes(i, 256)
            total[:, cols] += dot(context[...], bundle[s, 3 * width : 4 * width, cols])

        repeat(dim // 256, columns)

    repeat(shards, shard)
    if not last:
        outs[0][...] = total[...]
        return
    after_ref, rows_ref = outs
    after = x[...].astype(F32) + (total[...] + vector(vectors, OUT_BIAS))
    after_ref[...] = after
    normed, _ = norm(after)
    rows_ref[...] = (normed * vector(vectors, MLP_GAIN) + vector(vectors, MLP_SHIFT)).astype(BF)


def image_mlp_kernel(r0, r1, r2, r3, w1, vectors, w2, p0, p1, p2, p3, rows, active):
    size, dim = r0.shape
    for k, r in enumerate((r3, r1, r2, r0)):
        rows[k * size : (k + 1) * size, :] = r[...]

    def units(i):
        cols = lanes(i, 256)
        hidden = dot(rows[...], w1[:, cols]) + vectors[FC1_BIAS : FC1_BIAS + 1, cols]
        active[:, cols] = gelu_parts(hidden)[0].astype(BF)

    def columns(i):
        cols = lanes(i, 256)
        value = dot(active[...], w2[:, cols]).astype(BF)
        for k, p in enumerate((p3, p1, p2, p0)):
            p[:, cols] = value[k * size : (k + 1) * size]

    repeat(w1.shape[1] // 256, units)
    repeat(dim // 256, columns)


def image_out_kernel(after, mine, theirs, vectors, out):
    branch = mine[...].astype(F32) + theirs[...].astype(F32)
    out[...] = (after[...] + (branch + vector(vectors, FC2_BIAS))).astype(BF)


def core_swap(x):
    return lax.ppermute(x, "mp", [(i, i ^ 1) for i in range(lax.axis_size("mp"))])


def side_swap(x):
    return lax.ppermute(x, "mp", [(i, i ^ 2) for i in range(lax.axis_size("mp"))])


def dp_swap(x, bits):
    n_dp, n_mp = lax.axis_size("dp"), lax.axis_size("mp")
    pairs = [
        (d * n_mp + m, (d ^ bits[m % 2]) * n_mp + m) for d in range(n_dp) for m in range(n_mp)
    ]
    return lax.ppermute(x, ("dp", "mp"), pairs)


def per_device(
    text_in,
    segment_ids,
    valid_lengths,
    text_grad,
    attn_gain,
    attn_shift,
    qkv_weight,
    qv_bias,
    out_weight,
    out_bias,
    mlp_gain,
    mlp_shift,
    fc1_weight,
    fc1_bias,
    fc2_weight,
    fc2_bias,
    images,
    img_attn_gain,
    img_attn_shift,
    img_qkv_weight,
    img_qv_bias,
    img_out_weight,
    img_out_bias,
    img_mlp_gain,
    img_mlp_shift,
    img_fc1_weight,
    img_fc1_bias,
    img_fc2_weight,
    img_fc2_bias,
):
    size, dim = text_in.shape
    row_count, length = segment_ids.shape
    width = qkv_weight.shape[2]
    n_dp = lax.axis_size("dp")
    tokens = 4 * size

    w_t = qkv_weight.transpose(1, 2, 0).reshape(3 * width, dim)
    img_w_t = img_qkv_weight.transpose(1, 2, 0).reshape(3 * width, dim)
    used = 4 * width + 16
    total_rows = -(-used // (16 * n_dp)) * 16 * n_dp
    part_rows = total_rows // n_dp

    rows_first = 2 * size // length
    blocks = row_blocks(row_count, length, rows_first)
    blocks_first = [b for b in blocks if b[0] < rows_first * length]
    blocks_rest = [b for b in blocks if b[0] >= rows_first * length]

    run = Line()
    chunk = shape(size, dim)
    pair = shape(2 * size, dim)

    x0 = text_in
    x2 = side_swap(x0)
    x1 = core_swap(x0)
    vectors, img_vectors = run(
        vectors_kernel,
        [shape(8, dim, dtype=F32)] * 2,
        [
            attn_gain, attn_shift, out_bias, mlp_gain, mlp_shift, fc2_bias, fc1_bias,
            img_attn_gain, img_attn_shift, img_out_bias, img_mlp_gain, img_mlp_shift,
            img_fc2_bias, img_fc1_bias,
        ],
    )
    project_scratch = [pltpu.VMEM((2, size, dim), BF), pltpu.VMEM((8, width), F32)]
    rows_own, qkv_own = run(
        own_rows_kernel,
        [pair, shape(3, 2 * size, width)],
        [x0, x1, vectors, w_t, qv_bias],
        scratch=project_scratch,
    )
    mask = run(
        functools.partial(mask_kernel, blocks),
        [shape(tokens, 2 * length, dtype=F32)],
        [segment_ids, valid_lengths],
        scalars=(1,),
    )
    bundle = run(
        bundle_kernel,
        [shape(total_rows, dim)],
        [img_w_t, img_out_weight, img_qv_bias],
        scratch=[
            pltpu.VMEM((total_rows - 4 * width, dim), BF),
            pltpu.SemaphoreType.DMA((3,)),
        ],
        untouched=(0, 1),
        outside=True,
    )
    t1 = core_swap(text_grad)
    own_other = core_swap(bundle)
    image_rows = images.shape[0]

    def image_attn(first, last, operands, outs, sources):
        args = [images, img_vectors, *operands, *sources]
        shards = len(sources)
        return run(
            functools.partial(image_attn_kernel, first, last, shards),
            outs,
            args,
            scratch=[
                pltpu.VMEM((image_rows, dim), F32),
                pltpu.VMEM((image_rows, dim), BF),
                pltpu.VMEM((image_rows, width), BF),
                pltpu.VMEM((shards, used, dim), BF),
                pltpu.SemaphoreType.DMA((shards,)),
            ],
            untouched=tuple(range(len(args) - shards, len(args))),
        )

    image_wide = shape(image_rows, dim, dtype=F32)
    image_total = image_attn(True, False, [], [image_wide], [bundle])
    t0 = text_grad
    packed = run(
        far_operands_kernel,
        [shape(size + part_rows, dim)],
        [t0, bundle],
        scratch=[pltpu.SemaphoreType.DMA(())],
        untouched=(1,),
        after=[x2],
    )
    x2 = run.hold(x2)
    x3 = core_swap(x2)
    packed = side_swap(packed)

    rows_far, qkv, ctx, keep0, keep1, send0, send1 = run(
        functools.partial(attn_forward_kernel, blocks),
        [pair, shape(3, tokens, width), shape(tokens, width)] + [chunk] * 4,
        [x2, x3, qkv_own, vectors, w_t, qv_bias, out_weight, mask],
        scratch=project_scratch,
    )

    def after_attn(half, mine, theirs):
        stream, rows = run(
            functools.partial(after_attn_kernel, half),
            [shape(size, dim, dtype=F32), chunk],
            [x0, x2, mine, theirs, vectors],
        )
        return stream, rows, core_swap(rows)

    def mlp(half, rows, rows_other):
        return run(
            functools.partial(mlp_kernel, half),
            [pair] * 2 + [chunk] * 4,
            [rows, rows_other, t0, t1, t2, t3, fc1_weight, vectors, fc2_weight],
            scratch=[pltpu.VMEM((2 * size, dim), BF)] * 2,
        )

    def mlp_back(half, stream, mine, theirs):
        value, low, sums = run(
            functools.partial(mlp_back_kernel, half),
            [shape(size, dim, dtype=F32), chunk, shape(2, dim, dtype=F32)],
            [stream, mine, theirs, t0, t2, vectors],
        )
        return value, low, core_swap(low), sums

    other0, other1 = core_swap(send0), core_swap(send1)
    mine0 = run(add_kernel, [chunk], [keep0, other0], after=[packed])
    theirs0 = side_swap(mine0)
    t2, far_part = run(unpack_kernel, [chunk, shape(part_rows, dim)], [packed])
    t3 = core_swap(t2)
    far_bundle = lax.all_gather(far_part, "dp", axis=0, tiled=True)
    image_total = image_attn(False, False, [image_total], [image_wide], [own_other])
    mine1 = run(add_kernel, [chunk], [keep1, other1], after=[theirs0])
    theirs1 = side_swap(mine1)
    stream0, rows0, rows_other0 = after_attn(0, mine0, theirs0)
    act0, hg0, brk0, brs0, mgk0, mgs0 = mlp(0, rows0, rows_other0)
    mg0, br0 = run(
        add_pair_kernel,
        [chunk] * 2,
        [mgk0, core_swap(mgs0), brk0, core_swap(brs0)],
        after=[theirs1],
    )
    mg_theirs0 = side_swap(mg0)
    stream1, rows1, rows_other1 = after_attn(1, mine1, theirs1)
    act1, hg1, brk1, brs1, mgk1, mgs1 = mlp(1, rows1, rows_other1)
    mg1, br1 = run(
        add_pair_kernel,
        [chunk] * 2,
        [mgk1, core_swap(mgs1), brk1, core_swap(brs1)],
        after=[mg_theirs0],
    )
    mg_theirs1 = side_swap(mg1)
    after_grad0, og0, og_other0, mlp_sums0 = mlp_back(0, stream0, mg0, mg_theirs0)

    bits = [2**k for k in range(n_dp.bit_length() - 1)]
    orders = (tuple(bits), tuple(bits[1:] + bits[:1]))
    plain = 2 ** len(bits) != n_dp or dim % (16 * n_dp) != 0
    if plain:
        orders = None
    grad_shapes = [shape(dim, dim, dtype=F32)] if plain else [shape(dim // 2, dim)] * 2

    class Sum:
        def __init__(self, parts, last, sizes):
            self.last, self.sizes, self.step = last, sizes, 0
            if plain:
                total = lax.psum(parts[0], "dp")
                cuts = [sum(sizes[: i + 1]) for i in range(len(sizes) - 1)]
                self.result = jnp.split(total, cuts, axis=0)
                return
            self.keep = parts[0]
            self.exchange(parts[1], 0)

        def exchange(self, send, k):
            self.arriving = dp_swap(send, (orders[0][k], orders[1][k]))

        def advance(self):
            if plain:
                return
            self.step += 1
            rows, levels = self.keep.shape[0], len(bits)
            if self.step < levels:
                self.keep, send = run(
                    add_split_kernel, [shape(rows // 2, dim)] * 2, [self.keep, self.arriving]
                )
                self.exchange(send, self.step)
            elif self.step < 2 * levels:
                if self.step == levels:
                    self.keep = run(add_kernel, [shape(rows, dim)], [self.keep, self.arriving])
                else:
                    self.keep = run(
                        join_kernel, [shape(2 * rows, dim)], [self.keep, self.arriving]
                    )
                self.exchange(self.keep, 2 * levels - 1 - self.step)
            else:
                got = run(
                    functools.partial(self.last, orders),
                    [shape(n, dim, dtype=F32) for n in self.sizes],
                    [self.keep, self.arriving],
                    scratch=[pltpu.VMEM((dim, dim), F32)] if len(self.sizes) > 1 else [],
                )
                self.result = got if len(self.sizes) > 1 else [got]

    def fc_weight(kernel, args):
        *parts, sums = run(
            functools.partial(kernel, orders),
            grad_shapes + [shape(1, dim, dtype=F32)],
            args,
            scratch=[pltpu.VMEM((dim, dim), F32)] + [pltpu.VMEM((tokens, dim), BF)] * 2,
        )
        return Sum(parts, gather_blocks_kernel, (dim,)), sums

    fc2_sum, fc2_bias_sum = fc_weight(fc2_weight_kernel, [act0, act1, t0, t1, t2, t3])

    og_first, cg_first, pg_first = run(
        functools.partial(attn_back_first_kernel, blocks_first),
        [pair, shape(2 * size, width), shape(3, rows_first * length, width)],
        [og0, og_other0, qkv, mask, out_weight],
    )
    fc1_sum, fc1_bias_sum = fc_weight(
        fc1_weight_kernel, [rows0, rows_other0, rows1, rows_other1, hg0, hg1]
    )
    after_grad1, og1, og_other1, mlp_sums1 = mlp_back(1, stream1, mg1, mg_theirs1)
    fc2_sum.advance()
    og_second, pg, p0, p1, p2, p3 = run(
        functools.partial(attn_back_second_kernel, blocks_rest),
        [pair, shape(3, tokens, width)] + [chunk] * 4,
        [og1, og_other1, cg_first, pg_first, qkv, mask, out_weight, w_t],
        scratch=[pltpu.VMEM((tokens, width), BF)],
    )
    p_other1, p_other3 = core_swap(p1), core_swap(p3)
    *parts, out_sum, qv_sum = run(
        functools.partial(attn_weights_kernel, orders),
        grad_shapes + [shape(1, dim, dtype=F32), shape(2, width, dtype=F32)],
        [ctx, og_first, og_second, rows_own, rows_far, pg],
        scratch=[pltpu.VMEM((dim, dim), F32)] + [pltpu.VMEM((tokens, dim), BF)] * 2,
    )
    attn_sum = Sum(parts, gather_attn_kernel, (3 * width, width))
    p_mine, to_side = run(add_pair_kernel, [chunk] * 2, [p0, p_other1, p2, p_other3])
    p_theirs = side_swap(to_side)
    fc1_sum.advance()
    fc2_sum.advance()

    far_bundle = run.hold(far_bundle)
    far_other = core_swap(far_bundle)
    attn_sum.advance()
    image_chunk = shape(image_rows, dim)
    img_after, img_rows0 = image_attn(
        False, True, [image_total], [image_wide, image_chunk], [far_bundle, far_other]
    )
    img_rows2 = side_swap(img_rows0)
    img_rows1 = core_swap(img_rows0)
    fc1_sum.advance()
    fc2_sum.advance()
    text_in_grad, attn_sums = run(
        input_grad_kernel,
        [chunk, shape(2, dim, dtype=F32)],
        [text_in, p_mine, p_theirs, after_grad0, after_grad1, vectors],
    )
    small = run(norm_sums_kernel, [shape(4, dim, dtype=F32)], [mlp_sums0, mlp_sums1, attn_sums])
    attn_sum.advance()
    small = run(add_rows_kernel, [shape(4, dim, dtype=F32)], [small, core_swap(small)])
    small_far = side_swap(small)
    fc1_sum.advance()
    fc2_sum.advance()
    img_rows2 = run.hold(img_rows2)
    img_rows3 = core_swap(img_rows2)
    attn_sum.advance()
    i0, i1, i2, i3 = run(
        image_mlp_kernel,
        [image_chunk] * 4,
        [img_rows0, img_rows1, img_rows2, img_rows3, img_fc1_weight, img_vectors, img_fc2_weight],
        scratch=[pltpu.VMEM((4 * image_rows, dim), BF)] * 2,
        vmem=24,
    )
    i_mine, i_side = run(
        add_pair_kernel, [image_chunk] * 2, [i0, core_swap(i1), i2, core_swap(i3)]
    )
    i_theirs = side_swap(i_side)
    small = run(
        small_kernel,
        [shape(8, dim, dtype=F32)],
        [small, small_far, fc2_bias_sum, fc1_bias_sum, out_sum, qv_sum],
    )
    if plain:
        small_far = lax.psum(small, "dp")
        small = jnp.zeros_like(small)
    else:
        small_far = dp_swap(small, (bits[0], bits[0]))
    fc1_sum.advance()
    fc2_sum.advance()
    attn_sum.advance()
    if not plain:
        for bit in bits[1:]:
            small = run(add_rows_kernel, [shape(8, dim, dtype=F32)], [small, small_far])
            small_far = dp_swap(small, (bit, bit))
    image_out = run(
        image_out_kernel, [image_chunk], [img_after, i_mine, i_theirs, img_vectors]
    )
    far_branch = run(far_branch_kernel, [chunk], [br0, br1])
    br_theirs = side_swap(far_branch)
    fc1_sum.advance()
    fc2_sum.advance()
    attn_sum.advance()
    text_out = run(
        text_out_kernel,
        [chunk],
        [br0, br1, br_theirs, stream0, stream1, vectors],
    )
    for total in (fc2_sum, fc1_sum, attn_sum):
        while not plain and total.step < 2 * len(bits):
            total.advance()
    small = run(add_rows_kernel, [shape(8, dim, dtype=F32)], [small, small_far])
    (grad_fc2_weight,) = fc2_sum.result
    (grad_fc1_weight,) = fc1_sum.result
    grad_qkv, grad_out_weight = attn_sum.result
    return (
        text_out,
        image_out,
        text_in_grad,
        small[2],
        small[3],
        grad_qkv.reshape(3, width, dim).transpose(2, 0, 1),
        jnp.stack([small[7, :width], small[7, 2 * width : 3 * width]]),
        grad_out_weight,
        small[6],
        small[0],
        small[1],
        grad_fc1_weight,
        small[5],
        grad_fc2_weight,
        small[4],
    )


def solution(mesh):
    in_specs = (
        P(("dp", "mp"), None),
        P("dp", None),
        P("dp"),
        P(("dp", "mp"), None),
        P(),
        P(),
        P(None, None, "mp"),
        P(None, "mp"),
        P("mp", None),
        P(),
        P(),
        P(),
        P(None, "mp"),
        P("mp"),
        P("mp", None),
        P(),
        P(("dp", "mp"), None),
        P(),
        P(),
        P(None, None, "mp"),
        P(None, "mp"),
        P("mp", None),
        P(),
        P(),
        P(),
        P(None, "mp"),
        P("mp"),
        P("mp", None),
        P(),
    )
    out_specs = (
        P(("dp", "mp"), None),
        P(("dp", "mp"), None),
        P(("dp", "mp"), None),
        P(),
        P(),
        P(None, None, "mp"),
        P(None, "mp"),
        P("mp", None),
        P(),
        P(),
        P(),
        P(None, "mp"),
        P("mp"),
        P("mp", None),
        P(),
    )
    return jax.shard_map(
        per_device, mesh=mesh, in_specs=in_specs, out_specs=out_specs, check_vma=False
    )
```

profile of v0, /device:TPU:0, one launch (start us, length us, event | category | flops | bytes accessed | tf_op | source)
XLA Modules:
  0.0 260.1 jit_solution(3456278028672492907)
XLA Ops:
  33.6 5.1 %shard_map.395 = (bf16[544,768]{1,0:T(8,128)(2,1)S(1)}, bf16[3,1088,192]{2,1,0:T(8,128)(2,1)S(1)}, bf16[1088,192]{1,0:T(8,128)(2,1)S(1)}, bf16[272,768]{1,0:T(8,...) custom-call(bf16[272,768]{1,0:T(8,128)(2,1)S(1)} %get-tuple-element., ...), custom_call_target="tpu_custom_call" | custom-call | flops 1 | bytes 1 | tf_op jit(solution)/shard_map/pallas_call | solution.py:53
  40.9 6.6 %collective-permute-done.4.refs_2_.refs_0_ = bf16[384,768]{1,0:T(8,128)(2,1)S(1)} collective-permute-done((bf16[384,768]{1,0:T(8,128)(2,1)S(1)}, bf16[384,768]{1,0:T(8,128)(2,1)S(1)}, u32[]{:S(2)}, u32[]{:S(2)}) %collective-permute-start.4) | collective-permute-done | bytes 589856 | tf_op jit(solution)/shard_map/ppermute | solution.py:719
  52.1 6.5 %collective-permute-done.5.refs_2_.refs_3_ = bf16[272,768]{1,0:T(8,128)(2,1)S(1)} collective-permute-done((bf16[272,768]{1,0:T(8,128)(2,1)S(1)}, bf16[272,768]{1,0:T(8,128)(2,1)S(1)}, u32[]{:S(2)}, u32[]{:S(2)}) %collective-permute-start.5) | collective-permute-done | bytes 417824 | tf_op jit(solution)/shard_map/ppermute | solution.py:719
  61.7 5.5 %shard_map.401 = (bf16[544,768]{1,0:T(8,128)(2,1)S(1)}, bf16[544,768]{1,0:T(8,128)(2,1)S(1)}, bf16[272,768]{1,0:T(8,128)(2,1)S(1)}, bf16[272,768]{1,0:T(8,128)(2...) custom-call(bf16[272,768]{1,0:T(8,128)(2,1)S(1)} %get-tuple-element.212.refs_0_, ...), custom_call_target="tpu_custom_call" | custom-call | flops 1 | bytes 1 | tf_op jit(solution)/shard_map/pallas_call | solution.py:53
  81.1 4.8 %shard_map.404 = (bf16[544,768]{1,0:T(8,128)(2,1)S(1)}, bf16[544,768]{1,0:T(8,128)(2,1)S(1)}, bf16[272,768]{1,0:T(8,128)(2,1)S(1)}, bf16[272,768]{1,0:T(8,128)(2...) custom-call(bf16[272,768]{1,0:T(8,128)(2,1)S(1)} %get-tuple-element.223.refs_0_.refs_2_, ...), custom_call_target="tpu_custom_call" | custom-call | flops 1 | bytes 1 | tf_op jit(solution)/shard_map/pallas_call | solution.py:53
  86.5 4.9 %collective-permute-done.17.refs_4_.refs_2_ = bf16[272,768]{1,0:T(8,128)(2,1)S(1)} collective-permute-done((bf16[272,768]{1,0:T(8,128)(2,1)S(1)}, bf16[272,768]{1,0:T(8,128)(2,1)S(1)}, u32[]{:S(2)}, u32[]{:S(2)}) %collective-permute-start.17) | collective-permute-done | bytes 417824 | tf_op jit(solution)/shard_map/ppermute | solution.py:719
  99.2 3.5 %shard_map.408 = (bf16[544,768]{1,0:T(8,128)(2,1)S(1)}, bf16[544,192]{1,0:T(8,128)(2,1)S(1)}, bf16[3,512,192]{2,1,0:T(8,128)(2,1)S(1)}, f32[8,128]{1,0:T(8,128)S(1)}) custom-call(bf16[272,768]{1,0:T(8,128)(2,1)S(1)} %get-tuple-element.245.refs_0_, bf16[272,768]{1,0:T(8,128)(2,1)S(1)} %collective-permute-done.20.refs_1_, bf16[3,1088,192]{2,1,0:T(8,128)(2,1)S(1)} %copy-done.4, ...), custom_call_target="tpu_custom_call" | custom-call | flops 1 | bytes 1 | tf_op jit(solution)/shard_map/pallas_call | solution.py:53
  108.4 4.4 %collective-permute-done.18.refs_1_ = bf16[384,768]{1,0:T(8,128)(2,1)S(1)} collective-permute-done((bf16[384,768]{1,0:T(8,128)(2,1)S(1)}, bf16[384,768]{1,0:T(8,128)(2,1)S(1)}, u32[]{:S(2)}, u32[]{:S(2)}) %collective-permute-start.18) | collective-permute-done | bytes 589856 | tf_op jit(solution)/shard_map/ppermute | solution.py:727
  113.0 5.0 %shard_map.412 = (bf16[544,768]{1,0:T(8,128)(2,1)S(1)}, bf16[3,1088,192]{2,1,0:T(8,128)(2,1)S(1)}, bf16[272,768]{1,0:T(8,128)(2,1)S(1)}, bf16[272,768]{1,0:T(8,1...) custom-call(bf16[272,768]{1,0:T(8,128)(2,1)S(1)} %get-tuple-element.255.refs_0_, ...), custom_call_target="tpu_custom_call" | custom-call | flops 1 | bytes 1 | tf_op jit(solution)/shard_map/pallas_call | solution.py:53
  118.0 3.9 %collective-permute-start.24 = (bf16[272,768]{1,0:T(8,128)(2,1)S(1)}, bf16[272,768]{1,0:T(8,128)(2,1)S(1)}, u32[]{:S(2)}, u32[]{:S(2)}) collective-permute-start(bf16[272,768]{1,0:T(8,128)(2,1)S(1)} %get-tuple-element.260), channel_id=1, source_target_pairs={{0,1},{1,0},{2,3},{3,2},{4,5},{5,4},{6,7},{7,6},{8,9},{9,8},{10,11... | collective-permute-start | bytes 1253384 | tf_op jit(solution)/shard_map/ppermute | solution.py:715
  121.9 3.8 %shard_map.413 = (bf16[384,768]{1,0:T(8,128)(2,1)S(1)}, bf16[384,768]{1,0:T(8,128)(2,1)S(1)}, f32[1,768]{1,0:T(1,128)S(1)}, f32[2,192]{1,0:T(2,128)S(1)}, f32[8,128]{1,0:T(8,128)S(1)}) custom-call(bf16[1088,192]{1,0:T(8,128)(2,1)S(1)} %copy-done.50, bf16[544,768]{1,0:T(8,128)(2,1)S(1)} %get-tuple-element.264.refs_1_, ...), custom_call_target="tpu_custom_call" | custom-call | flops 1 | bytes 1 | tf_op jit(solution)/shard_map/pallas_call | solution.py:53
  127.6 3.8 %collective-permute-done.21.refs_1_ = bf16[192,768]{1,0:T(8,128)(2,1)S(1)} collective-permute-done((bf16[192,768]{1,0:T(8,128)(2,1)S(1)}, bf16[192,768]{1,0:T(8,128)(2,1)S(1)}, u32[]{:S(2)}, u32[]{:S(2)}) %collective-permute-start.21) | collective-permute-done | bytes 294944 | tf_op jit(solution)/shard_map/ppermute | solution.py:727
  133.6 8.4 %collective-permute-done.27.refs_1_ = bf16[384,768]{1,0:T(8,128)(2,1)S(1)} collective-permute-done((bf16[384,768]{1,0:T(8,128)(2,1)}, bf16[384,768]{1,0:T(8,128)(2,1)S(1)}, u32[]{:S(2)}, u32[]{:S(2)}) %collective-permute-start.27) | collective-permute-done | bytes 589856 | tf_op jit(solution)/shard_map/ppermute | solution.py:727
  142.2 6.0 %shard_map.419 = (f32[400,768]{1,0:T(8,128)S(1)}, bf16[400,768]{1,0:T(8,128)(2,1)S(1)}, f32[8,128]{1,0:T(8,128)S(1)}) custom-call(bf16[400,768]{1,0:T(8,128)(2,1)S(1)} %copy-done.7, f32[8,768]{1,0:T(8,128)S(1)} %get-tuple-element.192.refs_1_.refs_5_.refs_3_, f32[400,768]{1,0:T(8,128)S(1)} %copy-done.33, bf16[896,768]{1,0:T(8,128)(2,1)} %get-tuple-element.274.refs_3_, ...), custom_call_target="tpu_custom_call" | custom-call | flops 1 | bytes 1 | tf_op jit(solution)/shard_map/pallas_call | solution.py:53
  153.3 5.8 %collective-permute-done.31.refs_1_ = bf16[192,768]{1,0:T(8,128)(2,1)S(1)} collective-permute-done((bf16[192,768]{1,0:T(8,128)(2,1)S(1)}, bf16[192,768]{1,0:T(8,128)(2,1)S(1)}, u32[]{:S(2)}, u32[]{:S(2)}) %collective-permute-start.31) | collective-permute-done | bytes 294944 | tf_op jit(solution)/shard_map/ppermute | solution.py:727
  160.8 3.5 %collective-permute-done.30.refs_1_ = bf16[96,768]{1,0:T(8,128)(2,1)S(1)} collective-permute-done((bf16[96,768]{1,0:T(8,128)(2,1)S(1)}, bf16[96,768]{1,0:T(8,128)(2,1)S(1)}, u32[]{:S(2)}, u32[]{:S(2)}) %collective-permute-start.30) | collective-permute-done | bytes 147488 | tf_op jit(solution)/shard_map/ppermute | solution.py:727
  164.4 3.5 %collective-permute-start.32 = (bf16[96,768]{1,0:T(8,128)(2,1)S(1)}, bf16[96,768]{1,0:T(8,128)(2,1)S(1)}, u32[]{:S(2)}, u32[]{:S(2)}) collective-permute-start(bf16[96,768]{1,0:T(8,128)(2,1)S(1)} %get-tuple-element.287.refs_0_), channel_id=1, source_target_pairs={{0,16},{1,5},{2,18},{3,7},{4,20},{5,1},{6,22},{7,3},{8,24},{9,13},... | collective-permute-start | bytes 442376 | tf_op jit(solution)/shard_map/ppermute | solution.py:727
  167.9 4.5 %collective-permute-done.34.refs_2_ = bf16[272,768]{1,0:T(8,128)(2,1)S(1)} collective-permute-done((bf16[272,768]{1,0:T(8,128)(2,1)S(1)}, bf16[272,768]{1,0:T(8,128)(2,1)S(1)}, u32[]{:S(2)}, u32[]{:S(2)}) %collective-permute-start.34) | collective-permute-done | bytes 417824 | tf_op jit(solution)/shard_map/ppermute | solution.py:719
  176.6 6.3 %collective-permute-done.38.refs_1_ = bf16[96,768]{1,0:T(8,128)(2,1)S(1)} collective-permute-done((bf16[96,768]{1,0:T(8,128)(2,1)S(1)}, bf16[96,768]{1,0:T(8,128)(2,1)S(1)}, u32[]{:S(2)}, u32[]{:S(2)}) %collective-permute-start.38) | collective-permute-done | bytes 147488 | tf_op jit(solution)/shard_map/ppermute | solution.py:727
  182.9 5.7 %shard_map.430 = (bf16[400,768]{1,0:T(8,128)(2,1)S(1)}, bf16[400,768]{1,0:T(8,128)(2,1)S(1)}, bf16[400,768]{1,0:T(8,128)(2,1)S(1)}, bf16[400,768]{1,0:T(8,128)(2,1)S(1)}, f32[8,128]{1,0:T(8,128)S(1)}) custom-call(bf16[400,768]{1,0:T(8,128)(2,1)S(1)} %get-tuple-element.280.refs_0_, bf16[400,768]{1,0:T(8,128)(2,1)S(1)} %collective-permute-done.28.refs_1_, ...), custom_call_target="tpu_custom_call" | custom-call | flops 1 | bytes 1 | tf_op jit(solution)/shard_map/pallas_call | solution.py:53
  194.4 13.7 %collective-permute-done.42.refs_1_ = f32[4,768]{1,0:T(4,128)S(1)} collective-permute-done((f32[4,768]{1,0:T(4,128)S(1)}, f32[4,768]{1,0:T(4,128)S(1)}, u32[]{:S(2)}, u32[]{:S(2)}) %collective-permute-start.42) | collective-permute-done | bytes 12320 | tf_op jit(solution)/shard_map/ppermute | solution.py:719
  212.9 6.2 %collective-permute-done.44.refs_1_ = bf16[96,768]{1,0:T(8,128)(2,1)S(1)} collective-permute-done((bf16[96,768]{1,0:T(8,128)(2,1)S(1)}, bf16[96,768]{1,0:T(8,128)(2,1)S(1)}, u32[]{:S(2)}, u32[]{:S(2)}) %collective-permute-start.44) | collective-permute-done | bytes 147488 | tf_op jit(solution)/shard_map/ppermute | solution.py:727
  225.0 6.2 %collective-permute-done.47.refs_1_ = f32[8,768]{1,0:T(8,128)S(1)} collective-permute-done((f32[8,768]{1,0:T(8,128)S(1)}, f32[8,768]{1,0:T(8,128)S(1)}, u32[]{:S(2)}, u32[]{:S(2)}) %collective-permute-start.47) | collective-permute-done | bytes 24608 | tf_op jit(solution)/shard_map/ppermute | solution.py:727
  238.3 9.1 %collective-permute-done.48.refs_2_ = bf16[272,768]{1,0:T(8,128)(2,1)S(1)} collective-permute-done((bf16[272,768]{1,0:T(8,128)(2,1)S(1)}, bf16[272,768]{1,0:T(8,128)(2,1)S(1)}, u32[]{:S(2)}, u32[]{:S(2)}) %collective-permute-start.48) | collective-permute-done | bytes 417824 | tf_op jit(solution)/shard_map/ppermute | solution.py:719
  (321 shorter events, 108.5 us)
Async XLA Ops:
  7.2 124.3 %all-gather.2.cloned.1.call-start = ((), (), s32[]{:S(2)}) async-start(), calls=%async_computation | async-start | bytes 1548288 | tf_op jit(solution)/shard_map/all_gather | solution.py:890
  7.2 12.7 %collective-permute-start.1 = (bf16[272,768]{1,0:T(8,128)(2,1)}, bf16[272,768]{1,0:T(8,128)(2,1)S(1)}, u32[]{:S(2)}, u32[]{:S(2)}) collective-permute-start(bf16[272,768]{1,0:T(8,128)(2,1)} %refs_0_.19), channel_id=1, source_target_pairs={{0,1},{1,0},{2,3},{3,2},{4,5},{5,4},{6,7},{7,6},{8,9},{9,8},{10,11... | collective-permute-start | bytes 1253384 | tf_op jit(solution)/shard_map/ppermute | solution.py:715
  7.8 23.6 %collective-permute-start = (bf16[272,768]{1,0:T(8,128)(2,1)}, bf16[272,768]{1,0:T(8,128)(2,1)S(1)}, u32[]{:S(2)}, u32[]{:S(2)}) collective-permute-start(bf16[272,768]{1,0:T(8,128)(2,1)} %refs_0_.19), channel_id=1, source_target_pairs={{0,2},{1,3},{2,0},{3,1},{4,6},{5,7},{6,4},{7,5},{8,10},{9,11},{10,... | collective-permute-start | bytes 1253384 | tf_op jit(solution)/shard_map/ppermute | solution.py:719
  28.2 21.0 %collective-permute-start.7 = (bf16[896,768]{1,0:T(8,128)(2,1)S(1)}, bf16[896,768]{1,0:T(8,128)(2,1)S(1)}, u32[]{:S(2)}, u32[]{:S(2)}) collective-permute-start(bf16[896,768]{1,0:T(8,128)(2,1)S(1)} %get-tuple-element.191.refs_2_.refs_1_), channel_id=1, source_target_pairs={{0,1},{1,0},{2,3},{3,2},{4,5},{5,4},{6,7},{7,6},{8,9},{9,8},{10,11... | collective-permute-start | bytes 4128776 | tf_op jit(solution)/shard_map/ppermute | solution.py:715
  32.1 15.4 %collective-permute-start.4 = (bf16[384,768]{1,0:T(8,128)(2,1)S(1)}, bf16[384,768]{1,0:T(8,128)(2,1)S(1)}, u32[]{:S(2)}, u32[]{:S(2)}) collective-permute-start(bf16[384,768]{1,0:T(8,128)(2,1)S(1)} %get-tuple-element.202), channel_id=1, source_target_pairs={{0,2},{1,3},{2,0},{3,1},{4,6},{5,7},{6,4},{7,5},{8,10},{9,11},{10,... | collective-permute-start | bytes 1769480 | tf_op jit(solution)/shard_map/ppermute | solution.py:719
  48.0 12.7 %collective-permute-start.9 = (bf16[272,768]{1,0:T(8,128)(2,1)S(1)}, bf16[272,768]{1,0:T(8,128)(2,1)S(1)}, u32[]{:S(2)}, u32[]{:S(2)}) collective-permute-start(bf16[272,768]{1,0:T(8,128)(2,1)S(1)} %copy-done), channel_id=1, source_target_pairs={{0,1},{1,0},{2,3},{3,2},{4,5},{5,4},{6,7},{7,6},{8,9},{9,8},{10,11... | collective-permute-start | bytes 1253384 | tf_op jit(solution)/shard_map/ppermute | solution.py:715
  60.0 12.4 %collective-permute-start.13 = (bf16[272,768]{1,0:T(8,128)(2,1)}, bf16[272,768]{1,0:T(8,128)(2,1)}, u32[]{:S(2)}, u32[]{:S(2)}) collective-permute-start(bf16[272,768]{1,0:T(8,128)(2,1)} %get-tuple-element.219.refs_2_), channel_id=1, source_target_pairs={{0,2},{1,3},{2,0},{3,1},{4,6},{5,7},{6,4},{7,5},{8,10},{9,11},{10,... | collective-permute-start | bytes 1253384 | tf_op jit(solution)/shard_map/ppermute | solution.py:719
  94.0 12.1 %collective-permute-start.19 = (bf16[272,768]{1,0:T(8,128)(2,1)S(1)}, bf16[272,768]{1,0:T(8,128)(2,1)S(1)}, u32[]{:S(2)}, u32[]{:S(2)}) collective-permute-start(bf16[272,768]{1,0:T(8,128)(2,1)S(1)} %get-tuple-element.242.refs_1_), channel_id=1, source_target_pairs={{0,2},{1,3},{2,0},{3,1},{4,6},{5,7},{6,4},{7,5},{8,10},{9,11},{10,... | collective-permute-start | bytes 1253384 | tf_op jit(solution)/shard_map/ppermute | solution.py:719
  97.7 15.1 %collective-permute-start.18 = (bf16[384,768]{1,0:T(8,128)(2,1)S(1)}, bf16[384,768]{1,0:T(8,128)(2,1)S(1)}, u32[]{:S(2)}, u32[]{:S(2)}) collective-permute-start(bf16[384,768]{1,0:T(8,128)(2,1)S(1)} %get-tuple-element.240), channel_id=1, source_target_pairs={{0,4},{1,9},{2,6},{3,11},{4,0},{5,13},{6,2},{7,15},{8,12},{9,1},{1... | collective-permute-start | bytes 1769480 | tf_op jit(solution)/shard_map/ppermute | solution.py:727
  106.8 19.8 %collective-permute-start.22 = (bf16[384,768]{1,0:T(8,128)(2,1)S(1)}, bf16[384,768]{1,0:T(8,128)(2,1)S(1)}, u32[]{:S(2)}, u32[]{:S(2)}) collective-permute-start(bf16[384,768]{1,0:T(8,128)(2,1)S(1)} %get-tuple-element.254), channel_id=1, source_target_pairs={{0,4},{1,9},{2,6},{3,11},{4,0},{5,13},{6,2},{7,15},{8,12},{9,1},{1... | collective-permute-start | bytes 1769480 | tf_op jit(solution)/shard_map/ppermute | solution.py:727
  148.3 27.0 %collective-permute-start.29 = (bf16[400,768]{1,0:T(8,128)(2,1)S(1)}, bf16[400,768]{1,0:T(8,128)(2,1)S(1)}, u32[]{:S(2)}, u32[]{:S(2)}) collective-permute-start(bf16[400,768]{1,0:T(8,128)(2,1)S(1)} %get-tuple-element.280.refs_0_), channel_id=1, source_target_pairs={{0,2},{1,3},{2,0},{3,1},{4,6},{5,7},{6,4},{7,5},{8,10},{9,11},{10,... | collective-permute-start | bytes 1843208 | tf_op jit(solution)/shard_map/ppermute | solution.py:719
  150.1 22.3 %collective-permute-start.34 = (bf16[272,768]{1,0:T(8,128)(2,1)S(1)}, bf16[272,768]{1,0:T(8,128)(2,1)S(1)}, u32[]{:S(2)}, u32[]{:S(2)}) collective-permute-start(bf16[272,768]{1,0:T(8,128)(2,1)S(1)} %copy-done.82), channel_id=1, source_target_pairs={{0,2},{1,3},{2,0},{3,1},{4,6},{5,7},{6,4},{7,5},{8,10},{9,11},{10,... | collective-permute-start | bytes 1253384 | tf_op jit(solution)/shard_map/ppermute | solution.py:719
  150.6 23.3 %collective-permute-start.36 = (bf16[192,768]{1,0:T(8,128)(2,1)S(1)}, bf16[192,768]{1,0:T(8,128)(2,1)S(1)}, u32[]{:S(2)}, u32[]{:S(2)}) collective-permute-start(bf16[192,768]{1,0:T(8,128)(2,1)S(1)} %get-tuple-element.301), channel_id=1, source_target_pairs={{0,8},{1,17},{2,10},{3,19},{4,12},{5,21},{6,14},{7,23},{8,0},{9,25... | collective-permute-start | bytes 884744 | tf_op jit(solution)/shard_map/ppermute | solution.py:727
  159.2 16.0 %collective-permute-start.33 = (bf16[96,768]{1,0:T(8,128)(2,1)S(1)}, bf16[96,768]{1,0:T(8,128)(2,1)S(1)}, u32[]{:S(2)}, u32[]{:S(2)}) collective-permute-start(bf16[96,768]{1,0:T(8,128)(2,1)S(1)} %get-tuple-element.289), channel_id=1, source_target_pairs={{0,16},{1,5},{2,18},{3,7},{4,20},{5,1},{6,22},{7,3},{8,24},{9,13},... | collective-permute-start | bytes 442376 | tf_op jit(solution)/shard_map/ppermute | solution.py:727
  189.2 19.0 %collective-permute-start.45 = (bf16[192,768]{1,0:T(8,128)(2,1)S(1)}, bf16[192,768]{1,0:T(8,128)(2,1)S(1)}, u32[]{:S(2)}, u32[]{:S(2)}) collective-permute-start(bf16[192,768]{1,0:T(8,128)(2,1)S(1)} %get-tuple-element.327.refs_0_), channel_id=1, source_target_pairs={{0,8},{1,17},{2,10},{3,19},{4,12},{5,21},{6,14},{7,23},{8,0},{9,25... | collective-permute-start | bytes 884744 | tf_op jit(solution)/shard_map/ppermute | solution.py:727
  189.2 18.9 %collective-permute-start.46 = (bf16[96,768]{1,0:T(8,128)(2,1)S(1)}, bf16[96,768]{1,0:T(8,128)(2,1)S(1)}, u32[]{:S(2)}, u32[]{:S(2)}) collective-permute-start(bf16[96,768]{1,0:T(8,128)(2,1)S(1)} %get-tuple-element.328.refs_0_), channel_id=1, source_target_pairs={{0,16},{1,5},{2,18},{3,7},{4,20},{5,1},{6,22},{7,3},{8,24},{9,13},... | collective-permute-start | bytes 442376 | tf_op jit(solution)/shard_map/ppermute | solution.py:727
  192.3 39.0 %collective-permute-start.41 = (bf16[400,768]{1,0:T(8,128)(2,1)S(1)}, bf16[400,768]{1,0:T(8,128)(2,1)S(1)}, u32[]{:S(2)}, u32[]{:S(2)}) collective-permute-start(bf16[400,768]{1,0:T(8,128)(2,1)S(1)} %get-tuple-element.318), channel_id=1, source_target_pairs={{0,2},{1,3},{2,0},{3,1},{4,6},{5,7},{6,4},{7,5},{8,10},{9,11},{10,... | collective-permute-start | bytes 1843208 | tf_op jit(solution)/shard_map/ppermute | solution.py:719
  193.9 14.2 %collective-permute-start.42 = (f32[4,768]{1,0:T(4,128)S(1)}, f32[4,768]{1,0:T(4,128)S(1)}, u32[]{:S(2)}, u32[]{:S(2)}) collective-permute-start(f32[4,768]{1,0:T(4,128)S(1)} %get-tuple-element.319.refs_0_), channel_id=1, source_target_pairs={{0,2},{1,3},{2,0},{3,1},{4,6},{5,7},{6,4},{7,5},{8,10},{9,11},{10,... | collective-permute-start | bytes 36872 | tf_op jit(solution)/shard_map/ppermute | solution.py:719
  208.2 25.2 %collective-permute-start.50 = (bf16[384,768]{1,0:T(8,128)(2,1)S(1)}, bf16[384,768]{1,0:T(8,128)(2,1)S(1)}, u32[]{:S(2)}, u32[]{:S(2)}) collective-permute-start(bf16[384,768]{1,0:T(8,128)(2,1)S(1)} %get-tuple-element.339.refs_0_), channel_id=1, source_target_pairs={{0,4},{1,9},{2,6},{3,11},{4,0},{5,13},{6,2},{7,15},{8,12},{9,1},{1... | collective-permute-start | bytes 1769480 | tf_op jit(solution)/shard_map/ppermute | solution.py:727
  210.2 22.3 %collective-permute-start.51 = (bf16[192,768]{1,0:T(8,128)(2,1)S(1)}, bf16[192,768]{1,0:T(8,128)(2,1)S(1)}, u32[]{:S(2)}, u32[]{:S(2)}) collective-permute-start(bf16[192,768]{1,0:T(8,128)(2,1)S(1)} %get-tuple-element.340.refs_0_), channel_id=1, source_target_pairs={{0,8},{1,17},{2,10},{3,19},{4,12},{5,21},{6,14},{7,23},{8,0},{9,25... | collective-permute-start | bytes 884744 | tf_op jit(solution)/shard_map/ppermute | solution.py:727
  219.1 16.1 %collective-permute-start.49 = (bf16[192,768]{1,0:T(8,128)(2,1)S(1)}, bf16[192,768]{1,0:T(8,128)(2,1)S(1)}, u32[]{:S(2)}, u32[]{:S(2)}) collective-permute-start(bf16[192,768]{1,0:T(8,128)(2,1)S(1)} %get-tuple-element.338.refs_0_), channel_id=1, source_target_pairs={{0,8},{1,17},{2,10},{3,19},{4,12},{5,21},{6,14},{7,23},{8,0},{9,25... | collective-permute-start | bytes 884744 | tf_op jit(solution)/shard_map/ppermute | solution.py:727
  232.5 15.8 %collective-permute-start.54 = (bf16[384,768]{1,0:T(8,128)(2,1)S(1)}, bf16[384,768]{1,0:T(8,128)(2,1)S(1)}, u32[]{:S(2)}, u32[]{:S(2)}) collective-permute-start(bf16[384,768]{1,0:T(8,128)(2,1)S(1)} %get-tuple-element.350.refs_0_), channel_id=1, source_target_pairs={{0,4},{1,9},{2,6},{3,11},{4,0},{5,13},{6,2},{7,15},{8,12},{9,1},{1... | collective-permute-start | bytes 1769480 | tf_op jit(solution)/shard_map/ppermute | solution.py:727
  235.2 14.9 %collective-permute-start.53 = (bf16[384,768]{1,0:T(8,128)(2,1)S(1)}, bf16[384,768]{1,0:T(8,128)(2,1)S(1)}, u32[]{:S(2)}, u32[]{:S(2)}) collective-permute-start(bf16[384,768]{1,0:T(8,128)(2,1)S(1)} %get-tuple-element.349.refs_0_), channel_id=1, source_target_pairs={{0,4},{1,9},{2,6},{3,11},{4,0},{5,13},{6,2},{7,15},{8,12},{9,1},{1... | collective-permute-start | bytes 1769480 | tf_op jit(solution)/shard_map/ppermute | solution.py:727
  238.0 14.0 %collective-permute-start.52 = (f32[8,768]{1,0:T(8,128)S(1)}, f32[8,768]{1,0:T(8,128)S(1)}, u32[]{:S(2)}, u32[]{:S(2)}) collective-permute-start(f32[8,768]{1,0:T(8,128)S(1)} %get-tuple-element.348.refs_0_), channel_id=1, source_target_pairs={{0,16},{1,17},{2,18},{3,19},{4,20},{5,21},{6,22},{7,23},{8,24},{9,... | collective-permute-start | bytes 73736 | tf_op jit(solution)/shard_map/ppermute | solution.py:727
  (117 other events, 699.6 us)
Sparse Core Ops, SparseCore 0:
  71.3 45.8 all-gather.1
where the time goes:
time: 261 us; the launch traced here: 260 us
  waiting for transfers between devices  100 us (38%)
  Pallas kernels  71.4 us (27%)
  starting transfers between devices  46 us (18%)
  local copies, waits for them, and re-layouts  27 us (10%)
  between operations  15.1 us (6%)
    pallas_call x59, Pallas kernels, __call__(): pl.pallas_call(run, out_shape=(*outs, shape(8, 128, dtype=F32)), in_specs...  71.4 us
    ppermute x21, waiting for transfers between devices, dp_swap(): return lax.ppermute(x, ('dp', 'mp'), pairs)  48.2 us
    ppermute x11, waiting for transfers between devices, side_swap(): lax.ppermute(x, 'mp', [(i, i ^ 2) for i in range(lax.axis_size('mp'))])  46.7 us
    unnamed x170, local copies, waits for them, and re-layouts  26.3 us
    ppermute x21, starting transfers between devices, dp_swap(): return lax.ppermute(x, ('dp', 'mp'), pairs)  26.2 us
    ppermute x11, starting transfers between devices, side_swap(): lax.ppermute(x, 'mp', [(i, i ^ 2) for i in range(lax.axis_size('mp'))])  10.5 us
    ppermute x23, starting transfers between devices, core_swap(): lax.ppermute(x, 'mp', [(i, i ^ 1) for i in range(lax.axis_size('mp'))])  9.27 us
  transfers between devices with their start and end apart: 56, of which 23 were waited for; matrix products, arithmetic and copies ran while one was open for 0% of the time, Pallas kernels for 23%

commit v1 on v0

--- a/solution.py
+++ b/solution.py
@@ -30,44 +30,114 @@
     return jax.ShapeDtypeStruct(dims, dtype)
 
 
+class Late:
+    def __init__(self, value):
+        self.value, self.shape, self.dtype = value, value.shape, value.dtype
+
+
+class Fixed:
+    def __init__(self, value):
+        self.value, self.shape, self.dtype = value, value.shape, value.dtype
+
+
+class Early:
+    def __init__(self, *dims, dtype=BF):
+        self.shape, self.dtype = dims, dtype
+
+
+class Moving:
+    def __init__(self, source, target, held, sem):
+        self.held, self.shape = held, held.shape
+        self.copy = pltpu.make_async_copy(source, target, sem)
+        self.waits = False
+
+    def start(self):
+        self.copy.start()
+        self.waits = True
+
+    def get(self):
+        if self.waits:
+            self.copy.wait()
+            self.waits = False
+        return self.held
+
+
 class Line:
     def __init__(self):
         self.token = None
 
     def __call__(self, body, outs, args, scratch=(), vmem=16, untouched=(), scalars=(), after=(),
                  same=None, outside=False):
-        args = list(args)
-        real = len(args)
-        args += list(after) + ([] if self.token is None else [self.token])
-        given = len(args)
+        def place(a):
+            if isinstance(a, (Late, Fixed)):
+                return pltpu.with_memory_space_constraint(a.value, pltpu.HBM)
+            return a
+
+        kinds = list(args)
+        real = len(kinds)
+        values = [place(a) for a in kinds + list(after)]
+        values += [] if self.token is None else [self.token]
+        given = len(values)
+        late = [i for i, a in enumerate(kinds) if isinstance(a, Late)]
+        fixed = [i for i, a in enumerate(kinds) if isinstance(a, Fixed)]
+        early = [i for i, o in enumerate(outs) if isinstance(o, Early)]
 
         def in_space(i):
             if i >= real or i in untouched:
                 return pl.ANY
+            if i in late or i in fixed:
+                return pltpu.HBM
             return pltpu.SMEM if i in scalars else pltpu.VMEM
 
+        def out_space(i):
+            if outside or same is not None:
+                return pl.ANY
+            return pltpu.HBM if i in early else pltpu.VMEM
+
+        moving = [kinds[i] for i in late] + [outs[i] for i in early]
+        held = [pltpu.VMEM(m.shape, m.dtype) for m in moving]
+        sems = [pltpu.SemaphoreType.DMA((len(held),))] if held else []
+        first = given + len(outs) + 1
+
         def run(*refs):
-            body(*refs[:real], *refs[given : given + len(outs)], *refs[given + len(outs) + 1 :])
-
-        out_space = pl.ANY if outside or same is not None else pltpu.VMEM
+            ins, results = list(refs[:real]), list(refs[given : given + len(outs)])
+            places = refs[first : first + len(held)]
+            for k, i in enumerate(late):
+                ins[i] = Moving(ins[i], places[k], places[k], refs[-1].at[k])
+                ins[i].start()
+            for k, i in enumerate(early, len(late)):
+                results[i] = Moving(places[k], results[i], places[k], refs[-1].at[k])
+            body(*ins, *results, *refs[first + len(held) : len(refs) - len(sems)])
+            for moved in [ins[i] for i in late] + [results[i] for i in early]:
+                moved.get()
+
         results = pl.pallas_call(
             run,
-            out_shape=(*outs, shape(8, 128, dtype=F32)),
+            out_shape=(
+                *(
+                    pltpu.HBM(o.shape, o.dtype)
+                    if i in early
+                    else jax.ShapeDtypeStruct(o.shape, o.dtype)
+                    for i, o in enumerate(outs)
+                ),
+                shape(8, 128, dtype=F32),
+            ),
             in_specs=[pl.BlockSpec(memory_space=in_space(i)) for i in range(given)],
             out_specs=tuple(
-                pl.BlockSpec(memory_space=space) for space in [out_space] * len(outs) + [pl.ANY]
+                [pl.BlockSpec(memory_space=out_space(i)) for i in range(len(outs))]
+                + [pl.BlockSpec(memory_space=pl.ANY)]
             ),
-            scratch_shapes=list(scratch),
+            scratch_shapes=held + list(scratch) + sems,
             input_output_aliases={} if same is None else {same: 0},
             compiler_params=pltpu.CompilerParams(vmem_limit_bytes=vmem * 1024 * 1024),
             cost_estimate=pl.CostEstimate(flops=1, bytes_accessed=1, transcendentals=0),
-        )(*args)
+        )(*values)
         self.token = results[-1]
         return results[:-1] if len(outs) > 1 else results[0]
 
-    def hold(self, value):
+    def hold(self, value, after=()):
         return self(lambda *refs: None, [shape(*value.shape, dtype=value.dtype)], [value],
-                    untouched=(0,), same=0)
+                    untouched=(0,), same=0, after=after)
 
 
 def norm(x):
@@ -157,6 +227,22 @@
     return pl.ds(pl.multiple_of(index * size, 128), size)
 
 
+def pieces_of(count, parts):
+    most = -(-count // (16 * parts)) * 16
+    return [min(most, count - low) for low in range(0, count, most)]
+
+
+def put_pieces(value, outs):
+    low = 0
+    for out in outs:
+        out[...] = value[low : low + out.shape[0]]
+        low += out.shape[0]
+
+
+def join_pieces(refs):
+    return jnp.concatenate([ref[...] for ref in refs], axis=0)
+
+
 def chunk_start(index, size):
     return pl.ds(pl.multiple_of(index * size, 16), size)
 
@@ -213,14 +299,14 @@
     for out, own in ((text, items[: len(items) // 2]), (image, items[len(items) // 2 :])):
         out[...] = jnp.zeros(out.shape, F32)
         for k, item in enumerate(own):
-            out[k : k + 1, :] = item[...].astype(F32).reshape(1, -1)
+            out[k : k + 1, :] = item.get()[...].astype(F32).reshape(1, -1)
 
 
 def vector(vectors, index):
     return vectors[index : index + 1, :]
 
 
-def project(x_pair, vectors, w_t, bias, rows, qkv, bias_rows, at):
+def project(x_pair, vectors, w_t, bias, rows_out, qkv, bias_rows, at):
     size = x_pair.shape[1]
     width = bias.shape[1]
     gain, shift = vector(vectors, ATTN_GAIN), vector(vectors, ATTN_SHIFT)
@@ -236,7 +322,9 @@
         value = dot(rows[...], w_t[chunk_start(i, width), :], NT) + bias_rows[pl.ds(i, 1), :]
         qkv[i, at, :] = value.astype(BF)
 
+    rows = rows_out.held
     repeat(2, normalize)
+    rows_out.start()
     repeat(3, part)
 
 
@@ -258,10 +346,19 @@
     copy.wait()
 
 
-def unpack_kernel(packed, grad, part):
-    size = grad.shape[0]
-    grad[...] = packed[:size]
-    part[...] = packed[size:]
+def unpack_kernel(packed, part):
+    part[...] = packed[packed.shape[0] - part.shape[0] :]
+
+
+def arrange_kernel(t0, t1, packed, packed_other, half0, half1):
+    size = t0.shape[0]
+    here = lax.axis_index("mp") // 2 == 0
+    parts = ((slice(0, size), t0, packed), (slice(size, 2 * size), t1, packed_other))
+    for at, own, far in parts:
+        half0.held[at, :] = jnp.where(here, own[...], far[:size])
+        half1.held[at, :] = jnp.where(here, far[:size], own[...])
+    half0.start()
+    half1.start()
 
 
 def block_loop(blocks, body, unroll=False):
@@ -286,23 +383,30 @@
     repeat(len(pairs), pair)
 
 
-def attn_forward_kernel(blocks, x2, x3, qkv_own, vectors, w_t, bias, out_w, mask,
-                        rows_out, qkv, ctx, keep0, keep1, send0, send1, x_pair, bias_rows):
+def attn_forward_kernel(blocks, x0, x2, x3, qkv_own, vectors, w_t, bias, out_w, mask,
+                        rows_out, qkv_out, ctx_out, x_mine, keep0, keep1, send0, send1,
+                        x_pair, bias_rows):
+    qkv, ctx = qkv_out.held, ctx_out.held
     me = lax.axis_index("mp")
     core, side = me % 2, me // 2
     size, dim = x2.shape
     x_pair[core] = x2[...]
     x_pair[1 - core] = x3[...]
+    x_mine.held[side] = x0[...]
+    x_mine.held[1 - side] = x2[...]
+    x_mine.start()
     far = chunk_start(1 - side, 2 * size)
     project(x_pair, vectors, w_t, bias, rows_out, qkv, bias_rows, far)
     own = chunk_start(side, 2 * size)
     for part in range(3):
         qkv[part, own, :] = qkv_own[part]
+    qkv_out.start()
 
     def block(at, count):
         ctx[at, :] = attend(qkv[0, at, :], qkv[1, at, :], qkv[2, at, :], mask[at, :count])
 
     block_loop(blocks, block, unroll=True)
+    ctx_out.start()
 
     def columns(i):
         cols = lanes(i, 256)
@@ -320,6 +424,17 @@
     out[...] = (a[...].astype(F32) + b[...].astype(F32)).astype(BF)
 
 
+def add_pieces_kernel(a, *rest):
+    *pieces, out = rest
+    out[...] = (a[...].astype(F32) + join_pieces(pieces).astype(F32)).astype(BF)
+
+
+def branch_sums_kernel(keep0, other0, keep1, other1, mine0, mine1):
+    for keep, other, mine in ((keep0, other0, mine0), (keep1, other1, mine1)):
+        mine.held[...] = (keep[...].astype(F32) + other[...].astype(F32)).astype(BF)
+        mine.start()
+
+
 def add_pair_kernel(a0, b0, a1, b1, out0, out1):
     for a, b, out in ((a0, b0, out0), (a1, b1, out1)):
         out[...] = (a[...].astype(F32) + b[...].astype(F32)).astype(BF)
@@ -337,25 +452,26 @@
     out[half:] = b[...]
 
 
-def chosen(half, own, far):
-    return jnp.where(lax.axis_index("mp") // 2 == half, own[...], far[...])
-
-
-def after_attn_kernel(half, x0, x2, mine, theirs, vectors, after_out, rows):
+def after_attn_kernel(half, x_mine, mine, theirs, vectors, after_out, rows, *pieces):
     total = mine[...].astype(F32) + theirs[...].astype(F32)
-    stream = chosen(half, x0, x2).astype(F32) + (total + vector(vectors, OUT_BIAS))
-    after_out[...] = stream
+    stream = x_mine[half].astype(F32) + (total + vector(vectors, OUT_BIAS))
+    after_out.held[...] = stream
+    after_out.start()
     normed, _ = norm(stream)
-    rows[...] = (normed * vector(vectors, MLP_GAIN) + vector(vectors, MLP_SHIFT)).astype(BF)
-
-
-def mlp_kernel(half, rows0, rows1, t0, t1, t2, t3, w1, vectors, w2,
-               act, hid_grad, br_keep, br_send, mg_keep, mg_send, rows, grad):
+    value = (normed * vector(vectors, MLP_GAIN) + vector(vectors, MLP_SHIFT)).astype(BF)
+    rows[...] = value
+    put_pieces(value, pieces)
+
+
+def mlp_kernel(count, rows0, *rest):
+    pieces, (grad, w1, vectors, w2), rest = rest[:count], rest[count : count + 4], rest[count + 4 :]
+    rows_out, act_out, hg_out, br_keep, br_send, mg_keep, *mg_sends = rest
     size, dim = rows0.shape
+    rows, act, hid_grad = rows_out.held, act_out.held, hg_out.held
     rows[:size, :] = rows0[...]
-    rows[size:, :] = rows1[...]
-    grad[:size, :] = chosen(half, t0, t2)
-    grad[size:, :] = chosen(half, t1, t3)
+    rows[size:, :] = join_pieces(pieces)
+    rows_out.start()
+    grad = grad
 
     def units(i):
         cols = lanes(i, 256)
@@ -369,18 +485,30 @@
         cols = lanes(i, 256)
         value = dot(hid_grad[...], w1[cols, :], NT).astype(BF)
         mg_keep[:, cols] = value[:size]
-        mg_send[:, cols] = value[size:]
+        low = size
+        for send in mg_sends:
+            send[:, cols] = value[low : low + send.shape[0]]
+            low += send.shape[0]
+
+    def branch_columns(i):
+        cols = lanes(i, 256)
         value = dot(act[...], w2[:, cols]).astype(BF)
-        br_keep[:, cols] = value[:size]
-        br_send[:, cols] = value[size:]
+        br_keep.held[:, cols] = value[:size]
+        br_send.held[:, cols] = value[size:]
 
     repeat(w1.shape[1] // 256, units)
+    act_out.start()
+    hg_out.start()
+    repeat(dim // 256, branch_columns)
+    br_keep.start()
+    br_send.start()
     repeat(dim // 256, columns)
 
 
-def mlp_back_kernel(half, after, mine, theirs, t0, t2, vectors, after_grad, out_grad, sums):
+def mlp_back_kernel(after, mine, theirs, grad, vectors, ag_out, out_grad, sums, *pieces):
+    size = mine.shape[0]
+    rows_grad = mine[...].astype(F32) + theirs[...].astype(F32)
     normed, inverse = norm(after[...])
-    rows_grad = mine[...].astype(F32) + theirs[...].astype(F32)
     sums[...] = jnp.concatenate(
         [
             jnp.sum(rows_grad * normed, axis=0, keepdims=True),
@@ -388,19 +516,24 @@
         ],
         axis=0,
     )
-    value = chosen(half, t0, t2).astype(F32) + norm_back(
+    value = grad[:size, :].astype(F32) + norm_back(
         rows_grad, vector(vectors, MLP_GAIN), normed, inverse
     )
-    after_grad[...] = value
-    out_grad[...] = value.astype(BF)
-
-
-def attn_back_first_kernel(blocks, og_mine, og_other, qkv, mask, out_w, og, cg, pg):
+    ag_out.held[...] = value
+    ag_out.start()
+    low = value.astype(BF)
+    out_grad[...] = low
+    put_pieces(low, pieces)
+
+
+def attn_back_first_kernel(blocks, count, og_mine, *rest):
+    og_others, (qkv, mask, out_w, og, cg, pg) = rest[:count], rest[count:]
     core = lax.axis_index("mp") % 2
     size = og_mine.shape[0]
     og[chunk_start(core, size), :] = og_mine[...]
-    og[chunk_start(1 - core, size), :] = og_other[...]
+    og[chunk_start(1 - core, size), :] = join_pieces(og_others)
     cg[...] = dot(og[...], out_w[...], NT).astype(BF)
+    qkv = qkv
 
     def block(at, count):
         grads = attend_back(
@@ -412,8 +545,9 @@
     block_loop(blocks, block)
 
 
-def attn_back_second_kernel(blocks, og_mine, og_other, cg_first, pg_first, qkv, mask, out_w, w_t,
-                            og, pg, p0, p1, p2, p3, cg):
+def attn_back_second_kernel(blocks, count, og_mine, *rest):
+    og_others, rest = rest[:count], rest[count:]
+    cg_first, pg_first, qkv, mask, out_w, w_t, og, pg, p0, p1, p2, p3, cg = rest
     me = lax.axis_index("mp")
     core = me % 2
     size, dim = og_mine.shape
@@ -421,9 +555,10 @@
     half = 2 * size
     done = pg_first.shape[1]
     og[chunk_start(core, size), :] = og_mine[...]
-    og[chunk_start(1 - core, size), :] = og_other[...]
+    og[chunk_start(1 - core, size), :] = join_pieces(og_others)
     cg[half:, :] = dot(og[...], out_w[...], NT).astype(BF)
     cg[:half, :] = cg_first[...]
+    qkv = qkv
     for part in range(3):
         pg[part, :done, :] = pg_first[part]
 
@@ -496,26 +631,12 @@
     return jnp.sum(ref[...].astype(F32), axis=0, keepdims=True)
 
 
-def fc2_weight_kernel(orders, act0, act1, t0, t1, t2, t3, *rest):
+def fc_weight_kernel(orders, left0, left1, right0, right1, *rest):
     *outs, sums, full, left, right = rest
-    size = t0.shape[0]
-    side = lax.axis_index("mp") // 2
-    left[chunk_start(side, 2 * size), :] = act0[...]
-    left[chunk_start(1 - side, 2 * size), :] = act1[...]
-    for k, t in enumerate((t0, t1, t2, t3)):
-        right[k * size : (k + 1) * size, :] = t[...]
-    weight_product(left, right, full)
-    emit(full, outs, orders)
-    sums[...] = row_sum(right)
-
-
-def fc1_weight_kernel(orders, rows00, rows01, rows10, rows11, hg0, hg1, *rest):
-    *outs, sums, full, left, right = rest
-    size = rows00.shape[0]
-    for k, rows in enumerate((rows00, rows01, rows10, rows11)):
-        left[k * size : (k + 1) * size, :] = rows[...]
-    right[: 2 * size, :] = hg0[...]
-    right[2 * size :, :] = hg1[...]
+    half = left0.shape[0]
+    for at, a, b in ((slice(0, half), left0, right0), (slice(half, 2 * half), left1, right1)):
+        left[at, :] = a[...]
+        right[at, :] = b[...]
     weight_product(left, right, full)
     emit(full, outs, orders)
     sums[...] = row_sum(right)
@@ -629,81 +750,87 @@
     return windows
 
 
-def image_attn_kernel(first, last, shards, x, vectors, *rest):
-    rest = list(rest)
-    before = None if first else rest.pop(0)
-    sources, rest = rest[:shards], rest[shards:]
-    *outs, total, rows, context, bundle, sems = rest
-    count, dim = x.shape
+def image_attn_kernel(first, x0, x1, vectors, *rest):
+    if first:
+        source, result, rows, context, total, weights, sem = rest
+    else:
+        before, source, keep, *sends, rows, context, total, weights, sem = rest
+    count, dim = x0.shape
     images = count // IMG_SEQ
     width = dim // 4
-    copies = [
-        pltpu.make_async_copy(source.at[0 : 4 * width + 16], bundle.at[s], sems.at[s])
-        for s, source in enumerate(sources)
-    ]
-    for copy in copies:
-        copy.start()
-    normed, _ = norm(x[...].astype(F32))
-    rows[...] = (normed * vector(vectors, ATTN_GAIN) + vector(vectors, ATTN_SHIFT)).astype(BF)
-    total[...] = jnp.zeros((count, dim), F32) if first else before[...]
+    copy = pltpu.make_async_copy(source.at[0 : 4 * width + 16], weights, sem)
+    copy.start()
+    for k, x in enumerate((x0, x1)):
+        normed, _ = norm(x[...].astype(F32))
+        rows[k * count : (k + 1) * count, :] = (
+            normed * vector(vectors, ATTN_GAIN) + vector(vectors, ATTN_SHIFT)
+        ).astype(BF)
     windows = image_windows(count, images)
-
-    def shard(s):
-        for k in range(shards):
-
-            @pl.when(s == k)
-            def _():
-                copies[k].wait()
-
-        weights = bundle.at[s]
-        bias = weights[4 * width : 4 * width + 16, :].astype(F32)
-        q = (dot(rows[...], weights[:width, :], NT) + bias[0:1, :width]).astype(BF)
-        k = dot(rows[...], weights[width : 2 * width, :], NT).astype(BF)
-        v = (dot(rows[...], weights[2 * width : 3 * width, :], NT) + bias[1:2, :width]).astype(BF)
+    copy.wait()
+    bias = weights[4 * width : 4 * width + 16, :].astype(F32)
+
+    def chunk(c):
+        own = rows[chunk_start(c, count), :]
+        q = (dot(own, weights[:width, :], NT) + bias[0:1, :width]).astype(BF)
+        k = dot(own, weights[width : 2 * width, :], NT).astype(BF)
+        v = (dot(own, weights[2 * width : 3 * width, :], NT) + bias[1:2, :width]).astype(BF)
         for q_low, q_high, k_low, k_high in windows:
             extent = (q_high - q_low, k_high - k_low)
             q_image = (lax.broadcasted_iota(jnp.int32, extent, 0) + q_low) // IMG_SEQ
             k_image = (lax.broadcasted_iota(jnp.int32, extent, 1) + k_low) // IMG_SEQ
             mask = jnp.where(q_image == k_image, 1.0, 0.0)
-            context[q_low:q_high, :] = attend(
+            place = pl.ds(pl.multiple_of(c * count + q_low, 16), q_high - q_low)
+            context[place, :] = attend(
                 q[q_low:q_high], k[k_low:k_high], v[k_low:k_high], mask
             )
 
+    def columns(i):
+        cols = lanes(i, 256)
+        total[:, cols] = dot(context[...], weights[3 * width : 4 * width, cols])
+
+    repeat(2, chunk)
+    repeat(dim // 256, columns)
+    if first:
+        result.held[...] = total[...]
+        result.start()
+        return
+    keep[...] = total[:count, :] + before[:count, :]
+    put_pieces((total[count:, :] + before[count:, :]).astype(BF), sends)
+
+
+def image_norm_kernel(x, keep, vectors, *rest):
+    *others, after_out, rows = rest
+    total = keep[...] + join_pieces(others).astype(F32)
+    after = x[...].astype(F32) + (total + vector(vectors, OUT_BIAS))
+    after_out.held[...] = after
+    after_out.start()
+    normed, _ = norm(after)
+    rows[...] = (normed * vector(vectors, MLP_GAIN) + vector(vectors, MLP_SHIFT)).astype(BF)
+
+
+def image_mlp_kernel(rows0, rows2, vec0, vec1, w1a, w2a, w1b, w2b, mine, far, rows, active, total):
+    size, dim = rows0.shape
+    rows[:size, :] = rows0[...]
+    rows[size:, :] = rows2[...]
+    total[...] = jnp.zeros(total.shape, F32)
+    for vectors, w1, w2 in ((vec0, w1a, w2a), (vec1, w1b, w2b)):
+        w1 = w1.get()
+
+        def units(i):
+            cols = lanes(i, 256)
+            hidden = dot(rows[...], w1[:, cols]) + vectors[FC1_BIAS : FC1_BIAS + 1, cols]
+            active[:, cols] = gelu_parts(hidden)[0].astype(BF)
+
+        repeat(w1.shape[1] // 256, units)
+        w2 = w2.get()
+
         def columns(i):
             cols = lanes(i, 256)
-            total[:, cols] += dot(context[...], bundle[s, 3 * width : 4 * width, cols])
+            total[:, cols] += dot(active[...], w2[:, cols])
 
         repeat(dim // 256, columns)
-
-    repeat(shards, shard)
-    if not last:
-        outs[0][...] = total[...]
-        return
-    after_ref, rows_ref = outs
-    after = x[...].astype(F32) + (total[...] + vector(vectors, OUT_BIAS))
-    after_ref[...] = after
-    normed, _ = norm(after)
-    rows_ref[...] = (normed * vector(vectors, MLP_GAIN) + vector(vectors, MLP_SHIFT)).astype(BF)
-
-
-def image_mlp_kernel(r0, r1, r2, r3, w1, vectors, w2, p0, p1, p2, p3, rows, active):
-    size, dim = r0.shape
-    for k, r in enumerate((r3, r1, r2, r0)):
-        rows[k * size : (k + 1) * size, :] = r[...]
-
-    def units(i):
-        cols = lanes(i, 256)
-        hidden = dot(rows[...], w1[:, cols]) + vectors[FC1_BIAS : FC1_BIAS + 1, cols]
-        active[:, cols] = gelu_parts(hidden)[0].astype(BF)
-
-    def columns(i):
-        cols = lanes(i, 256)
-        value = dot(active[...], w2[:, cols]).astype(BF)
-        for k, p in enumerate((p3, p1, p2, p0)):
-            p[:, cols] = value[k * size : (k + 1) * size]
-
-    repeat(w1.shape[1] // 256, units)
-    repeat(dim // 256, columns)
+    mine[...] = total[:size, :].astype(BF)
+    far[...] = total[size:, :].astype(BF)
 
 
 def image_out_kernel(after, mine, theirs, vectors, out):
@@ -786,15 +913,18 @@
         vectors_kernel,
         [shape(8, dim, dtype=F32)] * 2,
         [
-            attn_gain, attn_shift, out_bias, mlp_gain, mlp_shift, fc2_bias, fc1_bias,
-            img_attn_gain, img_attn_shift, img_out_bias, img_mlp_gain, img_mlp_shift,
-            img_fc2_bias, img_fc1_bias,
+            Late(v)
+            for v in (
+                attn_gain, attn_shift, out_bias, mlp_gain, mlp_shift, fc2_bias, fc1_bias,
+                img_attn_gain, img_attn_shift, img_out_bias, img_mlp_gain, img_mlp_shift,
+                img_fc2_bias, img_fc1_bias,
+            )
         ],
     )
     project_scratch = [pltpu.VMEM((2, size, dim), BF), pltpu.VMEM((8, width), F32)]
     rows_own, qkv_own = run(
         own_rows_kernel,
-        [pair, shape(3, 2 * size, width)],
+        [Early(2 * size, dim), shape(3, 2 * size, width)],
         [x0, x1, vectors, w_t, qv_bias],
         scratch=project_scratch,
     )
@@ -815,30 +945,8 @@
         untouched=(0, 1),
         outside=True,
     )
-    t1 = core_swap(text_grad)
-    own_other = core_swap(bundle)
-    image_rows = images.shape[0]
-
-    def image_attn(first, last, operands, outs, sources):
-        args = [images, img_vectors, *operands, *sources]
-        shards = len(sources)
-        return run(
-            functools.partial(image_attn_kernel, first, last, shards),
-            outs,
-            args,
-            scratch=[
-                pltpu.VMEM((image_rows, dim), F32),
-                pltpu.VMEM((image_rows, dim), BF),
-                pltpu.VMEM((image_rows, width), BF),
-                pltpu.VMEM((shards, used, dim), BF),
-                pltpu.SemaphoreType.DMA((shards,)),
-            ],
-            untouched=tuple(range(len(args) - shards, len(args))),
-        )
-
-    image_wide = shape(image_rows, dim, dtype=F32)
-    image_total = image_attn(True, False, [], [image_wide], [bundle])
     t0 = text_grad
+    t1 = core_swap(t0)
     packed = run(
         far_operands_kernel,
         [shape(size + part_rows, dim)],
@@ -851,76 +959,98 @@
     x3 = core_swap(x2)
     packed = side_swap(packed)
 
-    rows_far, qkv, ctx, keep0, keep1, send0, send1 = run(
+    rows_far, qkv, ctx, x_mine, keep0, keep1, send0, send1 = run(
         functools.partial(attn_forward_kernel, blocks),
-        [pair, shape(3, tokens, width), shape(tokens, width)] + [chunk] * 4,
-        [x2, x3, qkv_own, vectors, w_t, qv_bias, out_weight, mask],
+        [
+            Early(2 * size, dim),
+            Early(3, tokens, width),
+            Early(tokens, width),
+            Early(2, size, dim),
+        ]
+        + [chunk] * 4,
+        [x0, x2, x3, qkv_own, vectors, w_t, qv_bias, out_weight, mask],
         scratch=project_scratch,
     )
 
+    thirds, halves = pieces_of(size, 3), pieces_of(size, 2)
+
     def after_attn(half, mine, theirs):
-        stream, rows = run(
+        stream, rows, *sends = run(
             functools.partial(after_attn_kernel, half),
-            [shape(size, dim, dtype=F32), chunk],
-            [x0, x2, mine, theirs, vectors],
+            [Early(size, dim, dtype=F32), chunk] + [shape(n, dim) for n in thirds],
+            [x_mine, mine, theirs, vectors],
         )
-        return stream, rows, core_swap(rows)
-
-    def mlp(half, rows, rows_other):
-        return run(
-            functools.partial(mlp_kernel, half),
-            [pair] * 2 + [chunk] * 4,
-            [rows, rows_other, t0, t1, t2, t3, fc1_weight, vectors, fc2_weight],
-            scratch=[pltpu.VMEM((2 * size, dim), BF)] * 2,
+        return stream, (rows, *map(core_swap, sends))
+
+    def mlp(rows, grad):
+        all_rows, act, hid_grad, br_keep, br_send, mg_keep, *mg_sends = run(
+            functools.partial(mlp_kernel, len(rows) - 1),
+            [Early(2 * size, dim)] * 3
+            + [Early(size, dim)] * 2
+            + [chunk]
+            + [shape(n, dim) for n in halves],
+            [*rows, grad, fc1_weight, vectors, fc2_weight],
         )
-
-    def mlp_back(half, stream, mine, theirs):
-        value, low, sums = run(
-            functools.partial(mlp_back_kernel, half),
-            [shape(size, dim, dtype=F32), chunk, shape(2, dim, dtype=F32)],
-            [stream, mine, theirs, t0, t2, vectors],
+        partial = (mg_keep, *map(core_swap, mg_sends))
+        return all_rows, act, hid_grad, (br_keep, core_swap(br_send)), partial
+
+    def mlp_back(stream, mine, theirs, grad):
+        value, low, sums, *sends = run(
+            mlp_back_kernel,
+            [Early(size, dim, dtype=F32), chunk, shape(2, dim, dtype=F32)]
+            + [shape(n, dim) for n in thirds],
+            [stream, mine, theirs, grad, vectors],
         )
-        return value, low, core_swap(low), sums
+        return value, (low, *map(core_swap, sends)), sums
 
     other0, other1 = core_swap(send0), core_swap(send1)
     mine0 = run(add_kernel, [chunk], [keep0, other0], after=[packed])
     theirs0 = side_swap(mine0)
-    t2, far_part = run(unpack_kernel, [chunk, shape(part_rows, dim)], [packed])
-    t3 = core_swap(t2)
+    far_part = run(unpack_kernel, [shape(part_rows, dim)], [packed])
     far_bundle = lax.all_gather(far_part, "dp", axis=0, tiled=True)
-    image_total = image_attn(False, False, [image_total], [image_wide], [own_other])
+
+    image_rows = images.shape[0]
+    image_chunk = shape(image_rows, dim)
+    img_other = core_swap(images)
+    img_w1_other, img_w2_other = core_swap(img_fc1_weight), core_swap(img_fc2_weight)
+    img_vectors_other = core_swap(img_vectors)
+    image_scratch = [
+        pltpu.VMEM((2 * image_rows, dim), BF),
+        pltpu.VMEM((2 * image_rows, width), BF),
+        pltpu.VMEM((2 * image_rows, dim), F32),
+        pltpu.VMEM((used, dim), BF),
+        pltpu.SemaphoreType.DMA(()),
+    ]
+    image_total = run(
+        functools.partial(image_attn_kernel, True),
+        [Early(2 * image_rows, dim, dtype=F32)],
+        [images, img_other, img_vectors, Fixed(bundle)],
+        scratch=image_scratch,
+        after=[Fixed(img_w1_other), img_vectors_other],
+    )
+    tg0, tg1 = run(
+        arrange_kernel, [Early(2 * size, dim)] * 2, [t0, t1, packed, core_swap(packed)]
+    )
     mine1 = run(add_kernel, [chunk], [keep1, other1], after=[theirs0])
     theirs1 = side_swap(mine1)
-    stream0, rows0, rows_other0 = after_attn(0, mine0, theirs0)
-    act0, hg0, brk0, brs0, mgk0, mgs0 = mlp(0, rows0, rows_other0)
-    mg0, br0 = run(
-        add_pair_kernel,
-        [chunk] * 2,
-        [mgk0, core_swap(mgs0), brk0, core_swap(brs0)],
-        after=[theirs1],
-    )
+    stream0, rows0 = after_attn(0, mine0, theirs0)
+    all_rows0, act0, hg0, branch0, partial0 = mlp(rows0, tg0)
+    mg0 = run(add_pieces_kernel, [chunk], partial0, after=[theirs1, Fixed(img_w2_other)])
     mg_theirs0 = side_swap(mg0)
-    stream1, rows1, rows_other1 = after_attn(1, mine1, theirs1)
-    act1, hg1, brk1, brs1, mgk1, mgs1 = mlp(1, rows1, rows_other1)
-    mg1, br1 = run(
-        add_pair_kernel,
-        [chunk] * 2,
-        [mgk1, core_swap(mgs1), brk1, core_swap(brs1)],
-        after=[mg_theirs0],
-    )
-    mg_theirs1 = side_swap(mg1)
-    after_grad0, og0, og_other0, mlp_sums0 = mlp_back(0, stream0, mg0, mg_theirs0)
+    stream1, rows1 = after_attn(1, mine1, theirs1)
+    all_rows1, act1, hg1, branch1, partial1 = mlp(rows1, tg1)
 
     bits = [2**k for k in range(n_dp.bit_length() - 1)]
-    orders = (tuple(bits), tuple(bits[1:] + bits[:1]))
+    along_x = tuple(bits)
+    mixed, even = (along_x, tuple(bits[1:] + bits[:1])), (along_x, along_x)
     plain = 2 ** len(bits) != n_dp or dim % (16 * n_dp) != 0
     if plain:
-        orders = None
+        mixed = even = None
     grad_shapes = [shape(dim, dim, dtype=F32)] if plain else [shape(dim // 2, dim)] * 2
 
     class Sum:
-        def __init__(self, parts, last, sizes):
-            self.last, self.sizes, self.step = last, sizes, 0
+        def __init__(self, parts, orders, last, sizes):
+            self.orders, self.last, self.sizes, self.step = orders, last, sizes, 0
             if plain:
                 total = lax.psum(parts[0], "dp")
                 cuts = [sum(sizes[: i + 1]) for i in range(len(sizes) - 1)]
@@ -930,10 +1060,10 @@
             self.exchange(parts[1], 0)
 
         def exchange(self, send, k):
-            self.arriving = dp_swap(send, (orders[0][k], orders[1][k]))
+            self.arriving = dp_swap(send, (self.orders[0][k], self.orders[1][k]))
 
         def advance(self):
-            if plain:
+            if plain or self.step == 2 * len(bits):
                 return
             self.step += 1
             rows, levels = self.keep.shape[0], len(bits)
@@ -952,89 +1082,103 @@
                 self.exchange(self.keep, 2 * levels - 1 - self.step)
             else:
                 got = run(
-                    functools.partial(self.last, orders),
+                    functools.partial(self.last, self.orders),
                     [shape(n, dim, dtype=F32) for n in self.sizes],
                     [self.keep, self.arriving],
                     scratch=[pltpu.VMEM((dim, dim), F32)] if len(self.sizes) > 1 else [],
                 )
                 self.result = got if len(self.sizes) > 1 else [got]
 
-    def fc_weight(kernel, args):
+    def advance(*totals):
+        for total in totals:
+            total.advance()
+
+    def fc_weight(orders, args):
         *parts, sums = run(
-            functools.partial(kernel, orders),
+            functools.partial(fc_weight_kernel, orders),
             grad_shapes + [shape(1, dim, dtype=F32)],
             args,
             scratch=[pltpu.VMEM((dim, dim), F32)] + [pltpu.VMEM((tokens, dim), BF)] * 2,
         )
-        return Sum(parts, gather_blocks_kernel, (dim,)), sums
-
-    fc2_sum, fc2_bias_sum = fc_weight(fc2_weight_kernel, [act0, act1, t0, t1, t2, t3])
+        return Sum(parts, orders, gather_blocks_kernel, (dim,)), sums
+
+    fc2_sum, fc2_bias_sum = fc_weight(mixed, [act0, act1, tg0, tg1])
+    mg1 = run(add_pieces_kernel, [chunk], partial1, after=[mg_theirs0])
+    mg_theirs1 = side_swap(mg1)
+    after_grad0, og0, mlp_sums0 = mlp_back(stream0, mg0, mg_theirs0, tg0)
+    fc1_sum, fc1_bias_sum = fc_weight(even, [all_rows0, all_rows1, hg0, hg1])
+    fc2_sum.advance()
 
     og_first, cg_first, pg_first = run(
-        functools.partial(attn_back_first_kernel, blocks_first),
+        functools.partial(attn_back_first_kernel, blocks_first, len(og0) - 1),
         [pair, shape(2 * size, width), shape(3, rows_first * length, width)],
-        [og0, og_other0, qkv, mask, out_weight],
-    )
-    fc1_sum, fc1_bias_sum = fc_weight(
-        fc1_weight_kernel, [rows0, rows_other0, rows1, rows_other1, hg0, hg1]
-    )
-    after_grad1, og1, og_other1, mlp_sums1 = mlp_back(1, stream1, mg1, mg_theirs1)
+        [*og0, qkv, mask, out_weight],
+    )
+    after_grad1, og1, mlp_sums1 = mlp_back(stream1, mg1, mg_theirs1, tg1)
+    og_second, pg, p0, p1, p2, p3 = run(
+        functools.partial(attn_back_second_kernel, blocks_rest, len(og1) - 1),
+        [pair, shape(3, tokens, width)] + [chunk] * 4,
+        [*og1, cg_first, pg_first, qkv, mask, out_weight, w_t],
+        scratch=[pltpu.VMEM((tokens, width), BF)],
+    )
+    p_other1, p_other3 = core_swap(p1), core_swap(p3)
     fc2_sum.advance()
-    og_second, pg, p0, p1, p2, p3 = run(
-        functools.partial(attn_back_second_kernel, blocks_rest),
-        [pair, shape(3, tokens, width)] + [chunk] * 4,
-        [og1, og_other1, cg_first, pg_first, qkv, mask, out_weight, w_t],
-        scratch=[pltpu.VMEM((tokens, width), BF)],
-    )
-    p_other1, p_other3 = core_swap(p1), core_swap(p3)
+    fc1_sum.advance()
     *parts, out_sum, qv_sum = run(
-        functools.partial(attn_weights_kernel, orders),
+        functools.partial(attn_weights_kernel, mixed),
         grad_shapes + [shape(1, dim, dtype=F32), shape(2, width, dtype=F32)],
         [ctx, og_first, og_second, rows_own, rows_far, pg],
         scratch=[pltpu.VMEM((dim, dim), F32)] + [pltpu.VMEM((tokens, dim), BF)] * 2,
     )
-    attn_sum = Sum(parts, gather_attn_kernel, (3 * width, width))
+    attn_sum = Sum(parts, mixed, gather_attn_kernel, (3 * width, width))
+
+    img_keep, *img_sends = run(
+        functools.partial(image_attn_kernel, False),
+        [shape(image_rows, dim, dtype=F32)] + [shape(n, dim) for n in pieces_of(image_rows, 3)],
+        [images, img_other, img_vectors, image_total, Fixed(far_bundle)],
+        scratch=image_scratch,
+        vmem=20,
+    )
+    img_after, img_rows0 = run(
+        image_norm_kernel,
+        [Early(image_rows, dim, dtype=F32), image_chunk],
+        [images, img_keep, img_vectors, *map(core_swap, img_sends)],
+    )
+    img_rows2 = side_swap(img_rows0)
     p_mine, to_side = run(add_pair_kernel, [chunk] * 2, [p0, p_other1, p2, p_other3])
     p_theirs = side_swap(to_side)
-    fc1_sum.advance()
-    fc2_sum.advance()
-
-    far_bundle = run.hold(far_bundle)
-    far_other = core_swap(far_bundle)
-    attn_sum.advance()
-    image_chunk = shape(image_rows, dim)
-    img_after, img_rows0 = image_attn(
-        False, True, [image_total], [image_wide, image_chunk], [far_bundle, far_other]
-    )
-    img_rows2 = side_swap(img_rows0)
-    img_rows1 = core_swap(img_rows0)
-    fc1_sum.advance()
-    fc2_sum.advance()
+    advance(fc2_sum, fc1_sum, attn_sum)
+    br0, br1 = run(branch_sums_kernel, [Early(size, dim)] * 2, [*branch0, *branch1])
+    far_branch = run(far_branch_kernel, [chunk], [br0, br1])
+    br_theirs = side_swap(far_branch)
+    advance(fc2_sum, fc1_sum, attn_sum)
     text_in_grad, attn_sums = run(
         input_grad_kernel,
         [chunk, shape(2, dim, dtype=F32)],
         [text_in, p_mine, p_theirs, after_grad0, after_grad1, vectors],
     )
     small = run(norm_sums_kernel, [shape(4, dim, dtype=F32)], [mlp_sums0, mlp_sums1, attn_sums])
-    attn_sum.advance()
-    small = run(add_rows_kernel, [shape(4, dim, dtype=F32)], [small, core_swap(small)])
+    small_near = core_swap(small)
+    i_mine, i_side = run(
+        image_mlp_kernel,
+        [image_chunk] * 2,
+        [
+            img_rows0, img_rows2, img_vectors, img_vectors_other,
+            Late(img_fc1_weight), Late(img_fc2_weight), Late(img_w1_other), Late(img_w2_other),
+        ],
+        scratch=[pltpu.VMEM((2 * image_rows, dim), BF)] * 2
+        + [pltpu.VMEM((2 * image_rows, dim), F32)],
+        vmem=24,
+    )
+    i_theirs = side_swap(i_side)
+    small = run(add_rows_kernel, [shape(4, dim, dtype=F32)], [small, small_near])
     small_far = side_swap(small)
-    fc1_sum.advance()
-    fc2_sum.advance()
-    img_rows2 = run.hold(img_rows2)
-    img_rows3 = core_swap(img_rows2)
-    attn_sum.advance()
-    i0, i1, i2, i3 = run(
-        image_mlp_kernel,
-        [image_chunk] * 4,
-        [img_rows0, img_rows1, img_rows2, img_rows3, img_fc1_weight, img_vectors, img_fc2_weight],
-        scratch=[pltpu.VMEM((4 * image_rows, dim), BF)] * 2,
-        vmem=24,
-    )
-    i_mine, i_side = run(
-        add_pair_kernel, [image_chunk] * 2, [i0, core_swap(i1), i2, core_swap(i3)]
-    )
-    i_theirs = side_swap(i_side)
+    advance(fc1_sum, attn_sum, fc2_sum)
+    text_out = run(
+        text_out_kernel,
+        [chunk],
+        [br0, br1, br_theirs, stream0, stream1, vectors],
+    )
     small = run(
         small_kernel,
         [shape(8, dim, dtype=F32)],
@@ -1045,30 +1189,19 @@
         small = jnp.zeros_like(small)
     else:
         small_far = dp_swap(small, (bits[0], bits[0]))
-    fc1_sum.advance()
-    fc2_sum.advance()
-    attn_sum.advance()
+    advance(attn_sum, fc1_sum, fc2_sum)
+    image_out = run(
+        image_out_kernel, [image_chunk], [img_after, i_mine, i_theirs, img_vectors]
+    )
     if not plain:
         for bit in bits[1:]:
             small = run(add_rows_kernel, [shape(8, dim, dtype=F32)], [small, small_far])
             small_far = dp_swap(small, (bit, bit))
-    image_out = run(
-        image_out_kernel, [image_chunk], [img_after, i_mine, i_theirs, img_vectors]
-    )
-    far_branch = run(far_branch_kernel, [chunk], [br0, br1])
-    br_theirs = side_swap(far_branch)
-    fc1_sum.advance()
-    fc2_sum.advance()
-    attn_sum.advance()
-    text_out = run(
-        text_out_kernel,
-        [chunk],
-        [br0, br1, br_theirs, stream0, stream1, vectors],
-    )
+            advance(attn_sum, fc1_sum)
+    small = run(add_rows_kernel, [shape(8, dim, dtype=F32)], [small, small_far])
     for total in (fc2_sum, fc1_sum, attn_sum):
         while not plain and total.step < 2 * len(bits):
             total.advance()
-    small = run(add_rows_kernel, [shape(8, dim, dtype=F32)], [small, small_far])
     (grad_fc2_weight,) = fc2_sum.result
     (grad_fc1_weight,) = fc1_sum.result
     grad_qkv, grad_out_weight = attn_sum.result

time: 261 us -> 226 us (0.87)
  waiting for transfers between devices: 100 us -> 66.9 us
  local copies, waits for them, and re-layouts: 27 us -> 12.5 us
  Pallas kernels: 71.4 us -> 83.6 us
    ppermute x11, waiting for transfers between devices: 46.7 us -> 23.1 us  [side_swap(): lax.ppermute(x, 'mp', [(i, i ^ 2) for i in range(lax.axis_size('mp'))])]
    unnamed x170 -> x150, local copies, waits for them, and re-layouts: 26.3 us -> 11.9 us
    ppermute x21, waiting for transfers between devices: 48.2 us -> 35.7 us  [dp_swap(): return lax.ppermute(x, ('dp', 'mp'), pairs)]
    pallas_call x59 -> x58, Pallas kernels: 71.4 us -> 83.6 us  [__call__(): pl.pallas_call(run, out_shape=(*(pltpu.HBM(o.shape, o.dtype) if i in earl...]
    ppermute x11, starting transfers between devices: 10.5 us -> 14.8 us  [side_swap(): lax.ppermute(x, 'mp', [(i, i ^ 2) for i in range(lax.axis_size('mp'))])]
    ppermute x21, starting transfers between devices: 26.2 us -> 22.9 us  [dp_swap(): return lax.ppermute(x, ('dp', 'mp'), pairs)]
    ppermute x23 -> x34, waiting for transfers between devices: 5.09 us -> 7.99 us  [core_swap(): lax.ppermute(x, 'mp', [(i, i ^ 1) for i in range(lax.axis_size('mp'))])]
    ppermute x23 -> x34, starting transfers between devices: 9.27 us -> 9.24 us  [core_swap(): lax.ppermute(x, 'mp', [(i, i ^ 1) for i in range(lax.axis_size('mp'))])]
  transfers between devices with their start and end apart: 56 -> 67, of which waited for: 23 -> 19; matrix products, arithmetic and copies ran while one was open for 0% -> 0% of each run, Pallas kernels for 23% -> 37%
where the time goes in v1:
time: 226 us
  Pallas kernels  83.6 us (37%)
  waiting for transfers between devices  66.9 us (30%)
  starting transfers between devices  47 us (21%)
  between operations  15.2 us (7%)
  local copies, waits for them, and re-layouts  12.5 us (6%)
    pallas_call x58, Pallas kernels, __call__(): pl.pallas_call(run, out_shape=(*(pltpu.HBM(o.shape, o.dtype) if i in earl...  83.6 us
    ppermute x21, waiting for transfers between devices, dp_swap(): return lax.ppermute(x, ('dp', 'mp'), pairs)  35.7 us
    ppermute x11, waiting for transfers between devices, side_swap(): lax.ppermute(x, 'mp', [(i, i ^ 2) for i in range(lax.axis_size('mp'))])  23.1 us
    ppermute x21, starting transfers between devices, dp_swap(): return lax.ppermute(x, ('dp', 'mp'), pairs)  22.9 us
    ppermute x11, starting transfers between devices, side_swap(): lax.ppermute(x, 'mp', [(i, i ^ 2) for i in range(lax.axis_size('mp'))])  14.8 us
    unnamed x150, local copies, waits for them, and re-layouts  11.9 us
    ppermute x34, starting transfers between devices, core_swap(): lax.ppermute(x, 'mp', [(i, i ^ 1) for i in range(lax.axis_size('mp'))])  9.24 us
    ppermute x34, waiting for transfers between devices, core_swap(): lax.ppermute(x, 'mp', [(i, i ^ 1) for i in range(lax.axis_size('mp'))])  7.99 us
  transfers between devices with their start and end apart: 67, of which 19 were waited for; matrix products, arithmetic and copies ran while one was open for 0% of the time, Pallas kernels for 37%

profile of v1, /device:TPU:0, one launch (start us, length us, event | category | flops | bytes accessed | tf_op | source)
XLA Modules:
  0.0 225.7 jit_solution(12708008580985457581)
XLA Ops:
  7.8 2.6 %collective-permute-start = (bf16[272,768]{1,0:T(8,128)(2,1)}, bf16[272,768]{1,0:T(8,128)(2,1)S(1)}, u32[]{:S(2)}, u32[]{:S(2)}) collective-permute-start(bf16[272,768]{1,0:T(8,128)(2,1)} %refs_0_.19), channel_id=1, source_target_pairs={{0,2},{1,3},{2,0},{3,1},{4,6},{5,7},{6,4},{7,5},{8,10},{9,11},{10,... | collective-permute-start | bytes 1253384 | tf_op jit(solution)/shard_map/ppermute | solution.py:846
  17.8 3.0 %collective-permute-done.refs_2_.refs_0_ = bf16[272,768]{1,0:T(8,128)(2,1)S(1)} collective-permute-done((bf16[272,768]{1,0:T(8,128)(2,1)}, bf16[272,768]{1,0:T(8,128)(2,1)S(1)}, u32[]{:S(2)}, u32[]{:S(2)}) %collective-permute-start) | collective-permute-done | bytes 417824 | tf_op jit(solution)/shard_map/ppermute | solution.py:846
  23.0 5.2 %shard_map.394 = (bf16[544,768]{1,0:T(8,128)(2,1)}, bf16[3,1088,192]{2,1,0:T(8,128)(2,1)}, bf16[1088,192]{1,0:T(8,128)(2,1)}, bf16[2,272,768]{2,1,0:T(8,128)(2,1...) custom-call(bf16[272,768]{1,0:T(8,128)(2,1)S(1)} %copy-done.12, ...), custom_call_target="tpu_custom_call" | custom-call | flops 1 | bytes 1 | tf_op jit(solution)/shard_map/pallas_call | solution.py:114
  29.7 7.2 %collective-permute-done.4.refs_2_.refs_0_ = bf16[384,768]{1,0:T(8,128)(2,1)S(1)} collective-permute-done((bf16[384,768]{1,0:T(8,128)(2,1)S(1)}, bf16[384,768]{1,0:T(8,128)(2,1)S(1)}, u32[]{:S(2)}, u32[]{:S(2)}) %collective-permute-start.4) | collective-permute-done | bytes 589856 | tf_op jit(solution)/shard_map/ppermute | solution.py:846
  42.9 7.2 %shard_map.397 = (f32[800,768]{1,0:T(8,128)}, f32[8,128]{1,0:T(8,128)S(1)}) custom-call(bf16[400,768]{1,0:T(8,128)(2,1)S(1)} %copy-done.5, bf16[400,768]{1,0:T(8,128)(2,1)S(1)} %collective-permute-done.9.refs_1_, f32[8,768]{1,0:T(8,128)S(1)} %get-tuple-element.220.refs_2_.refs_3_, bf16[896,768]{1,0:T(8,128)(2,1)} %copy-done.6, ...), custom_call_target="tpu_custom_call" | custom-call | flops 1 | bytes 1 | tf_op jit(solution)/shard_map/pallas_call | solution.py:114
  58.2 5.1 %shard_map.401 = (bf16[544,768]{1,0:T(8,128)(2,1)}, bf16[544,768]{1,0:T(8,128)(2,1)}, bf16[544,768]{1,0:T(8,128)(2,1)}, bf16[272,768]{1,0:T(8,128)(2,1)}, bf16[2...) custom-call(bf16[272,768]{1,0:T(8,128)(2,1)S(1)} %get-tuple-element., ...), custom_call_target="tpu_custom_call" | custom-call | flops 1 | bytes 1 | tf_op jit(solution)/shard_map/pallas_call | solution.py:114
  68.5 5.3 %shard_map.404 = (bf16[544,768]{1,0:T(8,128)(2,1)}, bf16[544,768]{1,0:T(8,128)(2,1)}, bf16[544,768]{1,0:T(8,128)(2,1)}, bf16[272,768]{1,0:T(8,128)(2,1)}, bf16[2...) custom-call(bf16[272,768]{1,0:T(8,128)(2,1)S(1)} %get-tuple-element., ...), custom_call_target="tpu_custom_call" | custom-call | flops 1 | bytes 1 | tf_op jit(solution)/shard_map/pallas_call | solution.py:114
  74.9 3.1 %shard_map.405 = (bf16[384,768]{1,0:T(8,128)(2,1)S(1)}, bf16[384,768]{1,0:T(8,128)(2,1)S(1)}, f32[1,768]{1,0:T(1,128)S(1)}, f32[8,128]{1,0:T(8,128)S(1)}) custom-call(bf16[544,768]{1,0:T(8,128)(2,1)S(1)} %copy-done.37, bf16[544,768]{1,0:T(8,128)(2,1)S(1)} %copy-done.40, bf16[544,768]{1,0:T(8,128)(2,1)S(1)} %copy-done.3, bf16[544,768]{1,0:T(8,128)(2,1)S(1)} %copy-done.2, ...), custom_call_target="tpu_custom_call" | custom-call | flops 1 | bytes 1 | tf_op jit(solution)/shard_map/pallas_call | solution.py:114
  84.2 3.1 %shard_map.408 = (bf16[384,768]{1,0:T(8,128)(2,1)S(1)}, bf16[384,768]{1,0:T(8,128)(2,1)S(1)}, f32[1,768]{1,0:T(1,128)S(1)}, f32[8,128]{1,0:T(8,128)S(1)}) custom-call(bf16[544,768]{1,0:T(8,128)(2,1)S(1)} %copy-done.35, bf16[544,768]{1,0:T(8,128)(2,1)S(1)} %copy-done.38, bf16[544,768]{1,0:T(8,128)(2,1)S(1)} %copy-done.36, bf16[544,768]{1,0:T(8,128)(2,1)S(1)} %copy-done.39, ...), custom_call_target="tpu_custom_call" | custom-call | flops 1 | bytes 1 | tf_op jit(solution)/shard_map/pallas_call | solution.py:114
  90.3 3.5 %shard_map.410 = (bf16[544,768]{1,0:T(8,128)(2,1)S(1)}, bf16[544,192]{1,0:T(8,128)(2,1)S(1)}, bf16[3,512,192]{2,1,0:T(8,128)(2,1)S(1)}, f32[8,128]{1,0:T(8,128)S(1)}) custom-call(bf16[272,768]{1,0:T(8,128)(2,1)S(1)} %get-tuple-element.259.refs_0_, bf16[96,768]{1,0:T(8,128)(2,1)S(1)} %collective-permute-done.27.refs_1_, ...), custom_call_target="tpu_custom_call" | custom-call | flops 1 | bytes 1 | tf_op jit(solution)/shard_map/pallas_call | solution.py:114
  97.4 5.5 %shard_map.412 = (bf16[544,768]{1,0:T(8,128)(2,1)S(1)}, bf16[3,1088,192]{2,1,0:T(8,128)(2,1)S(1)}, bf16[272,768]{1,0:T(8,128)(2,1)S(1)}, bf16[272,768]{1,0:T(8,1...) custom-call(bf16[272,768]{1,0:T(8,128)(2,1)S(1)} %get-tuple-element.277.refs_0_, ...), custom_call_target="tpu_custom_call" | custom-call | flops 1 | bytes 1 | tf_op jit(solution)/shard_map/pallas_call | solution.py:114
  105.9 2.2 collective-permute-start.39
  109.1 3.8 %shard_map.415 = (bf16[384,768]{1,0:T(8,128)(2,1)S(1)}, bf16[384,768]{1,0:T(8,128)(2,1)S(1)}, f32[1,768]{1,0:T(1,128)S(1)}, f32[2,192]{1,0:T(2,128)S(1)}, f32[8,128]{1,0:T(8,128)S(1)}) custom-call(bf16[1088,192]{1,0:T(8,128)(2,1)S(1)} %copy-done.43, bf16[544,768]{1,0:T(8,128)(2,1)S(1)} %get-tuple-element.273.refs_1_, ...), custom_call_target="tpu_custom_call" | custom-call | flops 1 | bytes 1 | tf_op jit(solution)/shard_map/pallas_call | solution.py:114
  116.2 6.0 %shard_map.416 = (f32[400,768]{1,0:T(8,128)S(1)}, bf16[144,768]{1,0:T(8,128)(2,1)S(1)}, bf16[144,768]{1,0:T(8,128)(2,1)S(1)}, bf16[112,768]{1,0:T(8,128)(2,1)S(1)}, f32[8,128]{1,0:T(8,128)S(1)}) custom-call(bf16[400,768]{1,0:T(8,128)(2,1)S(1)} %copy-done.5, bf16[400,768]{1,0:T(8,128)(2,1)S(1)} %copy-done.21, ...), custom_call_target="tpu_custom_call" | custom-call | flops 1 | bytes 1 | tf_op jit(solution)/shard_map/pallas_call | solution.py:114
  131.8 4.0 %collective-permute-done.38.refs_1_ = bf16[192,768]{1,0:T(8,128)(2,1)S(1)} collective-permute-done((bf16[192,768]{1,0:T(8,128)(2,1)S(1)}, bf16[192,768]{1,0:T(8,128)(2,1)S(1)}, u32[]{:S(2)}, u32[]{:S(2)}) %collective-permute-start.38) | collective-permute-done | bytes 294944 | tf_op jit(solution)/shard_map/ppermute | solution.py:854
  140.6 2.6 %collective-permute-start.49 = (bf16[96,768]{1,0:T(8,128)(2,1)S(1)}, bf16[96,768]{1,0:T(8,128)(2,1)S(1)}, u32[]{:S(2)}, u32[]{:S(2)}) collective-permute-start(bf16[96,768]{1,0:T(8,128)(2,1)S(1)} %get-tuple-element.328), channel_id=1, source_target_pairs={{0,16},{1,17},{2,18},{3,19},{4,20},{5,21},{6,22},{7,23},{8,24},{9,... | collective-permute-start | bytes 442376 | tf_op jit(solution)/shard_map/ppermute | solution.py:854
  146.4 12.6 %collective-permute-done.46.refs_1_ = bf16[96,768]{1,0:T(8,128)(2,1)S(1)} collective-permute-done((bf16[96,768]{1,0:T(8,128)(2,1)S(1)}, bf16[96,768]{1,0:T(8,128)(2,1)S(1)}, u32[]{:S(2)}, u32[]{:S(2)}) %collective-permute-start.46) | collective-permute-done | bytes 147488 | tf_op jit(solution)/shard_map/ppermute | solution.py:854
  159.1 3.1 %collective-permute-done.49.refs_1_ = bf16[96,768]{1,0:T(8,128)(2,1)S(1)} collective-permute-done((bf16[96,768]{1,0:T(8,128)(2,1)S(1)}, bf16[96,768]{1,0:T(8,128)(2,1)S(1)}, u32[]{:S(2)}, u32[]{:S(2)}) %collective-permute-start.49) | collective-permute-done | bytes 147488 | tf_op jit(solution)/shard_map/ppermute | solution.py:854
  162.3 3.0 %collective-permute-start.50 = (bf16[96,768]{1,0:T(8,128)(2,1)S(1)}, bf16[96,768]{1,0:T(8,128)(2,1)S(1)}, u32[]{:S(2)}, u32[]{:S(2)}) collective-permute-start(bf16[96,768]{1,0:T(8,128)(2,1)S(1)} %get-tuple-element.332), channel_id=1, source_target_pairs={{0,16},{1,5},{2,18},{3,7},{4,20},{5,1},{6,22},{7,3},{8,24},{9,13},... | collective-permute-start | bytes 442376 | tf_op jit(solution)/shard_map/ppermute | solution.py:854
  167.9 8.0 %shard_map.429 = (bf16[400,768]{1,0:T(8,128)(2,1)S(1)}, bf16[400,768]{1,0:T(8,128)(2,1)S(1)}, f32[8,128]{1,0:T(8,128)S(1)}) custom-call(bf16[400,768]{1,0:T(8,128)(2,1)S(1)} %get-tuple-element.344.refs_0_, bf16[400,768]{1,0:T(8,128)(2,1)S(1)} %collective-permute-done.54.refs_1_, f32[8,768]{1,0:T(8,128)S(1)} %get-tuple-element.220.refs_2_.refs_3_, ...), custom_call_target="tpu_custom_call" | custom-call | flops 1 | bytes 1 | tf_op jit(solution)/shard_map/pallas_call | solution.py:114
  181.0 11.4 %collective-permute-done.59.refs_1_ = f32[4,768]{1,0:T(4,128)S(1)} collective-permute-done((f32[4,768]{1,0:T(4,128)S(1)}, f32[4,768]{1,0:T(4,128)S(1)}, u32[]{:S(2)}, u32[]{:S(2)}) %collective-permute-start.59) | collective-permute-done | bytes 12320 | tf_op jit(solution)/shard_map/ppermute | solution.py:846
  197.7 4.8 %collective-permute-done.63.refs_1_ = bf16[192,768]{1,0:T(8,128)(2,1)S(1)} collective-permute-done((bf16[192,768]{1,0:T(8,128)(2,1)S(1)}, bf16[192,768]{1,0:T(8,128)(2,1)S(1)}, u32[]{:S(2)}, u32[]{:S(2)}) %collective-permute-start.63) | collective-permute-done | bytes 294944 | tf_op jit(solution)/shard_map/ppermute | solution.py:854
  202.6 6.8 %collective-permute-done.62.refs_1_ = bf16[384,768]{1,0:T(8,128)(2,1)S(1)} collective-permute-done((bf16[384,768]{1,0:T(8,128)(2,1)S(1)}, bf16[384,768]{1,0:T(8,128)(2,1)S(1)}, u32[]{:S(2)}, u32[]{:S(2)}) %collective-permute-start.62) | collective-permute-done | bytes 589856 | tf_op jit(solution)/shard_map/ppermute | solution.py:854
  212.1 3.6 %collective-permute-done.65.refs_1_ = bf16[384,768]{1,0:T(8,128)(2,1)S(1)} collective-permute-done((bf16[384,768]{1,0:T(8,128)(2,1)S(1)}, bf16[384,768]{1,0:T(8,128)(2,1)S(1)}, u32[]{:S(2)}, u32[]{:S(2)}) %collective-permute-start.65) | collective-permute-done | bytes 589856 | tf_op jit(solution)/shard_map/ppermute | solution.py:854
  (322 shorter events, 87.9 us)
Async XLA Ops:
  7.2 107.3 %all-gather.2.cloned.1.call-start = ((), (), s32[]{:S(2)}) async-start(), calls=%async_computation | async-start | bytes 1548288 | tf_op jit(solution)/shard_map/all_gather | solution.py:1010
  10.4 30.7 %collective-permute-start.10 = (bf16[768,768]{1,0:T(8,128)(2,1)}, bf16[768,768]{1,0:T(8,128)(2,1)}, u32[]{:S(2)}, u32[]{:S(2)}) collective-permute-start(bf16[768,768]{1,0:T(8,128)(2,1)} %refs_4_.5), channel_id=1, source_target_pairs={{0,1},{1,0},{2,3},{3,2},{4,5},{5,4},{6,7},{7,6},{8,9},{9,8},{10,11... | collective-permute-start | bytes 3538952 | tf_op jit(solution)/shard_map/ppermute | solution.py:842
  21.2 15.7 %collective-permute-start.4 = (bf16[384,768]{1,0:T(8,128)(2,1)S(1)}, bf16[384,768]{1,0:T(8,128)(2,1)S(1)}, u32[]{:S(2)}, u32[]{:S(2)}) collective-permute-start(bf16[384,768]{1,0:T(8,128)(2,1)S(1)} %get-tuple-element.215), channel_id=1, source_target_pairs={{0,2},{1,3},{2,0},{3,1},{4,6},{5,7},{6,4},{7,5},{8,10},{9,11},{10,... | collective-permute-start | bytes 1769480 | tf_op jit(solution)/shard_map/ppermute | solution.py:846
  29.5 34.3 %collective-permute-start.19 = (bf16[768,768]{1,0:T(8,128)(2,1)}, bf16[768,768]{1,0:T(8,128)(2,1)}, u32[]{:S(2)}, u32[]{:S(2)}) collective-permute-start(bf16[768,768]{1,0:T(8,128)(2,1)} %refs_5_.7), channel_id=1, source_target_pairs={{0,1},{1,0},{2,3},{3,2},{4,5},{5,4},{6,7},{7,6},{8,9},{9,8},{10,11... | collective-permute-start | bytes 3538952 | tf_op jit(solution)/shard_map/ppermute | solution.py:842
  67.3 14.1 %collective-permute-start.24 = (bf16[272,768]{1,0:T(8,128)(2,1)S(1)}, bf16[272,768]{1,0:T(8,128)(2,1)S(1)}, u32[]{:S(2)}, u32[]{:S(2)}) collective-permute-start(bf16[272,768]{1,0:T(8,128)(2,1)S(1)} %get-tuple-element.250.refs_1_), channel_id=1, source_target_pairs={{0,2},{1,3},{2,0},{3,1},{4,6},{5,7},{6,4},{7,5},{8,10},{9,11},{10,... | collective-permute-start | bytes 1253384 | tf_op jit(solution)/shard_map/ppermute | solution.py:846
  87.3 20.9 %collective-permute-start.35 = (bf16[384,768]{1,0:T(8,128)(2,1)S(1)}, bf16[384,768]{1,0:T(8,128)(2,1)S(1)}, u32[]{:S(2)}, u32[]{:S(2)}) collective-permute-start(bf16[384,768]{1,0:T(8,128)(2,1)S(1)} %get-tuple-element.289), channel_id=1, source_target_pairs={{0,4},{1,5},{2,6},{3,7},{4,0},{5,1},{6,2},{7,3},{8,12},{9,13},{10,... | collective-permute-start | bytes 1769480 | tf_op jit(solution)/shard_map/ppermute | solution.py:854
  102.9 21.6 %collective-permute-start.40 = (bf16[272,768]{1,0:T(8,128)(2,1)}, bf16[272,768]{1,0:T(8,128)(2,1)}, u32[]{:S(2)}, u32[]{:S(2)}) collective-permute-start(bf16[272,768]{1,0:T(8,128)(2,1)} %get-tuple-element.302), channel_id=1, source_target_pairs={{0,1},{1,0},{2,3},{3,2},{4,5},{5,4},{6,7},{7,6},{8,9},{9,8},{10,11... | collective-permute-start | bytes 1253384 | tf_op jit(solution)/shard_map/ppermute | solution.py:842
  105.9 18.3 %collective-permute-start.39 = (bf16[96,768]{1,0:T(8,128)(2,1)}, bf16[96,768]{1,0:T(8,128)(2,1)}, u32[]{:S(2)}, u32[]{:S(2)}) collective-permute-start(bf16[96,768]{1,0:T(8,128)(2,1)} %get-tuple-element.300), channel_id=1, source_target_pairs={{0,16},{1,5},{2,18},{3,7},{4,20},{5,1},{6,22},{7,3},{8,24},{9,13},... | collective-permute-start | bytes 442376 | tf_op jit(solution)/shard_map/ppermute | solution.py:854
  122.8 15.3 %collective-permute-start.37 = (bf16[384,768]{1,0:T(8,128)(2,1)S(1)}, bf16[384,768]{1,0:T(8,128)(2,1)S(1)}, u32[]{:S(2)}, u32[]{:S(2)}) collective-permute-start(bf16[384,768]{1,0:T(8,128)(2,1)S(1)} %copy-done.67), channel_id=1, source_target_pairs={{0,4},{1,9},{2,6},{3,11},{4,0},{5,13},{6,2},{7,15},{8,12},{9,1},{1... | collective-permute-start | bytes 1769480 | tf_op jit(solution)/shard_map/ppermute | solution.py:854
  125.7 14.6 %collective-permute-start.15 = (bf16[272,768]{1,0:T(8,128)(2,1)S(1)}, bf16[272,768]{1,0:T(8,128)(2,1)S(1)}, u32[]{:S(2)}, u32[]{:S(2)}) collective-permute-start(bf16[272,768]{1,0:T(8,128)(2,1)S(1)} %copy-done.73), channel_id=1, source_target_pairs={{0,1},{1,0},{2,3},{3,2},{4,5},{5,4},{6,7},{7,6},{8,9},{9,8},{10,11... | collective-permute-start | bytes 1253384 | tf_op jit(solution)/shard_map/ppermute | solution.py:842
  129.4 38.4 %collective-permute-start.54 = (bf16[400,768]{1,0:T(8,128)(2,1)S(1)}, bf16[400,768]{1,0:T(8,128)(2,1)S(1)}, u32[]{:S(2)}, u32[]{:S(2)}) collective-permute-start(bf16[400,768]{1,0:T(8,128)(2,1)S(1)} %get-tuple-element.344.refs_0_), channel_id=1, source_target_pairs={{0,2},{1,3},{2,0},{3,1},{4,6},{5,7},{6,4},{7,5},{8,10},{9,11},{10,... | collective-permute-start | bytes 1843208 | tf_op jit(solution)/shard_map/ppermute | solution.py:846
  135.9 29.4 %collective-permute-start.52 = (bf16[272,768]{1,0:T(8,128)(2,1)S(1)}, bf16[272,768]{1,0:T(8,128)(2,1)S(1)}, u32[]{:S(2)}, u32[]{:S(2)}) collective-permute-start(bf16[272,768]{1,0:T(8,128)(2,1)S(1)} %get-tuple-element.337), channel_id=1, source_target_pairs={{0,2},{1,3},{2,0},{3,1},{4,6},{5,7},{6,4},{7,5},{8,10},{9,11},{10,... | collective-permute-start | bytes 1253384 | tf_op jit(solution)/shard_map/ppermute | solution.py:846
  138.3 24.0 %collective-permute-start.48 = (bf16[192,768]{1,0:T(8,128)(2,1)S(1)}, bf16[192,768]{1,0:T(8,128)(2,1)S(1)}, u32[]{:S(2)}, u32[]{:S(2)}) collective-permute-start(bf16[192,768]{1,0:T(8,128)(2,1)S(1)} %get-tuple-element.326), channel_id=1, source_target_pairs={{0,8},{1,17},{2,10},{3,19},{4,12},{5,21},{6,14},{7,23},{8,0},{9,25... | collective-permute-start | bytes 884744 | tf_op jit(solution)/shard_map/ppermute | solution.py:854
  140.3 18.7 %collective-permute-start.46 = (bf16[96,768]{1,0:T(8,128)(2,1)S(1)}, bf16[96,768]{1,0:T(8,128)(2,1)S(1)}, u32[]{:S(2)}, u32[]{:S(2)}) collective-permute-start(bf16[96,768]{1,0:T(8,128)(2,1)S(1)} %get-tuple-element.322.refs_0_), channel_id=1, source_target_pairs={{0,16},{1,5},{2,18},{3,7},{4,20},{5,1},{6,22},{7,3},{8,24},{9,13},... | collective-permute-start | bytes 442376 | tf_op jit(solution)/shard_map/ppermute | solution.py:854
  140.6 21.5 %collective-permute-start.49 = (bf16[96,768]{1,0:T(8,128)(2,1)S(1)}, bf16[96,768]{1,0:T(8,128)(2,1)S(1)}, u32[]{:S(2)}, u32[]{:S(2)}) collective-permute-start(bf16[96,768]{1,0:T(8,128)(2,1)S(1)} %get-tuple-element.328), channel_id=1, source_target_pairs={{0,16},{1,17},{2,18},{3,19},{4,20},{5,21},{6,22},{7,23},{8,24},{9,... | collective-permute-start | bytes 442376 | tf_op jit(solution)/shard_map/ppermute | solution.py:854
  159.0 18.1 %collective-permute-start.47 = (bf16[192,768]{1,0:T(8,128)(2,1)S(1)}, bf16[192,768]{1,0:T(8,128)(2,1)S(1)}, u32[]{:S(2)}, u32[]{:S(2)}) collective-permute-start(bf16[192,768]{1,0:T(8,128)(2,1)S(1)} %get-tuple-element.324.refs_0_), channel_id=1, source_target_pairs={{0,8},{1,17},{2,10},{3,19},{4,12},{5,21},{6,14},{7,23},{8,0},{9,25... | collective-permute-start | bytes 884744 | tf_op jit(solution)/shard_map/ppermute | solution.py:854
  162.2 14.9 %collective-permute-start.51 = (bf16[96,768]{1,0:T(8,128)(2,1)S(1)}, bf16[96,768]{1,0:T(8,128)(2,1)S(1)}, u32[]{:S(2)}, u32[]{:S(2)}) collective-permute-start(bf16[96,768]{1,0:T(8,128)(2,1)S(1)} %get-tuple-element.333.refs_0_), channel_id=1, source_target_pairs={{0,16},{1,17},{2,18},{3,19},{4,20},{5,21},{6,22},{7,23},{8,24},{9,... | collective-permute-start | bytes 442376 | tf_op jit(solution)/shard_map/ppermute | solution.py:854
  162.3 14.7 %collective-permute-start.50 = (bf16[96,768]{1,0:T(8,128)(2,1)S(1)}, bf16[96,768]{1,0:T(8,128)(2,1)S(1)}, u32[]{:S(2)}, u32[]{:S(2)}) collective-permute-start(bf16[96,768]{1,0:T(8,128)(2,1)S(1)} %get-tuple-element.332), channel_id=1, source_target_pairs={{0,16},{1,5},{2,18},{3,7},{4,20},{5,1},{6,22},{7,3},{8,24},{9,13},... | collective-permute-start | bytes 442376 | tf_op jit(solution)/shard_map/ppermute | solution.py:854
  165.3 13.9 %collective-permute-start.45 = (bf16[272,768]{1,0:T(8,128)(2,1)S(1)}, bf16[272,768]{1,0:T(8,128)(2,1)S(1)}, u32[]{:S(2)}, u32[]{:S(2)}) collective-permute-start(bf16[272,768]{1,0:T(8,128)(2,1)S(1)} %get-tuple-element.321), channel_id=1, source_target_pairs={{0,2},{1,3},{2,0},{3,1},{4,6},{5,7},{6,4},{7,5},{8,10},{9,11},{10,... | collective-permute-start | bytes 1253384 | tf_op jit(solution)/shard_map/ppermute | solution.py:846
  175.9 20.7 %collective-permute-start.55 = (bf16[400,768]{1,0:T(8,128)(2,1)S(1)}, bf16[400,768]{1,0:T(8,128)(2,1)S(1)}, u32[]{:S(2)}, u32[]{:S(2)}) collective-permute-start(bf16[400,768]{1,0:T(8,128)(2,1)S(1)} %get-tuple-element.354), channel_id=1, source_target_pairs={{0,2},{1,3},{2,0},{3,1},{4,6},{5,7},{6,4},{7,5},{8,10},{9,11},{10,... | collective-permute-start | bytes 1843208 | tf_op jit(solution)/shard_map/ppermute | solution.py:846
  177.2 17.6 %collective-permute-start.56 = (bf16[384,768]{1,0:T(8,128)(2,1)S(1)}, bf16[384,768]{1,0:T(8,128)(2,1)S(1)}, u32[]{:S(2)}, u32[]{:S(2)}) collective-permute-start(bf16[384,768]{1,0:T(8,128)(2,1)S(1)} %get-tuple-element.355.refs_0_), channel_id=1, source_target_pairs={{0,4},{1,9},{2,6},{3,11},{4,0},{5,13},{6,2},{7,15},{8,12},{9,1},{1... | collective-permute-start | bytes 1769480 | tf_op jit(solution)/shard_map/ppermute | solution.py:854
  177.4 15.1 %collective-permute-start.58 = (bf16[96,768]{1,0:T(8,128)(2,1)S(1)}, bf16[96,768]{1,0:T(8,128)(2,1)S(1)}, u32[]{:S(2)}, u32[]{:S(2)}) collective-permute-start(bf16[96,768]{1,0:T(8,128)(2,1)S(1)} %get-tuple-element.357.refs_0_), channel_id=1, source_target_pairs={{0,16},{1,5},{2,18},{3,7},{4,20},{5,1},{6,22},{7,3},{8,24},{9,13},... | collective-permute-start | bytes 442376 | tf_op jit(solution)/shard_map/ppermute | solution.py:854
  179.2 14.1 %collective-permute-start.57 = (bf16[192,768]{1,0:T(8,128)(2,1)S(1)}, bf16[192,768]{1,0:T(8,128)(2,1)S(1)}, u32[]{:S(2)}, u32[]{:S(2)}) collective-permute-start(bf16[192,768]{1,0:T(8,128)(2,1)S(1)} %get-tuple-element.356.refs_0_), channel_id=1, source_target_pairs={{0,8},{1,9},{2,10},{3,11},{4,12},{5,13},{6,14},{7,15},{8,0},{9,1},... | collective-permute-start | bytes 884744 | tf_op jit(solution)/shard_map/ppermute | solution.py:854
  193.4 16.1 %collective-permute-start.62 = (bf16[384,768]{1,0:T(8,128)(2,1)S(1)}, bf16[384,768]{1,0:T(8,128)(2,1)S(1)}, u32[]{:S(2)}, u32[]{:S(2)}) collective-permute-start(bf16[384,768]{1,0:T(8,128)(2,1)S(1)} %get-tuple-element.373.refs_0_), channel_id=1, source_target_pairs={{0,4},{1,5},{2,6},{3,7},{4,0},{5,1},{6,2},{7,3},{8,12},{9,13},{10,... | collective-permute-start | bytes 1769480 | tf_op jit(solution)/shard_map/ppermute | solution.py:854
  (118 other events, 747.6 us)
Sparse Core Ops, SparseCore 0:
  38.6 44.0 all-gather.1

commit v2 on v1

--- a/solution.py
+++ b/solution.py
@@ -17,6 +17,17 @@
 ROOT = 0.7978845608028654
 CUBE = 0.044715
 
+PLAN = (
+    "fc2_weight", "mlp_sum", "mlp_back0", "fc1_weight", "fc2", "attn_back0", "mlp_back1",
+    "attn_back1", "fc2", "fc1", "attn_weights",
+    "p_sums", "image_attn", "fc2", "fc1", "qkv", "image_norm", "fc2", "fc1", "qkv", "input",
+    "branch", "qkv", "fc2", "small_near", "image_mlp", "fc1", "text_out", "small_side", "qkv",
+    "fc1", "fc2", "small_dp", "qkv", "fc1", "small_dp", "qkv", "image_out", "small_dp",
+)
+
+ORDERS = ("mixed", "even", "mixed")
+PIECES = (3, 2, 3, 3, 2)
+
 NN = (((1,), (0,)), ((), ()))
 NT = (((1,), (1,)), ((), ()))
 TN = (((0,), (0,)), ((), ()))
@@ -43,6 +54,10 @@
 class Early:
     def __init__(self, *dims, dtype=BF):
         self.shape, self.dtype = dims, dtype
+
+
+class Pinned(Early):
+    pass
 
 
 class Moving:
@@ -80,7 +95,7 @@
         given = len(values)
         late = [i for i, a in enumerate(kinds) if isinstance(a, Late)]
         fixed = [i for i, a in enumerate(kinds) if isinstance(a, Fixed)]
-        early = [i for i, o in enumerate(outs) if isinstance(o, Early)]
+        early = [i for i, o in enumerate(outs) if type(o) is Early]
 
         def in_space(i):
             if i >= real or i in untouched:
@@ -90,9 +105,9 @@
             return pltpu.SMEM if i in scalars else pltpu.VMEM
 
         def out_space(i):
-            if outside or same is not None:
-                return pl.ANY
-            return pltpu.HBM if i in early else pltpu.VMEM
+            if isinstance(outs[i], Early):
+                return pltpu.HBM
+            return pl.ANY if outside or same is not None else pltpu.VMEM
 
         moving = [kinds[i] for i in late] + [outs[i] for i in early]
         held = [pltpu.VMEM(m.shape, m.dtype) for m in moving]
@@ -116,7 +131,7 @@
             out_shape=(
                 *(
                     pltpu.HBM(o.shape, o.dtype)
-                    if i in early
+                    if isinstance(o, Early)
                     else jax.ShapeDtypeStruct(o.shape, o.dtype)
                     for i, o in enumerate(outs)
                 ),
@@ -291,12 +306,12 @@
         copy.wait()
 
 
-ATTN_GAIN, ATTN_SHIFT, OUT_BIAS, MLP_GAIN, MLP_SHIFT, FC2_BIAS, FC1_BIAS = range(7)
+ATTN_GAIN, ATTN_SHIFT, OUT_BIAS, MLP_GAIN, MLP_SHIFT, FC2_BIAS, FC1_BIAS, FC1_BIAS_OTHER = range(8)
 
 
 def vectors_kernel(*refs):
     *items, text, image = refs
-    for out, own in ((text, items[: len(items) // 2]), (image, items[len(items) // 2 :])):
+    for out, own in ((text, items[:7]), (image, items[7:])):
         out[...] = jnp.zeros(out.shape, F32)
         for k, item in enumerate(own):
             out[k : k + 1, :] = item.get()[...].astype(F32).reshape(1, -1)
@@ -619,70 +634,73 @@
     repeat(blocks, block)
 
 
-def weight_product(left, right, full):
-    def block(i):
-        at = pl.ds(pl.multiple_of(i * 256, 256), 256)
-        full[at, :] = dot(left[:, lanes(i, 256)], right[...], TN)
-
-    repeat(left.shape[1] // 256, block)
-
-
 def row_sum(ref):
     return jnp.sum(ref[...].astype(F32), axis=0, keepdims=True)
 
 
 def fc_weight_kernel(orders, left0, left1, right0, right1, *rest):
-    *outs, sums, full, left, right = rest
-    half = left0.shape[0]
-    for at, a, b in ((slice(0, half), left0, right0), (slice(half, 2 * half), left1, right1)):
-        left[at, :] = a[...]
-        right[at, :] = b[...]
-    weight_product(left, right, full)
+    *outs, sums, full = rest
+
+    def block(i):
+        cols = lanes(i, 256)
+        full[pl.ds(pl.multiple_of(i * 256, 256), 256), :] = dot(
+            left0[:, cols], right0[...], TN
+        ) + dot(left1[:, cols], right1[...], TN)
+
+    repeat(left0.shape[1] // 256, block)
     emit(full, outs, orders)
-    sums[...] = row_sum(right)
+    sums[...] = row_sum(right0) + row_sum(right1)
 
 
 def attn_weights_kernel(orders, ctx, og0, og1, rows_own, rows_far, pg, *rest):
-    *outs, out_sum, qv_sum, full, rows, og = rest
+    *outs, out_sum, qv_sum, full = rest
     half = og0.shape[0]
     side = lax.axis_index("mp") // 2
     width = ctx.shape[1]
-    rows[chunk_start(side, half), :] = rows_own[...]
-    rows[chunk_start(1 - side, half), :] = rows_far[...]
-    og[:half, :] = og0[...]
-    og[half:, :] = og1[...]
+    own, far = chunk_start(side, half), chunk_start(1 - side, half)
 
     def part(i):
-        full[chunk_start(i, width), :] = dot(pg[i], rows[...], TN)
+        full[chunk_start(i, width), :] = dot(pg[i, own, :], rows_own[...], TN) + dot(
+            pg[i, far, :], rows_far[...], TN
+        )
 
     repeat(3, part)
-    full[3 * width :, :] = dot(ctx[...], og[...], TN)
+    full[3 * width :, :] = dot(ctx[:half, :], og0[...], TN) + dot(ctx[half:, :], og1[...], TN)
     emit(full, outs, orders)
-    out_sum[...] = row_sum(og)
+    out_sum[...] = row_sum(og0) + row_sum(og1)
     qv_sum[...] = jnp.concatenate(
         [jnp.sum(pg[part].astype(F32), axis=0, keepdims=True) for part in (0, 2)], axis=0
     )
 
 
-def gather_blocks_kernel(orders, low_half, high_half, out):
+def gather_blocks_kernel(orders, low_half, high_half, *rest):
+    *outs, held, sems = rest
     blocks = 2 ** len(orders[0])
     size = 2 * low_half.shape[0] // blocks
     here = lax.axis_index("dp")
-
-    def block(b):
+    copies, out, low = [], 0, 0
+    for b in range(blocks):
         place = place_of(here ^ b, orders)
         at = chunk_start(place % (blocks // 2), size)
         value = jnp.where(place < blocks // 2, low_half[at, :], high_half[at, :])
-        out[chunk_start(b, size), :] = value.astype(F32)
-
-    repeat(blocks, block)
-
-
-def gather_attn_kernel(orders, low_half, high_half, qkv, out_w, full):
-    gather_blocks_kernel(orders, low_half, high_half, full)
-    rows = qkv.shape[0]
-    qkv[...] = full[:rows, :]
-    out_w[...] = full[rows:, :]
+        held[b * size : (b + 1) * size, :] = value.astype(F32)
+        done = 0
+        while done < size:
+            count = min(size - done, outs[out].shape[0] - low)
+            start = b * size + done
+            copies.append(
+                pltpu.make_async_copy(
+                    held.at[start : start + count],
+                    outs[out].at[low : low + count],
+                    sems.at[len(copies)],
+                )
+            )
+            copies[-1].start()
+            done, low = done + count, low + count
+            if low == outs[out].shape[0]:
+                out, low = out + 1, 0
+    for copy in copies:
+        copy.wait()
 
 
 def input_grad_kernel(x, mine, theirs, after_grad0, after_grad1, vectors, grad, sums):
@@ -752,28 +770,35 @@
 
 def image_attn_kernel(first, x0, x1, vectors, *rest):
     if first:
-        source, result, rows, context, total, weights, sem = rest
+        source, own_out, other_out, rows, qkv, context, total, weights, sem = rest
     else:
-        before, source, keep, *sends, rows, context, total, weights, sem = rest
+        own_before, other_before, source, keep, *sends, rows, qkv, context, total, weights, sem = rest
     count, dim = x0.shape
     images = count // IMG_SEQ
     width = dim // 4
     copy = pltpu.make_async_copy(source.at[0 : 4 * width + 16], weights, sem)
     copy.start()
-    for k, x in enumerate((x0, x1)):
-        normed, _ = norm(x[...].astype(F32))
-        rows[k * count : (k + 1) * count, :] = (
+    rows[:count, :] = x0.get()[...]
+    rows[count:, :] = x1.get()[...]
+
+    def normalize(c):
+        at = chunk_start(c, count)
+        normed, _ = norm(rows[at, :].astype(F32))
+        rows[at, :] = (
             normed * vector(vectors, ATTN_GAIN) + vector(vectors, ATTN_SHIFT)
         ).astype(BF)
+
+    repeat(2, normalize)
     windows = image_windows(count, images)
     copy.wait()
     bias = weights[4 * width : 4 * width + 16, :].astype(F32)
+    bias_rows = (bias[0:1, :width], jnp.zeros((1, width), F32), bias[1:2, :width])
 
     def chunk(c):
         own = rows[chunk_start(c, count), :]
-        q = (dot(own, weights[:width, :], NT) + bias[0:1, :width]).astype(BF)
-        k = dot(own, weights[width : 2 * width, :], NT).astype(BF)
-        v = (dot(own, weights[2 * width : 3 * width, :], NT) + bias[1:2, :width]).astype(BF)
+        for part in range(3):
+            value = dot(own, weights[part * width : (part + 1) * width, :], NT)
+            qkv[part] = (value + bias_rows[part]).astype(BF)
         for q_low, q_high, k_low, k_high in windows:
             extent = (q_high - q_low, k_high - k_low)
             q_image = (lax.broadcasted_iota(jnp.int32, extent, 0) + q_low) // IMG_SEQ
@@ -781,7 +806,7 @@
             mask = jnp.where(q_image == k_image, 1.0, 0.0)
             place = pl.ds(pl.multiple_of(c * count + q_low, 16), q_high - q_low)
             context[place, :] = attend(
-                q[q_low:q_high], k[k_low:k_high], v[k_low:k_high], mask
+                qkv[0, q_low:q_high, :], qkv[1, k_low:k_high, :], qkv[2, k_low:k_high, :], mask
             )
 
     def columns(i):
@@ -791,11 +816,13 @@
     repeat(2, chunk)
     repeat(dim // 256, columns)
     if first:
-        result.held[...] = total[...]
-        result.start()
+        own_out.held[...] = total[:count, :]
+        own_out.start()
+        other_out.held[...] = total[count:, :].astype(BF)
+        other_out.start()
         return
-    keep[...] = total[:count, :] + before[:count, :]
-    put_pieces((total[count:, :] + before[count:, :]).astype(BF), sends)
+    keep[...] = total[:count, :] + own_before.get()[...]
+    put_pieces((total[count:, :] + other_before.get()[...].astype(F32)).astype(BF), sends)
 
 
 def image_norm_kernel(x, keep, vectors, *rest):
@@ -808,17 +835,16 @@
     rows[...] = (normed * vector(vectors, MLP_GAIN) + vector(vectors, MLP_SHIFT)).astype(BF)
 
 
-def image_mlp_kernel(rows0, rows2, vec0, vec1, w1a, w2a, w1b, w2b, mine, far, rows, active, total):
+def image_mlp_kernel(rows0, rows2, vectors, w1a, w2a, w1b, w2b, mine, far, rows, active, total):
     size, dim = rows0.shape
     rows[:size, :] = rows0[...]
     rows[size:, :] = rows2[...]
-    total[...] = jnp.zeros(total.shape, F32)
-    for vectors, w1, w2 in ((vec0, w1a, w2a), (vec1, w1b, w2b)):
+    for bias, w1, w2 in ((FC1_BIAS, w1a, w2a), (FC1_BIAS_OTHER, w1b, w2b)):
         w1 = w1.get()
 
         def units(i):
             cols = lanes(i, 256)
-            hidden = dot(rows[...], w1[:, cols]) + vectors[FC1_BIAS : FC1_BIAS + 1, cols]
+            hidden = dot(rows[...], w1[:, cols]) + vectors[bias : bias + 1, cols]
             active[:, cols] = gelu_parts(hidden)[0].astype(BF)
 
         repeat(w1.shape[1] // 256, units)
@@ -826,7 +852,8 @@
 
         def columns(i):
             cols = lanes(i, 256)
-            total[:, cols] += dot(active[...], w2[:, cols])
+            value = dot(active[...], w2[:, cols])
+            total[:, cols] = value if bias == FC1_BIAS else total[:, cols] + value
 
         repeat(dim // 256, columns)
     mine[...] = total[:size, :].astype(BF)
@@ -917,7 +944,7 @@
             for v in (
                 attn_gain, attn_shift, out_bias, mlp_gain, mlp_shift, fc2_bias, fc1_bias,
                 img_attn_gain, img_attn_shift, img_out_bias, img_mlp_gain, img_mlp_shift,
-                img_fc2_bias, img_fc1_bias,
+                img_fc2_bias, img_fc1_bias, core_swap(img_fc1_bias),
             )
         ],
     )
@@ -972,12 +999,12 @@
         scratch=project_scratch,
     )
 
-    thirds, halves = pieces_of(size, 3), pieces_of(size, 2)
+    row_cuts, sum_cuts, *og_cuts = [pieces_of(size, n) for n in PIECES[:4]]
 
     def after_attn(half, mine, theirs):
         stream, rows, *sends = run(
             functools.partial(after_attn_kernel, half),
-            [Early(size, dim, dtype=F32), chunk] + [shape(n, dim) for n in thirds],
+            [Early(size, dim, dtype=F32), chunk] + [shape(n, dim) for n in row_cuts],
             [x_mine, mine, theirs, vectors],
         )
         return stream, (rows, *map(core_swap, sends))
@@ -988,17 +1015,17 @@
             [Early(2 * size, dim)] * 3
             + [Early(size, dim)] * 2
             + [chunk]
-            + [shape(n, dim) for n in halves],
+            + [shape(n, dim) for n in sum_cuts],
             [*rows, grad, fc1_weight, vectors, fc2_weight],
         )
         partial = (mg_keep, *map(core_swap, mg_sends))
         return all_rows, act, hid_grad, (br_keep, core_swap(br_send)), partial
 
-    def mlp_back(stream, mine, theirs, grad):
+    def mlp_back(half, stream, mine, theirs, grad):
         value, low, sums, *sends = run(
             mlp_back_kernel,
             [Early(size, dim, dtype=F32), chunk, shape(2, dim, dtype=F32)]
-            + [shape(n, dim) for n in thirds],
+            + [shape(n, dim) for n in og_cuts[half]],
             [stream, mine, theirs, grad, vectors],
         )
         return value, (low, *map(core_swap, sends)), sums
@@ -1013,9 +1040,9 @@
     image_chunk = shape(image_rows, dim)
     img_other = core_swap(images)
     img_w1_other, img_w2_other = core_swap(img_fc1_weight), core_swap(img_fc2_weight)
-    img_vectors_other = core_swap(img_vectors)
     image_scratch = [
         pltpu.VMEM((2 * image_rows, dim), BF),
+        pltpu.VMEM((3, image_rows, width), BF),
         pltpu.VMEM((2 * image_rows, width), BF),
         pltpu.VMEM((2 * image_rows, dim), F32),
         pltpu.VMEM((used, dim), BF),
@@ -1023,17 +1050,17 @@
     ]
     image_total = run(
         functools.partial(image_attn_kernel, True),
-        [Early(2 * image_rows, dim, dtype=F32)],
-        [images, img_other, img_vectors, Fixed(bundle)],
+        [Early(image_rows, dim, dtype=F32), Early(image_rows, dim)],
+        [Late(images), Late(img_other), img_vectors, Fixed(bundle)],
         scratch=image_scratch,
-        after=[Fixed(img_w1_other), img_vectors_other],
-    )
-    tg0, tg1 = run(
-        arrange_kernel, [Early(2 * size, dim)] * 2, [t0, t1, packed, core_swap(packed)]
+        after=[Fixed(img_w1_other)],
     )
     mine1 = run(add_kernel, [chunk], [keep1, other1], after=[theirs0])
     theirs1 = side_swap(mine1)
     stream0, rows0 = after_attn(0, mine0, theirs0)
+    tg0, tg1 = run(
+        arrange_kernel, [Early(2 * size, dim)] * 2, [t0, t1, packed, core_swap(packed)]
+    )
     all_rows0, act0, hg0, branch0, partial0 = mlp(rows0, tg0)
     mg0 = run(add_pieces_kernel, [chunk], partial0, after=[theirs1, Fixed(img_w2_other)])
     mg_theirs0 = side_swap(mg0)
@@ -1042,15 +1069,18 @@
 
     bits = [2**k for k in range(n_dp.bit_length() - 1)]
     along_x = tuple(bits)
-    mixed, even = (along_x, tuple(bits[1:] + bits[:1])), (along_x, along_x)
+    kinds = {
+        "even": (along_x, along_x),
+        "mixed": (along_x, tuple(bits[1:] + bits[:1])),
+        "turned": (along_x, tuple(bits[1:2] + bits[:1] + bits[2:])),
+    }
     plain = 2 ** len(bits) != n_dp or dim % (16 * n_dp) != 0
-    if plain:
-        mixed = even = None
+    fc2_order, fc1_order, qkv_order = [None if plain else kinds[name] for name in ORDERS]
     grad_shapes = [shape(dim, dim, dtype=F32)] if plain else [shape(dim // 2, dim)] * 2
 
     class Sum:
-        def __init__(self, parts, orders, last, sizes):
-            self.orders, self.last, self.sizes, self.step = orders, last, sizes, 0
+        def __init__(self, parts, orders, sizes):
+            self.orders, self.sizes, self.step = orders, sizes, 0
             if plain:
                 total = lax.psum(parts[0], "dp")
                 cuts = [sum(sizes[: i + 1]) for i in range(len(sizes) - 1)]
@@ -1082,133 +1112,194 @@
                 self.exchange(self.keep, 2 * levels - 1 - self.step)
             else:
                 got = run(
-                    functools.partial(self.last, self.orders),
-                    [shape(n, dim, dtype=F32) for n in self.sizes],
+                    functools.partial(gather_blocks_kernel, self.orders),
+                    [Pinned(n, dim, dtype=F32) for n in self.sizes],
                     [self.keep, self.arriving],
-                    scratch=[pltpu.VMEM((dim, dim), F32)] if len(self.sizes) > 1 else [],
+                    scratch=[
+                        pltpu.VMEM((dim, dim), F32),
+                        pltpu.SemaphoreType.DMA((n_dp + len(self.sizes),)),
+                    ],
                 )
                 self.result = got if len(self.sizes) > 1 else [got]
-
-    def advance(*totals):
-        for total in totals:
-            total.advance()
 
     def fc_weight(orders, args):
         *parts, sums = run(
             functools.partial(fc_weight_kernel, orders),
             grad_shapes + [shape(1, dim, dtype=F32)],
             args,
-            scratch=[pltpu.VMEM((dim, dim), F32)] + [pltpu.VMEM((tokens, dim), BF)] * 2,
-        )
-        return Sum(parts, orders, gather_blocks_kernel, (dim,)), sums
-
-    fc2_sum, fc2_bias_sum = fc_weight(mixed, [act0, act1, tg0, tg1])
-    mg1 = run(add_pieces_kernel, [chunk], partial1, after=[mg_theirs0])
-    mg_theirs1 = side_swap(mg1)
-    after_grad0, og0, mlp_sums0 = mlp_back(stream0, mg0, mg_theirs0, tg0)
-    fc1_sum, fc1_bias_sum = fc_weight(even, [all_rows0, all_rows1, hg0, hg1])
-    fc2_sum.advance()
-
-    og_first, cg_first, pg_first = run(
-        functools.partial(attn_back_first_kernel, blocks_first, len(og0) - 1),
-        [pair, shape(2 * size, width), shape(3, rows_first * length, width)],
-        [*og0, qkv, mask, out_weight],
-    )
-    after_grad1, og1, mlp_sums1 = mlp_back(stream1, mg1, mg_theirs1, tg1)
-    og_second, pg, p0, p1, p2, p3 = run(
-        functools.partial(attn_back_second_kernel, blocks_rest, len(og1) - 1),
-        [pair, shape(3, tokens, width)] + [chunk] * 4,
-        [*og1, cg_first, pg_first, qkv, mask, out_weight, w_t],
-        scratch=[pltpu.VMEM((tokens, width), BF)],
-    )
-    p_other1, p_other3 = core_swap(p1), core_swap(p3)
-    fc2_sum.advance()
-    fc1_sum.advance()
-    *parts, out_sum, qv_sum = run(
-        functools.partial(attn_weights_kernel, mixed),
-        grad_shapes + [shape(1, dim, dtype=F32), shape(2, width, dtype=F32)],
-        [ctx, og_first, og_second, rows_own, rows_far, pg],
-        scratch=[pltpu.VMEM((dim, dim), F32)] + [pltpu.VMEM((tokens, dim), BF)] * 2,
-    )
-    attn_sum = Sum(parts, mixed, gather_attn_kernel, (3 * width, width))
-
-    img_keep, *img_sends = run(
-        functools.partial(image_attn_kernel, False),
-        [shape(image_rows, dim, dtype=F32)] + [shape(n, dim) for n in pieces_of(image_rows, 3)],
-        [images, img_other, img_vectors, image_total, Fixed(far_bundle)],
-        scratch=image_scratch,
-        vmem=20,
-    )
-    img_after, img_rows0 = run(
-        image_norm_kernel,
-        [Early(image_rows, dim, dtype=F32), image_chunk],
-        [images, img_keep, img_vectors, *map(core_swap, img_sends)],
-    )
-    img_rows2 = side_swap(img_rows0)
-    p_mine, to_side = run(add_pair_kernel, [chunk] * 2, [p0, p_other1, p2, p_other3])
-    p_theirs = side_swap(to_side)
-    advance(fc2_sum, fc1_sum, attn_sum)
-    br0, br1 = run(branch_sums_kernel, [Early(size, dim)] * 2, [*branch0, *branch1])
-    far_branch = run(far_branch_kernel, [chunk], [br0, br1])
-    br_theirs = side_swap(far_branch)
-    advance(fc2_sum, fc1_sum, attn_sum)
-    text_in_grad, attn_sums = run(
-        input_grad_kernel,
-        [chunk, shape(2, dim, dtype=F32)],
-        [text_in, p_mine, p_theirs, after_grad0, after_grad1, vectors],
-    )
-    small = run(norm_sums_kernel, [shape(4, dim, dtype=F32)], [mlp_sums0, mlp_sums1, attn_sums])
-    small_near = core_swap(small)
-    i_mine, i_side = run(
-        image_mlp_kernel,
-        [image_chunk] * 2,
-        [
-            img_rows0, img_rows2, img_vectors, img_vectors_other,
-            Late(img_fc1_weight), Late(img_fc2_weight), Late(img_w1_other), Late(img_w2_other),
-        ],
-        scratch=[pltpu.VMEM((2 * image_rows, dim), BF)] * 2
-        + [pltpu.VMEM((2 * image_rows, dim), F32)],
-        vmem=24,
-    )
-    i_theirs = side_swap(i_side)
-    small = run(add_rows_kernel, [shape(4, dim, dtype=F32)], [small, small_near])
-    small_far = side_swap(small)
-    advance(fc1_sum, attn_sum, fc2_sum)
-    text_out = run(
-        text_out_kernel,
-        [chunk],
-        [br0, br1, br_theirs, stream0, stream1, vectors],
-    )
-    small = run(
-        small_kernel,
-        [shape(8, dim, dtype=F32)],
-        [small, small_far, fc2_bias_sum, fc1_bias_sum, out_sum, qv_sum],
-    )
-    if plain:
-        small_far = lax.psum(small, "dp")
-        small = jnp.zeros_like(small)
-    else:
-        small_far = dp_swap(small, (bits[0], bits[0]))
-    advance(attn_sum, fc1_sum, fc2_sum)
-    image_out = run(
-        image_out_kernel, [image_chunk], [img_after, i_mine, i_theirs, img_vectors]
-    )
-    if not plain:
-        for bit in bits[1:]:
-            small = run(add_rows_kernel, [shape(8, dim, dtype=F32)], [small, small_far])
-            small_far = dp_swap(small, (bit, bit))
-            advance(attn_sum, fc1_sum)
-    small = run(add_rows_kernel, [shape(8, dim, dtype=F32)], [small, small_far])
-    for total in (fc2_sum, fc1_sum, attn_sum):
-        while not plain and total.step < 2 * len(bits):
-            total.advance()
-    (grad_fc2_weight,) = fc2_sum.result
-    (grad_fc1_weight,) = fc1_sum.result
-    grad_qkv, grad_out_weight = attn_sum.result
+            scratch=[pltpu.VMEM((dim, dim), F32)],
+        )
+        return Sum(parts, orders, (dim,)), sums
+
+    got = {}
+
+    def fc2_weight():
+        got["fc2"], got["fc2_bias"] = fc_weight(fc2_order, [act0, act1, tg0, tg1])
+
+    def fc1_weight():
+        got["fc1"], got["fc1_bias"] = fc_weight(fc1_order, [all_rows0, all_rows1, hg0, hg1])
+
+    def mlp_sum():
+        got["mg1"] = run(add_pieces_kernel, [chunk], partial1, after=[mg_theirs0])
+        got["mg_theirs1"] = side_swap(got["mg1"])
+
+    def mlp_back0():
+        got["grad0"], got["og0"], got["sums0"] = mlp_back(0, stream0, mg0, mg_theirs0, tg0)
+
+    def mlp_back1():
+        got["grad1"], got["og1"], got["sums1"] = mlp_back(
+            1, stream1, got["mg1"], got["mg_theirs1"], tg1
+        )
+
+    def attn_back0():
+        og = got["og0"]
+        got["first"] = run(
+            functools.partial(attn_back_first_kernel, blocks_first, len(og) - 1),
+            [pair, shape(2 * size, width), shape(3, rows_first * length, width)],
+            [*og, qkv, mask, out_weight],
+        )
+
+    def attn_back1():
+        og = got["og1"]
+        got["og_second"], got["pg"], p0, p1, p2, p3 = run(
+            functools.partial(attn_back_second_kernel, blocks_rest, len(og) - 1),
+            [pair, shape(3, tokens, width)] + [chunk] * 4,
+            [*og, *got["first"][1:], qkv, mask, out_weight, w_t],
+            scratch=[pltpu.VMEM((tokens, width), BF)],
+        )
+        got["parts"] = [p0, core_swap(p1), p2, core_swap(p3)]
+
+    def attn_weights():
+        *parts, got["out_bias"], got["qv_bias"] = run(
+            functools.partial(attn_weights_kernel, qkv_order),
+            grad_shapes + [shape(1, dim, dtype=F32), shape(2, width, dtype=F32)],
+            [ctx, got["first"][0], got["og_second"], rows_own, rows_far, got["pg"]],
+            scratch=[pltpu.VMEM((dim, dim), F32)],
+        )
+        got["qkv"] = Sum(parts, qkv_order, (3 * width, width))
+
+    image_cuts = pieces_of(image_rows, PIECES[4])
+
+    def p_sums():
+        got["p"], to_side = run(add_pair_kernel, [chunk] * 2, got["parts"])
+        got["p_far"] = side_swap(to_side)
+
+    def image_attn():
+        got["img"], *sends = run(
+            functools.partial(image_attn_kernel, False),
+            [shape(image_rows, dim, dtype=F32)] + [shape(n, dim) for n in image_cuts],
+            [
+                Late(images), Late(img_other), img_vectors, *map(Late, image_total),
+                Fixed(far_bundle),
+            ],
+            scratch=image_scratch,
+            vmem=20,
+        )
+        got["img_others"] = [core_swap(part) for part in sends]
+
+    def image_norm():
+        got["img_after"], got["rows0"] = run(
+            image_norm_kernel,
+            [Early(image_rows, dim, dtype=F32), image_chunk],
+            [images, got["img"], img_vectors, *got["img_others"]],
+        )
+        got["rows2"] = side_swap(got["rows0"])
+
+    def image_mlp():
+        got["img_mine"], far = run(
+            image_mlp_kernel,
+            [image_chunk] * 2,
+            [
+                got["rows0"], got["rows2"], img_vectors,
+                Late(img_fc1_weight), Late(img_fc2_weight),
+                Late(img_w1_other), Late(img_w2_other),
+            ],
+            scratch=[pltpu.VMEM((2 * image_rows, dim), BF)] * 2
+            + [pltpu.VMEM((2 * image_rows, dim), F32)],
+            vmem=24,
+        )
+        got["img_far"] = side_swap(far)
+
+    def image_out():
+        got["image_out"] = run(
+            image_out_kernel,
+            [image_chunk],
+            [got["img_after"], got["img_mine"], got["img_far"], img_vectors],
+        )
+
+    def input_grad():
+        got["input"], attn_sums = run(
+            input_grad_kernel,
+            [chunk, shape(2, dim, dtype=F32)],
+            [text_in, got["p"], got["p_far"], got["grad0"], got["grad1"], vectors],
+        )
+        got["small"] = run(
+            norm_sums_kernel, [shape(4, dim, dtype=F32)], [got["sums0"], got["sums1"], attn_sums]
+        )
+        got["small_far"] = core_swap(got["small"])
+
+    def branch():
+        br0, br1 = run(branch_sums_kernel, [Early(size, dim)] * 2, [*branch0, *branch1])
+        far = run(far_branch_kernel, [chunk], [br0, br1])
+        got["branch"] = (br0, br1, side_swap(far))
+
+    def text_out():
+        got["text_out"] = run(
+            text_out_kernel, [chunk], [*got["branch"], stream0, stream1, vectors]
+        )
+
+    def small_near():
+        got["small"] = run(
+            add_rows_kernel, [shape(4, dim, dtype=F32)], [got["small"], got["small_far"]]
+        )
+        got["small_far"] = side_swap(got["small"])
+
+    later = [] if plain else list(bits)
+
+    def small_next():
+        if later:
+            bit = later.pop(0)
+            got["small_far"] = dp_swap(got["small"], (bit, bit))
+
+    def small_side():
+        got["small"] = run(
+            small_kernel,
+            [shape(8, dim, dtype=F32)],
+            [
+                got["small"], got["small_far"],
+                got["fc2_bias"], got["fc1_bias"], got["out_bias"], got["qv_bias"],
+            ],
+        )
+        small_next()
+
+    def small_dp():
+        if not plain:
+            got["small"] = run(
+                add_rows_kernel, [shape(8, dim, dtype=F32)], [got["small"], got["small_far"]]
+            )
+            small_next()
+
+    steps = dict(
+        fc2_weight=fc2_weight, fc1_weight=fc1_weight, mlp_sum=mlp_sum,
+        mlp_back0=mlp_back0, mlp_back1=mlp_back1, attn_back0=attn_back0, attn_back1=attn_back1,
+        attn_weights=attn_weights,
+        p_sums=p_sums, image_attn=image_attn, image_norm=image_norm, image_mlp=image_mlp,
+        image_out=image_out, input=input_grad, branch=branch, text_out=text_out,
+        small_near=small_near, small_side=small_side, small_dp=small_dp,
+        fc1=lambda: got["fc1"].advance(),
+        fc2=lambda: got["fc2"].advance(),
+        qkv=lambda: got["qkv"].advance(),
+    )
+    for name in PLAN:
+        steps[name]()
+    small = lax.psum(got["small"], "dp") if plain else got["small"]
+    (grad_fc2_weight,) = got["fc2"].result
+    (grad_fc1_weight,) = got["fc1"].result
+    grad_qkv, grad_out_weight = got["qkv"].result
     return (
-        text_out,
-        image_out,
-        text_in_grad,
+        got["text_out"],
+        got["image_out"],
+        got["input"],
         small[2],
         small[3],
         grad_qkv.reshape(3, width, dim).transpose(2, 0, 1),

time: 226 us -> 211 us (0.934)
  waiting for transfers between devices: 66.9 us -> 47.4 us
  starting transfers between devices: 47 us -> 52.9 us
    ppermute x11, waiting for transfers between devices: 23.1 us -> 13.1 us  [side_swap(): lax.ppermute(x, 'mp', [(i, i ^ 2) for i in range(lax.axis_size('mp'))])]
    ppermute x21, waiting for transfers between devices: 35.7 us -> 25.8 us  [dp_swap(): return lax.ppermute(x, ('dp', 'mp'), pairs)]
    ppermute x34 -> x33, starting transfers between devices: 9.24 us -> 15.5 us  [core_swap(): lax.ppermute(x, 'mp', [(i, i ^ 1) for i in range(lax.axis_size('mp'))])]
    ppermute x11, starting transfers between devices: 14.8 us -> 12.1 us  [side_swap(): lax.ppermute(x, 'mp', [(i, i ^ 2) for i in range(lax.axis_size('mp'))])]
    ppermute x21, starting transfers between devices: 22.9 us -> 25.2 us  [dp_swap(): return lax.ppermute(x, ('dp', 'mp'), pairs)]
    ppermute x34 -> x33, waiting for transfers between devices: 7.99 us -> 8.56 us  [core_swap(): lax.ppermute(x, 'mp', [(i, i ^ 1) for i in range(lax.axis_size('mp'))])]
    unnamed x150 -> x118, local copies, waits for them, and re-layouts: 11.9 us -> 11.8 us
  transfers between devices with their start and end apart: 67 -> 66, of which waited for: 19 -> 18; matrix products, arithmetic and copies ran while one was open for 0% -> 0% of each run, Pallas kernels for 37% -> 39%
where the time goes in v2:
time: 211 us; the launch traced here: 210 us
  Pallas kernels  81.9 us (39%)
  starting transfers between devices  52.9 us (25%)
  waiting for transfers between devices  47.4 us (22%)
  between operations  15.1 us (7%)
  local copies, waits for them, and re-layouts  12.5 us (6%)
    pallas_call x58, Pallas kernels, __call__(): pl.pallas_call(run, out_shape=(*(pltpu.HBM(o.shape, o.dtype) if isinstanc...  81.9 us
    ppermute x21, waiting for transfers between devices, dp_swap(): return lax.ppermute(x, ('dp', 'mp'), pairs)  25.8 us
    ppermute x21, starting transfers between devices, dp_swap(): return lax.ppermute(x, ('dp', 'mp'), pairs)  25.2 us
    ppermute x33, starting transfers between devices, core_swap(): lax.ppermute(x, 'mp', [(i, i ^ 1) for i in range(lax.axis_size('mp'))])  15.5 us
    ppermute x11, waiting for transfers between devices, side_swap(): lax.ppermute(x, 'mp', [(i, i ^ 2) for i in range(lax.axis_size('mp'))])  13.1 us
    ppermute x11, starting transfers between devices, side_swap(): lax.ppermute(x, 'mp', [(i, i ^ 2) for i in range(lax.axis_size('mp'))])  12.1 us
    unnamed x118, local copies, waits for them, and re-layouts  11.8 us
    ppermute x33, waiting for transfers between devices, core_swap(): lax.ppermute(x, 'mp', [(i, i ^ 1) for i in range(lax.axis_size('mp'))])  8.56 us
  transfers between devices with their start and end apart: 66, of which 18 were waited for; matrix products, arithmetic and copies ran while one was open for 0% of the time, Pallas kernels for 39%

profile of v2, /device:TPU:0, one launch (start us, length us, event | category | flops | bytes accessed | tf_op | source)
XLA Modules:
  0.0 210.4 jit_solution(1795282249949246710)
XLA Ops:
  7.8 2.6 %collective-permute-start = (bf16[272,768]{1,0:T(8,128)(2,1)}, bf16[272,768]{1,0:T(8,128)(2,1)S(1)}, u32[]{:S(2)}, u32[]{:S(2)}) collective-permute-start(bf16[272,768]{1,0:T(8,128)(2,1)} %refs_0_.19), channel_id=1, source_target_pairs={{0,2},{1,3},{2,0},{3,1},{4,6},{5,7},{6,4},{7,5},{8,10},{9,11},{10,... | collective-permute-start | bytes 1253384 | tf_op jit(solution)/shard_map/ppermute | solution.py:873
  10.9 2.5 %collective-permute-done.2.refs_14_ = bf16[768]{0:T(1024)(128)(2,1)S(1)} collective-permute-done((bf16[768]{0:T(1024)(128)(2,1)}, bf16[768]{0:T(1024)(128)(2,1)S(1)}, u32[]{:S(2)}, u32[]{:S(2)}) %collective-permute-start.2) | collective-permute-done | bytes 1568 | tf_op jit(solution)/shard_map/ppermute | solution.py:869
  24.1 5.2 %shard_map.394 = (bf16[544,768]{1,0:T(8,128)(2,1)}, bf16[3,1088,192]{2,1,0:T(8,128)(2,1)}, bf16[1088,192]{1,0:T(8,128)(2,1)}, bf16[2,272,768]{2,1,0:T(8,128)(2,1...) custom-call(bf16[272,768]{1,0:T(8,128)(2,1)S(1)} %copy-done.12, ...), custom_call_target="tpu_custom_call" | custom-call | flops 1 | bytes 1 | tf_op jit(solution)/shard_map/pallas_call | solution.py:129
  30.6 7.5 %collective-permute-done.5.refs_2_.refs_0_ = bf16[384,768]{1,0:T(8,128)(2,1)S(1)} collective-permute-done((bf16[384,768]{1,0:T(8,128)(2,1)S(1)}, bf16[384,768]{1,0:T(8,128)(2,1)S(1)}, u32[]{:S(2)}, u32[]{:S(2)}) %collective-permute-start.5) | collective-permute-done | bytes 589856 | tf_op jit(solution)/shard_map/ppermute | solution.py:873
  40.9 7.2 %shard_map.397 = (f32[400,768]{1,0:T(8,128)}, bf16[400,768]{1,0:T(8,128)(2,1)}, f32[8,128]{1,0:T(8,128)S(1)}) custom-call(bf16[400,768]{1,0:T(8,128)(2,1)} %refs_0_.18, bf16[400,768]{1,0:T(8,128)(2,1)} %collective-permute-done.8.refs_1_, f32[8,768]{1,0:T(8,128)S(1)} %get-tuple-element.220.refs_2_.refs_3_, bf16[896,768]{1,0:T(8,128)(2,1)} %copy-done.8, ...), custom_call_target="tpu_custom_call" | custom-call | flops 1 | bytes 1 | tf_op jit(solution)/shard_map/pallas_call | solution.py:129
  48.2 3.9 %collective-permute-done.6.refs_2_ = bf16[272,768]{1,0:T(8,128)(2,1)S(1)} collective-permute-done((bf16[272,768]{1,0:T(8,128)(2,1)}, bf16[272,768]{1,0:T(8,128)(2,1)S(1)}, u32[]{:S(2)}, u32[]{:S(2)}) %collective-permute-start.6) | collective-permute-done | bytes 417824 | tf_op jit(solution)/shard_map/ppermute | solution.py:873
  57.4 5.1 %shard_map.401 = (bf16[544,768]{1,0:T(8,128)(2,1)}, bf16[544,768]{1,0:T(8,128)(2,1)}, bf16[544,768]{1,0:T(8,128)(2,1)}, bf16[272,768]{1,0:T(8,128)(2,1)}, bf16[2...) custom-call(bf16[272,768]{1,0:T(8,128)(2,1)S(1)} %get-tuple-element., ...), custom_call_target="tpu_custom_call" | custom-call | flops 1 | bytes 1 | tf_op jit(solution)/shard_map/pallas_call | solution.py:129
  68.1 5.1 %shard_map.404 = (bf16[544,768]{1,0:T(8,128)(2,1)}, bf16[544,768]{1,0:T(8,128)(2,1)}, bf16[544,768]{1,0:T(8,128)(2,1)}, bf16[272,768]{1,0:T(8,128)(2,1)}, bf16[2...) custom-call(bf16[272,768]{1,0:T(8,128)(2,1)S(1)} %get-tuple-element., ...), custom_call_target="tpu_custom_call" | custom-call | flops 1 | bytes 1 | tf_op jit(solution)/shard_map/pallas_call | solution.py:129
  74.4 3.2 %shard_map.405 = (bf16[384,768]{1,0:T(8,128)(2,1)S(1)}, bf16[384,768]{1,0:T(8,128)(2,1)S(1)}, f32[1,768]{1,0:T(1,128)S(1)}, f32[8,128]{1,0:T(8,128)S(1)}) custom-call(bf16[544,768]{1,0:T(8,128)(2,1)S(1)} %copy-done.32, bf16[544,768]{1,0:T(8,128)(2,1)S(1)} %copy-done.35, bf16[544,768]{1,0:T(8,128)(2,1)S(1)} %copy-done.4, bf16[544,768]{1,0:T(8,128)(2,1)S(1)} %copy-done.2, ...), custom_call_target="tpu_custom_call" | custom-call | flops 1 | bytes 1 | tf_op jit(solution)/shard_map/pallas_call | solution.py:129
  83.9 3.1 %shard_map.408 = (bf16[384,768]{1,0:T(8,128)(2,1)S(1)}, bf16[384,768]{1,0:T(8,128)(2,1)S(1)}, f32[1,768]{1,0:T(1,128)S(1)}, f32[8,128]{1,0:T(8,128)S(1)}) custom-call(bf16[544,768]{1,0:T(8,128)(2,1)S(1)} %copy-done.30, bf16[544,768]{1,0:T(8,128)(2,1)S(1)} %copy-done.33, bf16[544,768]{1,0:T(8,128)(2,1)S(1)} %copy-done.31, bf16[544,768]{1,0:T(8,128)(2,1)S(1)} %copy-done.34, ...), custom_call_target="tpu_custom_call" | custom-call | flops 1 | bytes 1 | tf_op jit(solution)/shard_map/pallas_call | solution.py:129
  90.6 3.5 %shard_map.410 = (bf16[544,768]{1,0:T(8,128)(2,1)S(1)}, bf16[544,192]{1,0:T(8,128)(2,1)S(1)}, bf16[3,512,192]{2,1,0:T(8,128)(2,1)S(1)}, f32[8,128]{1,0:T(8,128)S(1)}) custom-call(bf16[272,768]{1,0:T(8,128)(2,1)S(1)} %get-tuple-element.261.refs_0_, bf16[96,768]{1,0:T(8,128)(2,1)S(1)} %collective-permute-done.28.refs_1_, ...), custom_call_target="tpu_custom_call" | custom-call | flops 1 | bytes 1 | tf_op jit(solution)/shard_map/pallas_call | solution.py:129
  98.9 5.0 %shard_map.412 = (bf16[544,768]{1,0:T(8,128)(2,1)S(1)}, bf16[3,1088,192]{2,1,0:T(8,128)(2,1)S(1)}, bf16[272,768]{1,0:T(8,128)(2,1)S(1)}, bf16[272,768]{1,0:T(8,1...) custom-call(bf16[272,768]{1,0:T(8,128)(2,1)S(1)} %get-tuple-element.277.refs_0_, ...), custom_call_target="tpu_custom_call" | custom-call | flops 1 | bytes 1 | tf_op jit(solution)/shard_map/pallas_call | solution.py:129
  105.4 4.0 %shard_map.415 = (bf16[384,768]{1,0:T(8,128)(2,1)S(1)}, bf16[384,768]{1,0:T(8,128)(2,1)}, f32[1,768]{1,0:T(1,128)S(1)}, f32[2,192]{1,0:T(2,128)S(1)}, f32[8,128]{1,0:T(8,128)S(1)}) custom-call(bf16[1088,192]{1,0:T(8,128)(2,1)S(1)} %copy-done.36, bf16[544,768]{1,0:T(8,128)(2,1)S(1)} %get-tuple-element.289.refs_1_, ...), custom_call_target="tpu_custom_call" | custom-call | flops 1 | bytes 1 | tf_op jit(solution)/shard_map/pallas_call | solution.py:129
  114.5 6.5 %shard_map.417 = (f32[400,768]{1,0:T(8,128)S(1)}, bf16[208,768]{1,0:T(8,128)(2,1)S(1)}, bf16[192,768]{1,0:T(8,128)(2,1)S(1)}, f32[8,128]{1,0:T(8,128)S(1)}) custom-call(bf16[400,768]{1,0:T(8,128)(2,1)} %refs_0_.18, bf16[400,768]{1,0:T(8,128)(2,1)} %collective-permute-done.8.refs_1_, f32[8,768]{1,0:T(8,128)S(1)} %get-tuple-element.220.refs_2_.refs_3_, ...), custom_call_target="tpu_custom_call" | custom-call | flops 1 | bytes 1 | tf_op jit(solution)/shard_map/pallas_call | solution.py:129
  123.7 3.4 %collective-permute-start.44 = (bf16[96,768]{1,0:T(8,128)(2,1)S(1)}, bf16[96,768]{1,0:T(8,128)(2,1)S(1)}, u32[]{:S(2)}, u32[]{:S(2)}) collective-permute-start(bf16[96,768]{1,0:T(8,128)(2,1)S(1)} %get-tuple-element.322), channel_id=1, source_target_pairs={{0,16},{1,17},{2,18},{3,19},{4,20},{5,21},{6,22},{7,23},{8,24},{9,... | collective-permute-start | bytes 442376 | tf_op jit(solution)/shard_map/ppermute | solution.py:881
  128.4 2.2 %collective-permute-done.44.refs_1_ = bf16[96,768]{1,0:T(8,128)(2,1)S(1)} collective-permute-done((bf16[96,768]{1,0:T(8,128)(2,1)S(1)}, bf16[96,768]{1,0:T(8,128)(2,1)S(1)}, u32[]{:S(2)}, u32[]{:S(2)}) %collective-permute-start.44) | collective-permute-done | bytes 147488 | tf_op jit(solution)/shard_map/ppermute | solution.py:881
  130.6 5.2 %collective-permute-start.15 = (bf16[272,768]{1,0:T(8,128)(2,1)S(1)}, bf16[272,768]{1,0:T(8,128)(2,1)S(1)}, u32[]{:S(2)}, u32[]{:S(2)}) collective-permute-start(bf16[272,768]{1,0:T(8,128)(2,1)S(1)} %copy-done.57), channel_id=1, source_target_pairs={{0,1},{1,0},{2,3},{3,2},{4,5},{5,4},{6,7},{7,6},{8,9},{9,8},{10,11... | collective-permute-start | bytes 1253384 | tf_op jit(solution)/shard_map/ppermute | solution.py:869
  137.2 7.6 %collective-permute-done.45.refs_1_ = bf16[96,768]{1,0:T(8,128)(2,1)S(1)} collective-permute-done((bf16[96,768]{1,0:T(8,128)(2,1)S(1)}, bf16[96,768]{1,0:T(8,128)(2,1)S(1)}, u32[]{:S(2)}, u32[]{:S(2)}) %collective-permute-start.45) | collective-permute-done | bytes 147488 | tf_op jit(solution)/shard_map/ppermute | solution.py:881
  146.0 2.5 %collective-permute-start.53 = (bf16[96,768]{1,0:T(8,128)(2,1)S(1)}, bf16[96,768]{1,0:T(8,128)(2,1)S(1)}, u32[]{:S(2)}, u32[]{:S(2)}) collective-permute-start(bf16[96,768]{1,0:T(8,128)(2,1)S(1)} %get-tuple-element.344), channel_id=1, source_target_pairs={{0,16},{1,5},{2,18},{3,7},{4,20},{5,1},{6,22},{7,3},{8,24},{9,13},... | collective-permute-start | bytes 442376 | tf_op jit(solution)/shard_map/ppermute | solution.py:881
  159.9 2.0 collective-permute-start.55
  162.0 8.0 %shard_map.432 = (bf16[400,768]{1,0:T(8,128)(2,1)S(1)}, bf16[400,768]{1,0:T(8,128)(2,1)S(1)}, f32[8,128]{1,0:T(8,128)S(1)}) custom-call(bf16[400,768]{1,0:T(8,128)(2,1)S(1)} %get-tuple-element.340.refs_0_, bf16[400,768]{1,0:T(8,128)(2,1)S(1)} %collective-permute-done.50.refs_1_, f32[8,768]{1,0:T(8,128)S(1)} %get-tuple-element.220.refs_2_.refs_3_, ...), custom_call_target="tpu_custom_call" | custom-call | flops 1 | bytes 1 | tf_op jit(solution)/shard_map/pallas_call | solution.py:129
  177.5 4.3 %collective-permute-done.60.refs_1_ = bf16[192,768]{1,0:T(8,128)(2,1)S(1)} collective-permute-done((bf16[192,768]{1,0:T(8,128)(2,1)S(1)}, bf16[192,768]{1,0:T(8,128)(2,1)S(1)}, u32[]{:S(2)}, u32[]{:S(2)}) %collective-permute-start.60) | collective-permute-done | bytes 294944 | tf_op jit(solution)/shard_map/ppermute | solution.py:881
  187.3 6.0 %collective-permute-done.63.refs_1_ = bf16[384,768]{1,0:T(8,128)(2,1)S(1)} collective-permute-done((bf16[384,768]{1,0:T(8,128)(2,1)S(1)}, bf16[384,768]{1,0:T(8,128)(2,1)S(1)}, u32[]{:S(2)}, u32[]{:S(2)}) %collective-permute-start.63) | collective-permute-done | bytes 589856 | tf_op jit(solution)/shard_map/ppermute | solution.py:881
  194.9 2.9 %collective-permute-start.64 = (f32[8,768]{1,0:T(8,128)S(1)}, f32[8,768]{1,0:T(8,128)S(1)}, u32[]{:S(2)}, u32[]{:S(2)}) collective-permute-start(f32[8,768]{1,0:T(8,128)S(1)} %get-tuple-element.380.refs_0_), channel_id=1, source_target_pairs={{0,16},{1,17},{2,18},{3,19},{4,20},{5,21},{6,22},{7,23},{8,24},{9,... | collective-permute-start | bytes 73736 | tf_op jit(solution)/shard_map/ppermute | solution.py:881
  (288 shorter events, 86.7 us)
Async XLA Ops:
  7.2 107.3 %all-gather.2.cloned.1.call-start = ((), (), s32[]{:S(2)}) async-start(), calls=%async_computation | async-start | bytes 1548288 | tf_op jit(solution)/shard_map/all_gather | solution.py:1037
  7.8 13.5 %collective-permute-start = (bf16[272,768]{1,0:T(8,128)(2,1)}, bf16[272,768]{1,0:T(8,128)(2,1)S(1)}, u32[]{:S(2)}, u32[]{:S(2)}) collective-permute-start(bf16[272,768]{1,0:T(8,128)(2,1)} %refs_0_.19), channel_id=1, source_target_pairs={{0,2},{1,3},{2,0},{3,1},{4,6},{5,7},{6,4},{7,5},{8,10},{9,11},{10,... | collective-permute-start | bytes 1253384 | tf_op jit(solution)/shard_map/ppermute | solution.py:873
  10.4 30.5 %collective-permute-start.9 = (bf16[768,768]{1,0:T(8,128)(2,1)}, bf16[768,768]{1,0:T(8,128)(2,1)}, u32[]{:S(2)}, u32[]{:S(2)}) collective-permute-start(bf16[768,768]{1,0:T(8,128)(2,1)} %refs_3_.3), channel_id=1, source_target_pairs={{0,1},{1,0},{2,3},{3,2},{4,5},{5,4},{6,7},{7,6},{8,9},{9,8},{10,11... | collective-permute-start | bytes 3538952 | tf_op jit(solution)/shard_map/ppermute | solution.py:869
  22.5 15.5 %collective-permute-start.5 = (bf16[384,768]{1,0:T(8,128)(2,1)S(1)}, bf16[384,768]{1,0:T(8,128)(2,1)S(1)}, u32[]{:S(2)}, u32[]{:S(2)}) collective-permute-start(bf16[384,768]{1,0:T(8,128)(2,1)S(1)} %get-tuple-element.215), channel_id=1, source_target_pairs={{0,2},{1,3},{2,0},{3,1},{4,6},{5,7},{6,4},{7,5},{8,10},{9,11},{10,... | collective-permute-start | bytes 1769480 | tf_op jit(solution)/shard_map/ppermute | solution.py:873
  23.1 17.2 %collective-permute-start.8 = (bf16[400,768]{1,0:T(8,128)(2,1)S(1)}, bf16[400,768]{1,0:T(8,128)(2,1)}, u32[]{:S(2)}, u32[]{:S(2)}) collective-permute-start(bf16[400,768]{1,0:T(8,128)(2,1)S(1)} %copy-done.6), channel_id=1, source_target_pairs={{0,1},{1,0},{2,3},{3,2},{4,5},{5,4},{6,7},{7,6},{8,9},{9,8},{10,11... | collective-permute-start | bytes 1843208 | tf_op jit(solution)/shard_map/ppermute | solution.py:869
  30.3 32.8 %collective-permute-start.19 = (bf16[768,768]{1,0:T(8,128)(2,1)}, bf16[768,768]{1,0:T(8,128)(2,1)}, u32[]{:S(2)}, u32[]{:S(2)}) collective-permute-start(bf16[768,768]{1,0:T(8,128)(2,1)} %refs_4_.5), channel_id=1, source_target_pairs={{0,1},{1,0},{2,3},{3,2},{4,5},{5,4},{6,7},{7,6},{8,9},{9,8},{10,11... | collective-permute-start | bytes 3538952 | tf_op jit(solution)/shard_map/ppermute | solution.py:869
  39.6 15.1 %collective-permute-start.14 = (bf16[384,768]{1,0:T(8,128)(2,1)S(1)}, bf16[384,768]{1,0:T(8,128)(2,1)S(1)}, u32[]{:S(2)}, u32[]{:S(2)}) collective-permute-start(bf16[384,768]{1,0:T(8,128)(2,1)S(1)} %collective-permute-done.5.refs_2_.refs_0_), channel_id=1, source_target_pairs={{0,1},{1,0},{2,3},{3,2},{4,5},{5,4},{6,7},{7,6},{8,9},{9,8},{10,11... | collective-permute-start | bytes 1769480 | tf_op jit(solution)/shard_map/ppermute | solution.py:869
  40.9 13.4 %collective-permute-start.13 = (bf16[272,768]{1,0:T(8,128)(2,1)S(1)}, bf16[272,768]{1,0:T(8,128)(2,1)S(1)}, u32[]{:S(2)}, u32[]{:S(2)}) collective-permute-start(bf16[272,768]{1,0:T(8,128)(2,1)S(1)} %copy-done.23), channel_id=1, source_target_pairs={{0,1},{1,0},{2,3},{3,2},{4,5},{5,4},{6,7},{7,6},{8,9},{9,8},{10,11... | collective-permute-start | bytes 1253384 | tf_op jit(solution)/shard_map/ppermute | solution.py:869
  66.7 14.2 %collective-permute-start.24 = (bf16[272,768]{1,0:T(8,128)(2,1)S(1)}, bf16[272,768]{1,0:T(8,128)(2,1)S(1)}, u32[]{:S(2)}, u32[]{:S(2)}) collective-permute-start(bf16[272,768]{1,0:T(8,128)(2,1)S(1)} %get-tuple-element.249.refs_1_), channel_id=1, source_target_pairs={{0,2},{1,3},{2,0},{3,1},{4,6},{5,7},{6,4},{7,5},{8,10},{9,11},{10,... | collective-permute-start | bytes 1253384 | tf_op jit(solution)/shard_map/ppermute | solution.py:873
  87.0 17.5 %collective-permute-start.37 = (bf16[384,768]{1,0:T(8,128)(2,1)S(1)}, bf16[384,768]{1,0:T(8,128)(2,1)S(1)}, u32[]{:S(2)}, u32[]{:S(2)}) collective-permute-start(bf16[384,768]{1,0:T(8,128)(2,1)S(1)} %get-tuple-element.295), channel_id=1, source_target_pairs={{0,4},{1,5},{2,6},{3,7},{4,0},{5,1},{6,2},{7,3},{8,12},{9,13},{10,... | collective-permute-start | bytes 1769480 | tf_op jit(solution)/shard_map/ppermute | solution.py:881
  89.7 14.8 %collective-permute-start.38 = (bf16[192,768]{1,0:T(8,128)(2,1)S(1)}, bf16[192,768]{1,0:T(8,128)(2,1)S(1)}, u32[]{:S(2)}, u32[]{:S(2)}) collective-permute-start(bf16[192,768]{1,0:T(8,128)(2,1)S(1)} %get-tuple-element.297), channel_id=1, source_target_pairs={{0,8},{1,17},{2,10},{3,19},{4,12},{5,21},{6,14},{7,23},{8,0},{9,25... | collective-permute-start | bytes 884744 | tf_op jit(solution)/shard_map/ppermute | solution.py:881
  109.4 17.7 %collective-permute-start.40 = (bf16[384,768]{1,0:T(8,128)(2,1)}, bf16[384,768]{1,0:T(8,128)(2,1)S(1)}, u32[]{:S(2)}, u32[]{:S(2)}) collective-permute-start(bf16[384,768]{1,0:T(8,128)(2,1)} %get-tuple-element.307), channel_id=1, source_target_pairs={{0,4},{1,9},{2,6},{3,11},{4,0},{5,13},{6,2},{7,15},{8,12},{9,1},{1... | collective-permute-start | bytes 1769480 | tf_op jit(solution)/shard_map/ppermute | solution.py:881
  121.1 14.7 %collective-permute-start.47 = (bf16[192,768]{1,0:T(8,128)(2,1)S(1)}, bf16[192,768]{1,0:T(8,128)(2,1)S(1)}, u32[]{:S(2)}, u32[]{:S(2)}) collective-permute-start(bf16[192,768]{1,0:T(8,128)(2,1)S(1)} %get-tuple-element.326), channel_id=1, source_target_pairs={{0,1},{1,0},{2,3},{3,2},{4,5},{5,4},{6,7},{7,6},{8,9},{9,8},{10,11... | collective-permute-start | bytes 884744 | tf_op jit(solution)/shard_map/ppermute | solution.py:869
  121.1 14.7 %collective-permute-start.46 = (bf16[208,768]{1,0:T(8,128)(2,1)S(1)}, bf16[208,768]{1,0:T(8,128)(2,1)S(1)}, u32[]{:S(2)}, u32[]{:S(2)}) collective-permute-start(bf16[208,768]{1,0:T(8,128)(2,1)S(1)} %get-tuple-element.325), channel_id=1, source_target_pairs={{0,1},{1,0},{2,3},{3,2},{4,5},{5,4},{6,7},{7,6},{8,9},{9,8},{10,11... | collective-permute-start | bytes 958472 | tf_op jit(solution)/shard_map/ppermute | solution.py:869
  127.3 18.5 %collective-permute-start.43 = (bf16[192,768]{1,0:T(8,128)(2,1)S(1)}, bf16[192,768]{1,0:T(8,128)(2,1)S(1)}, u32[]{:S(2)}, u32[]{:S(2)}) collective-permute-start(bf16[192,768]{1,0:T(8,128)(2,1)S(1)} %get-tuple-element.320), channel_id=1, source_target_pairs={{0,8},{1,17},{2,10},{3,19},{4,12},{5,21},{6,14},{7,23},{8,0},{9,25... | collective-permute-start | bytes 884744 | tf_op jit(solution)/shard_map/ppermute | solution.py:881
  127.4 18.7 %collective-permute-start.39 = (bf16[272,768]{1,0:T(8,128)(2,1)S(1)}, bf16[272,768]{1,0:T(8,128)(2,1)S(1)}, u32[]{:S(2)}, u32[]{:S(2)}) collective-permute-start(bf16[272,768]{1,0:T(8,128)(2,1)S(1)} %copy-done.54), channel_id=1, source_target_pairs={{0,2},{1,3},{2,0},{3,1},{4,6},{5,7},{6,4},{7,5},{8,10},{9,11},{10,... | collective-permute-start | bytes 1253384 | tf_op jit(solution)/shard_map/ppermute | solution.py:873
  130.6 19.5 %collective-permute-start.15 = (bf16[272,768]{1,0:T(8,128)(2,1)S(1)}, bf16[272,768]{1,0:T(8,128)(2,1)S(1)}, u32[]{:S(2)}, u32[]{:S(2)}) collective-permute-start(bf16[272,768]{1,0:T(8,128)(2,1)S(1)} %copy-done.57), channel_id=1, source_target_pairs={{0,1},{1,0},{2,3},{3,2},{4,5},{5,4},{6,7},{7,6},{8,9},{9,8},{10,11... | collective-permute-start | bytes 1253384 | tf_op jit(solution)/shard_map/ppermute | solution.py:869
  135.8 14.4 %collective-permute-start.23 = (bf16[272,768]{1,0:T(8,128)(2,1)S(1)}, bf16[272,768]{1,0:T(8,128)(2,1)S(1)}, u32[]{:S(2)}, u32[]{:S(2)}) collective-permute-start(bf16[272,768]{1,0:T(8,128)(2,1)S(1)} %copy-done.58), channel_id=1, source_target_pairs={{0,1},{1,0},{2,3},{3,2},{4,5},{5,4},{6,7},{7,6},{8,9},{9,8},{10,11... | collective-permute-start | bytes 1253384 | tf_op jit(solution)/shard_map/ppermute | solution.py:869
  144.8 17.2 %collective-permute-start.50 = (bf16[400,768]{1,0:T(8,128)(2,1)S(1)}, bf16[400,768]{1,0:T(8,128)(2,1)S(1)}, u32[]{:S(2)}, u32[]{:S(2)}) collective-permute-start(bf16[400,768]{1,0:T(8,128)(2,1)S(1)} %get-tuple-element.340.refs_0_), channel_id=1, source_target_pairs={{0,2},{1,3},{2,0},{3,1},{4,6},{5,7},{6,4},{7,5},{8,10},{9,11},{10,... | collective-permute-start | bytes 1843208 | tf_op jit(solution)/shard_map/ppermute | solution.py:873
  153.3 18.2 %collective-permute-start.48 = (bf16[272,768]{1,0:T(8,128)(2,1)S(1)}, bf16[272,768]{1,0:T(8,128)(2,1)S(1)}, u32[]{:S(2)}, u32[]{:S(2)}) collective-permute-start(bf16[272,768]{1,0:T(8,128)(2,1)S(1)} %get-tuple-element.338), channel_id=1, source_target_pairs={{0,2},{1,3},{2,0},{3,1},{4,6},{5,7},{6,4},{7,5},{8,10},{9,11},{10,... | collective-permute-start | bytes 1253384 | tf_op jit(solution)/shard_map/ppermute | solution.py:873
  157.3 26.1 %collective-permute-start.59 = (bf16[384,768]{1,0:T(8,128)(2,1)S(1)}, bf16[384,768]{1,0:T(8,128)(2,1)S(1)}, u32[]{:S(2)}, u32[]{:S(2)}) collective-permute-start(bf16[384,768]{1,0:T(8,128)(2,1)S(1)} %get-tuple-element.365.refs_0_), channel_id=1, source_target_pairs={{0,4},{1,9},{2,6},{3,11},{4,0},{5,13},{6,2},{7,15},{8,12},{9,1},{1... | collective-permute-start | bytes 1769480 | tf_op jit(solution)/shard_map/ppermute | solution.py:881
  159.9 14.3 %collective-permute-start.55 = (bf16[96,768]{1,0:T(8,128)(2,1)S(1)}, bf16[96,768]{1,0:T(8,128)(2,1)S(1)}, u32[]{:S(2)}, u32[]{:S(2)}) collective-permute-start(bf16[96,768]{1,0:T(8,128)(2,1)S(1)} %get-tuple-element.355.refs_0_), channel_id=1, source_target_pairs={{0,16},{1,5},{2,18},{3,7},{4,20},{5,1},{6,22},{7,3},{8,24},{9,13},... | collective-permute-start | bytes 442376 | tf_op jit(solution)/shard_map/ppermute | solution.py:881
  182.4 18.8 %collective-permute-start.54 = (bf16[400,768]{1,0:T(8,128)(2,1)S(1)}, bf16[400,768]{1,0:T(8,128)(2,1)S(1)}, u32[]{:S(2)}, u32[]{:S(2)}) collective-permute-start(bf16[400,768]{1,0:T(8,128)(2,1)S(1)} %get-tuple-element.354), channel_id=1, source_target_pairs={{0,2},{1,3},{2,0},{3,1},{4,6},{5,7},{6,4},{7,5},{8,10},{9,11},{10,... | collective-permute-start | bytes 1843208 | tf_op jit(solution)/shard_map/ppermute | solution.py:873
  185.0 14.6 %collective-permute-start.61 = (bf16[384,768]{1,0:T(8,128)(2,1)S(1)}, bf16[384,768]{1,0:T(8,128)(2,1)S(1)}, u32[]{:S(2)}, u32[]{:S(2)}) collective-permute-start(bf16[384,768]{1,0:T(8,128)(2,1)S(1)} %get-tuple-element.371.refs_0_), channel_id=1, source_target_pairs={{0,4},{1,9},{2,6},{3,11},{4,0},{5,13},{6,2},{7,15},{8,12},{9,1},{1... | collective-permute-start | bytes 1769480 | tf_op jit(solution)/shard_map/ppermute | solution.py:881
  (101 other events, 569.2 us)
Sparse Core Ops, SparseCore 0:
  39.8 42.8 all-gather.1

commit v3 on v2

--- a/solution.py
+++ b/solution.py
@@ -19,13 +19,13 @@
 
 PLAN = (
     "fc2_weight", "mlp_sum", "mlp_back0", "fc1_weight", "fc2", "attn_back0", "mlp_back1",
-    "attn_back1", "fc2", "fc1", "attn_weights",
-    "p_sums", "image_attn", "fc2", "fc1", "qkv", "image_norm", "fc2", "fc1", "qkv", "input",
-    "branch", "qkv", "fc2", "small_near", "image_mlp", "fc1", "text_out", "small_side", "qkv",
-    "fc1", "fc2", "small_dp", "qkv", "fc1", "small_dp", "qkv", "image_out", "small_dp",
+    "attn_back1", "fc2", "fc1", "attn_weights", "p_sums", "image_attn", "fc1", "fc2", "qkv",
+    "image_norm", "fc2", "fc1", "qkv", "branch", "input", "qkv", "fc2", "small_near", "image_mlp",
+    "fc1", "text_out", "small_side", "qkv", "fc1", "fc2", "small_dp", "qkv", "fc1", "small_dp",
+    "image_out", "qkv", "small_dp",
 )
 
-ORDERS = ("mixed", "even", "mixed")
+ORDERS = ("mixed", "even", "turned")
 PIECES = (3, 2, 3, 3, 2)
 
 NN = (((1,), (0,)), ((), ()))

time: 211 us -> 208 us (0.986)
  starting transfers between devices: 52.9 us -> 46.2 us
  waiting for transfers between devices: 47.4 us -> 51.2 us
    ppermute x21, starting transfers between devices: 25.2 us -> 21.9 us  [dp_swap(): return lax.ppermute(x, ('dp', 'mp'), pairs)]
    ppermute x33, starting transfers between devices: 15.5 us -> 12.1 us  [core_swap(): lax.ppermute(x, 'mp', [(i, i ^ 1) for i in range(lax.axis_size('mp'))])]
    ppermute x21, waiting for transfers between devices: 25.8 us -> 28.6 us  [dp_swap(): return lax.ppermute(x, ('dp', 'mp'), pairs)]
    unnamed x118 -> x122, local copies, waits for them, and re-layouts: 11.8 us -> 12 us
  transfers between devices with their start and end apart: 66 -> 66, of which waited for: 18 -> 19; matrix products, arithmetic and copies ran while one was open for 0% -> 0% of each run, Pallas kernels for 39% -> 39%
where the time goes in v3:
time: 208 us
  Pallas kernels  81.9 us (39%)
  waiting for transfers between devices  51.2 us (25%)
  starting transfers between devices  46.2 us (22%)
  between operations  15.1 us (7%)
  local copies, waits for them, and re-layouts  12.6 us (6%)
    pallas_call x58, Pallas kernels, __call__(): pl.pallas_call(run, out_shape=(*(pltpu.HBM(o.shape, o.dtype) if isinstanc...  81.9 us
    ppermute x21, waiting for transfers between devices, dp_swap(): return lax.ppermute(x, ('dp', 'mp'), pairs)  28.6 us
    ppermute x21, starting transfers between devices, dp_swap(): return lax.ppermute(x, ('dp', 'mp'), pairs)  21.9 us
    ppermute x11, waiting for transfers between devices, side_swap(): lax.ppermute(x, 'mp', [(i, i ^ 2) for i in range(lax.axis_size('mp'))])  14 us
    ppermute x33, starting transfers between devices, core_swap(): lax.ppermute(x, 'mp', [(i, i ^ 1) for i in range(lax.axis_size('mp'))])  12.1 us
    ppermute x11, starting transfers between devices, side_swap(): lax.ppermute(x, 'mp', [(i, i ^ 2) for i in range(lax.axis_size('mp'))])  12.1 us
    unnamed x122, local copies, waits for them, and re-layouts  12 us
    ppermute x33, waiting for transfers between devices, core_swap(): lax.ppermute(x, 'mp', [(i, i ^ 1) for i in range(lax.axis_size('mp'))])  8.56 us
  transfers between devices with their start and end apart: 66, of which 19 were waited for; matrix products, arithmetic and copies ran while one was open for 0% of the time, Pallas kernels for 39%

profile of v3, /device:TPU:0, one launch (start us, length us, event | category | flops | bytes accessed | tf_op | source)
XLA Modules:
  0.0 207.7 jit_solution(8075649780839223744)
XLA Ops:
  7.8 2.6 %collective-permute-start = (bf16[272,768]{1,0:T(8,128)(2,1)}, bf16[272,768]{1,0:T(8,128)(2,1)S(1)}, u32[]{:S(2)}, u32[]{:S(2)}) collective-permute-start(bf16[272,768]{1,0:T(8,128)(2,1)} %refs_0_.19), channel_id=1, source_target_pairs={{0,2},{1,3},{2,0},{3,1},{4,6},{5,7},{6,4},{7,5},{8,10},{9,11},{10,... | collective-permute-start | bytes 1253384 | tf_op jit(solution)/shard_map/ppermute | solution.py:873
  10.9 2.5 %collective-permute-done.2.refs_14_ = bf16[768]{0:T(1024)(128)(2,1)S(1)} collective-permute-done((bf16[768]{0:T(1024)(128)(2,1)}, bf16[768]{0:T(1024)(128)(2,1)S(1)}, u32[]{:S(2)}, u32[]{:S(2)}) %collective-permute-start.2) | collective-permute-done | bytes 1568 | tf_op jit(solution)/shard_map/ppermute | solution.py:869
  24.1 5.2 %shard_map.394 = (bf16[544,768]{1,0:T(8,128)(2,1)}, bf16[3,1088,192]{2,1,0:T(8,128)(2,1)}, bf16[1088,192]{1,0:T(8,128)(2,1)}, bf16[2,272,768]{2,1,0:T(8,128)(2,1...) custom-call(bf16[272,768]{1,0:T(8,128)(2,1)S(1)} %copy-done.12, ...), custom_call_target="tpu_custom_call" | custom-call | flops 1 | bytes 1 | tf_op jit(solution)/shard_map/pallas_call | solution.py:129
  30.6 7.5 %collective-permute-done.5.refs_2_.refs_0_ = bf16[384,768]{1,0:T(8,128)(2,1)S(1)} collective-permute-done((bf16[384,768]{1,0:T(8,128)(2,1)S(1)}, bf16[384,768]{1,0:T(8,128)(2,1)S(1)}, u32[]{:S(2)}, u32[]{:S(2)}) %collective-permute-start.5) | collective-permute-done | bytes 589856 | tf_op jit(solution)/shard_map/ppermute | solution.py:873
  40.9 7.2 %shard_map.397 = (f32[400,768]{1,0:T(8,128)}, bf16[400,768]{1,0:T(8,128)(2,1)}, f32[8,128]{1,0:T(8,128)S(1)}) custom-call(bf16[400,768]{1,0:T(8,128)(2,1)} %refs_0_.18, bf16[400,768]{1,0:T(8,128)(2,1)} %collective-permute-done.8.refs_1_, f32[8,768]{1,0:T(8,128)S(1)} %get-tuple-element.220.refs_2_.refs_3_, bf16[896,768]{1,0:T(8,128)(2,1)} %copy-done.8, ...), custom_call_target="tpu_custom_call" | custom-call | flops 1 | bytes 1 | tf_op jit(solution)/shard_map/pallas_call | solution.py:129
  48.2 3.9 %collective-permute-done.6.refs_2_ = bf16[272,768]{1,0:T(8,128)(2,1)S(1)} collective-permute-done((bf16[272,768]{1,0:T(8,128)(2,1)}, bf16[272,768]{1,0:T(8,128)(2,1)S(1)}, u32[]{:S(2)}, u32[]{:S(2)}) %collective-permute-start.6) | collective-permute-done | bytes 417824 | tf_op jit(solution)/shard_map/ppermute | solution.py:873
  57.4 5.1 %shard_map.401 = (bf16[544,768]{1,0:T(8,128)(2,1)}, bf16[544,768]{1,0:T(8,128)(2,1)}, bf16[544,768]{1,0:T(8,128)(2,1)}, bf16[272,768]{1,0:T(8,128)(2,1)}, bf16[2...) custom-call(bf16[272,768]{1,0:T(8,128)(2,1)S(1)} %get-tuple-element., ...), custom_call_target="tpu_custom_call" | custom-call | flops 1 | bytes 1 | tf_op jit(solution)/shard_map/pallas_call | solution.py:129
  68.1 5.1 %shard_map.404 = (bf16[544,768]{1,0:T(8,128)(2,1)}, bf16[544,768]{1,0:T(8,128)(2,1)}, bf16[544,768]{1,0:T(8,128)(2,1)}, bf16[272,768]{1,0:T(8,128)(2,1)}, bf16[2...) custom-call(bf16[272,768]{1,0:T(8,128)(2,1)S(1)} %get-tuple-element., ...), custom_call_target="tpu_custom_call" | custom-call | flops 1 | bytes 1 | tf_op jit(solution)/shard_map/pallas_call | solution.py:129
  74.4 3.2 %shard_map.405 = (bf16[384,768]{1,0:T(8,128)(2,1)S(1)}, bf16[384,768]{1,0:T(8,128)(2,1)S(1)}, f32[1,768]{1,0:T(1,128)S(1)}, f32[8,128]{1,0:T(8,128)S(1)}) custom-call(bf16[544,768]{1,0:T(8,128)(2,1)S(1)} %copy-done.32, bf16[544,768]{1,0:T(8,128)(2,1)S(1)} %copy-done.35, bf16[544,768]{1,0:T(8,128)(2,1)S(1)} %copy-done.4, bf16[544,768]{1,0:T(8,128)(2,1)S(1)} %copy-done.2, ...), custom_call_target="tpu_custom_call" | custom-call | flops 1 | bytes 1 | tf_op jit(solution)/shard_map/pallas_call | solution.py:129
  83.9 3.1 %shard_map.408 = (bf16[384,768]{1,0:T(8,128)(2,1)S(1)}, bf16[384,768]{1,0:T(8,128)(2,1)S(1)}, f32[1,768]{1,0:T(1,128)S(1)}, f32[8,128]{1,0:T(8,128)S(1)}) custom-call(bf16[544,768]{1,0:T(8,128)(2,1)S(1)} %copy-done.30, bf16[544,768]{1,0:T(8,128)(2,1)S(1)} %copy-done.33, bf16[544,768]{1,0:T(8,128)(2,1)S(1)} %copy-done.31, bf16[544,768]{1,0:T(8,128)(2,1)S(1)} %copy-done.34, ...), custom_call_target="tpu_custom_call" | custom-call | flops 1 | bytes 1 | tf_op jit(solution)/shard_map/pallas_call | solution.py:129
  90.6 3.5 %shard_map.410 = (bf16[544,768]{1,0:T(8,128)(2,1)S(1)}, bf16[544,192]{1,0:T(8,128)(2,1)S(1)}, bf16[3,512,192]{2,1,0:T(8,128)(2,1)S(1)}, f32[8,128]{1,0:T(8,128)S(1)}) custom-call(bf16[272,768]{1,0:T(8,128)(2,1)S(1)} %get-tuple-element.259.refs_0_, bf16[96,768]{1,0:T(8,128)(2,1)S(1)} %collective-permute-done.27.refs_1_, ...), custom_call_target="tpu_custom_call" | custom-call | flops 1 | bytes 1 | tf_op jit(solution)/shard_map/pallas_call | solution.py:129
  99.0 5.0 %shard_map.412 = (bf16[544,768]{1,0:T(8,128)(2,1)S(1)}, bf16[3,1088,192]{2,1,0:T(8,128)(2,1)S(1)}, bf16[272,768]{1,0:T(8,128)(2,1)S(1)}, bf16[272,768]{1,0:T(8,1...) custom-call(bf16[272,768]{1,0:T(8,128)(2,1)S(1)} %get-tuple-element.277.refs_0_, ...), custom_call_target="tpu_custom_call" | custom-call | flops 1 | bytes 1 | tf_op jit(solution)/shard_map/pallas_call | solution.py:129
  105.5 4.0 %shard_map.415 = (bf16[384,768]{1,0:T(8,128)(2,1)S(1)}, bf16[384,768]{1,0:T(8,128)(2,1)}, f32[1,768]{1,0:T(1,128)S(1)}, f32[2,192]{1,0:T(2,128)S(1)}, f32[8,128]{1,0:T(8,128)S(1)}) custom-call(bf16[1088,192]{1,0:T(8,128)(2,1)S(1)} %copy-done.36, bf16[544,768]{1,0:T(8,128)(2,1)S(1)} %get-tuple-element.273.refs_1_, ...), custom_call_target="tpu_custom_call" | custom-call | flops 1 | bytes 1 | tf_op jit(solution)/shard_map/pallas_call | solution.py:129
  113.6 6.5 %shard_map.417 = (f32[400,768]{1,0:T(8,128)S(1)}, bf16[208,768]{1,0:T(8,128)(2,1)S(1)}, bf16[192,768]{1,0:T(8,128)(2,1)S(1)}, f32[8,128]{1,0:T(8,128)S(1)}) custom-call(bf16[400,768]{1,0:T(8,128)(2,1)} %refs_0_.18, bf16[400,768]{1,0:T(8,128)(2,1)} %collective-permute-done.8.refs_1_, f32[8,768]{1,0:T(8,128)S(1)} %get-tuple-element.220.refs_2_.refs_3_, ...), custom_call_target="tpu_custom_call" | custom-call | flops 1 | bytes 1 | tf_op jit(solution)/shard_map/pallas_call | solution.py:129
  124.7 5.2 %collective-permute-done.38.refs_1_ = bf16[96,768]{1,0:T(8,128)(2,1)S(1)} collective-permute-done((bf16[96,768]{1,0:T(8,128)(2,1)S(1)}, bf16[96,768]{1,0:T(8,128)(2,1)S(1)}, u32[]{:S(2)}, u32[]{:S(2)}) %collective-permute-start.38) | collective-permute-done | bytes 147488 | tf_op jit(solution)/shard_map/ppermute | solution.py:881
  130.3 4.2 %collective-permute-done.43.refs_1_ = bf16[96,768]{1,0:T(8,128)(2,1)S(1)} collective-permute-done((bf16[96,768]{1,0:T(8,128)(2,1)S(1)}, bf16[96,768]{1,0:T(8,128)(2,1)S(1)}, u32[]{:S(2)}, u32[]{:S(2)}) %collective-permute-start.43) | collective-permute-done | bytes 147488 | tf_op jit(solution)/shard_map/ppermute | solution.py:881
  137.2 4.2 %collective-permute-done.44.refs_1_ = bf16[96,768]{1,0:T(8,128)(2,1)S(1)} collective-permute-done((bf16[96,768]{1,0:T(8,128)(2,1)S(1)}, bf16[96,768]{1,0:T(8,128)(2,1)S(1)}, u32[]{:S(2)}, u32[]{:S(2)}) %collective-permute-start.44) | collective-permute-done | bytes 147488 | tf_op jit(solution)/shard_map/ppermute | solution.py:881
  142.6 2.6 %collective-permute-start.53 = (bf16[96,768]{1,0:T(8,128)(2,1)S(1)}, bf16[96,768]{1,0:T(8,128)(2,1)S(1)}, u32[]{:S(2)}, u32[]{:S(2)}) collective-permute-start(bf16[96,768]{1,0:T(8,128)(2,1)S(1)} %get-tuple-element.344), channel_id=1, source_target_pairs={{0,16},{1,17},{2,18},{3,19},{4,20},{5,21},{6,22},{7,23},{8,24},{9,... | collective-permute-start | bytes 442376 | tf_op jit(solution)/shard_map/ppermute | solution.py:881
  150.9 2.3 %collective-permute-done.53.refs_1_ = bf16[96,768]{1,0:T(8,128)(2,1)S(1)} collective-permute-done((bf16[96,768]{1,0:T(8,128)(2,1)S(1)}, bf16[96,768]{1,0:T(8,128)(2,1)S(1)}, u32[]{:S(2)}, u32[]{:S(2)}) %collective-permute-start.53) | collective-permute-done | bytes 147488 | tf_op jit(solution)/shard_map/ppermute | solution.py:881
  154.6 3.1 %collective-permute-start.51 = (f32[4,768]{1,0:T(4,128)S(1)}, f32[4,768]{1,0:T(4,128)S(1)}, u32[]{:S(2)}, u32[]{:S(2)}) collective-permute-start(f32[4,768]{1,0:T(4,128)S(1)} %get-tuple-element.341.refs_0_), channel_id=1, source_target_pairs={{0,1},{1,0},{2,3},{3,2},{4,5},{5,4},{6,7},{7,6},{8,9},{9,8},{10,11... | collective-permute-start | bytes 36872 | tf_op jit(solution)/shard_map/ppermute | solution.py:869
  160.3 8.0 %shard_map.432 = (bf16[400,768]{1,0:T(8,128)(2,1)S(1)}, bf16[400,768]{1,0:T(8,128)(2,1)S(1)}, f32[8,128]{1,0:T(8,128)S(1)}) custom-call(bf16[400,768]{1,0:T(8,128)(2,1)S(1)} %get-tuple-element.331.refs_0_, bf16[400,768]{1,0:T(8,128)(2,1)S(1)} %collective-permute-done.49.refs_1_, f32[8,768]{1,0:T(8,128)S(1)} %get-tuple-element.220.refs_2_.refs_3_, ...), custom_call_target="tpu_custom_call" | custom-call | flops 1 | bytes 1 | tf_op jit(solution)/shard_map/pallas_call | solution.py:129
  168.3 2.8 %collective-permute-start.58 = (bf16[192,768]{1,0:T(8,128)(2,1)S(1)}, bf16[192,768]{1,0:T(8,128)(2,1)S(1)}, u32[]{:S(2)}, u32[]{:S(2)}) collective-permute-start(bf16[192,768]{1,0:T(8,128)(2,1)S(1)} %get-tuple-element.363.refs_0_), channel_id=1, source_target_pairs={{0,8},{1,9},{2,10},{3,11},{4,12},{5,13},{6,14},{7,15},{8,0},{9,1},... | collective-permute-start | bytes 884744 | tf_op jit(solution)/shard_map/ppermute | solution.py:881
  183.1 8.6 %collective-permute-done.61.refs_1_ = bf16[384,768]{1,0:T(8,128)(2,1)S(1)} collective-permute-done((bf16[384,768]{1,0:T(8,128)(2,1)S(1)}, bf16[384,768]{1,0:T(8,128)(2,1)S(1)}, u32[]{:S(2)}, u32[]{:S(2)}) %collective-permute-start.61) | collective-permute-done | bytes 589856 | tf_op jit(solution)/shard_map/ppermute | solution.py:881
  195.8 2.3 %collective-permute-done.64.refs_1_ = bf16[384,768]{1,0:T(8,128)(2,1)S(1)} collective-permute-done((bf16[384,768]{1,0:T(8,128)(2,1)S(1)}, bf16[384,768]{1,0:T(8,128)(2,1)S(1)}, u32[]{:S(2)}, u32[]{:S(2)}) %collective-permute-start.64) | collective-permute-done | bytes 589856 | tf_op jit(solution)/shard_map/ppermute | solution.py:881
  (292 shorter events, 85.0 us)
Async XLA Ops:
  7.2 106.3 %all-gather.2.cloned.1.call-start = ((), (), s32[]{:S(2)}) async-start(), calls=%async_computation | async-start | bytes 1548288 | tf_op jit(solution)/shard_map/all_gather | solution.py:1037
  7.8 13.5 %collective-permute-start = (bf16[272,768]{1,0:T(8,128)(2,1)}, bf16[272,768]{1,0:T(8,128)(2,1)S(1)}, u32[]{:S(2)}, u32[]{:S(2)}) collective-permute-start(bf16[272,768]{1,0:T(8,128)(2,1)} %refs_0_.19), channel_id=1, source_target_pairs={{0,2},{1,3},{2,0},{3,1},{4,6},{5,7},{6,4},{7,5},{8,10},{9,11},{10,... | collective-permute-start | bytes 1253384 | tf_op jit(solution)/shard_map/ppermute | solution.py:873
  10.4 30.5 %collective-permute-start.9 = (bf16[768,768]{1,0:T(8,128)(2,1)}, bf16[768,768]{1,0:T(8,128)(2,1)}, u32[]{:S(2)}, u32[]{:S(2)}) collective-permute-start(bf16[768,768]{1,0:T(8,128)(2,1)} %refs_3_.3), channel_id=1, source_target_pairs={{0,1},{1,0},{2,3},{3,2},{4,5},{5,4},{6,7},{7,6},{8,9},{9,8},{10,11... | collective-permute-start | bytes 3538952 | tf_op jit(solution)/shard_map/ppermute | solution.py:869
  22.5 15.5 %collective-permute-start.5 = (bf16[384,768]{1,0:T(8,128)(2,1)S(1)}, bf16[384,768]{1,0:T(8,128)(2,1)S(1)}, u32[]{:S(2)}, u32[]{:S(2)}) collective-permute-start(bf16[384,768]{1,0:T(8,128)(2,1)S(1)} %get-tuple-element.215), channel_id=1, source_target_pairs={{0,2},{1,3},{2,0},{3,1},{4,6},{5,7},{6,4},{7,5},{8,10},{9,11},{10,... | collective-permute-start | bytes 1769480 | tf_op jit(solution)/shard_map/ppermute | solution.py:873
  23.1 17.1 %collective-permute-start.8 = (bf16[400,768]{1,0:T(8,128)(2,1)S(1)}, bf16[400,768]{1,0:T(8,128)(2,1)}, u32[]{:S(2)}, u32[]{:S(2)}) collective-permute-start(bf16[400,768]{1,0:T(8,128)(2,1)S(1)} %copy-done.6), channel_id=1, source_target_pairs={{0,1},{1,0},{2,3},{3,2},{4,5},{5,4},{6,7},{7,6},{8,9},{9,8},{10,11... | collective-permute-start | bytes 1843208 | tf_op jit(solution)/shard_map/ppermute | solution.py:869
  30.3 32.8 %collective-permute-start.19 = (bf16[768,768]{1,0:T(8,128)(2,1)}, bf16[768,768]{1,0:T(8,128)(2,1)}, u32[]{:S(2)}, u32[]{:S(2)}) collective-permute-start(bf16[768,768]{1,0:T(8,128)(2,1)} %refs_4_.5), channel_id=1, source_target_pairs={{0,1},{1,0},{2,3},{3,2},{4,5},{5,4},{6,7},{7,6},{8,9},{9,8},{10,11... | collective-permute-start | bytes 3538952 | tf_op jit(solution)/shard_map/ppermute | solution.py:869
  39.6 15.1 %collective-permute-start.14 = (bf16[384,768]{1,0:T(8,128)(2,1)S(1)}, bf16[384,768]{1,0:T(8,128)(2,1)S(1)}, u32[]{:S(2)}, u32[]{:S(2)}) collective-permute-start(bf16[384,768]{1,0:T(8,128)(2,1)S(1)} %collective-permute-done.5.refs_2_.refs_0_), channel_id=1, source_target_pairs={{0,1},{1,0},{2,3},{3,2},{4,5},{5,4},{6,7},{7,6},{8,9},{9,8},{10,11... | collective-permute-start | bytes 1769480 | tf_op jit(solution)/shard_map/ppermute | solution.py:869
  40.9 13.4 %collective-permute-start.13 = (bf16[272,768]{1,0:T(8,128)(2,1)S(1)}, bf16[272,768]{1,0:T(8,128)(2,1)S(1)}, u32[]{:S(2)}, u32[]{:S(2)}) collective-permute-start(bf16[272,768]{1,0:T(8,128)(2,1)S(1)} %copy-done.23), channel_id=1, source_target_pairs={{0,1},{1,0},{2,3},{3,2},{4,5},{5,4},{6,7},{7,6},{8,9},{9,8},{10,11... | collective-permute-start | bytes 1253384 | tf_op jit(solution)/shard_map/ppermute | solution.py:869
  66.8 14.2 %collective-permute-start.24 = (bf16[272,768]{1,0:T(8,128)(2,1)S(1)}, bf16[272,768]{1,0:T(8,128)(2,1)S(1)}, u32[]{:S(2)}, u32[]{:S(2)}) collective-permute-start(bf16[272,768]{1,0:T(8,128)(2,1)S(1)} %get-tuple-element.250.refs_1_), channel_id=1, source_target_pairs={{0,2},{1,3},{2,0},{3,1},{4,6},{5,7},{6,4},{7,5},{8,10},{9,11},{10,... | collective-permute-start | bytes 1253384 | tf_op jit(solution)/shard_map/ppermute | solution.py:873
  81.0 13.0 %collective-permute-start.31 = (bf16[272,768]{1,0:T(8,128)(2,1)S(1)}, bf16[272,768]{1,0:T(8,128)(2,1)S(1)}, u32[]{:S(2)}, u32[]{:S(2)}) collective-permute-start(bf16[272,768]{1,0:T(8,128)(2,1)S(1)} %get-tuple-element.275.refs_1_), channel_id=1, source_target_pairs={{0,2},{1,3},{2,0},{3,1},{4,6},{5,7},{6,4},{7,5},{8,10},{9,11},{10,... | collective-permute-start | bytes 1253384 | tf_op jit(solution)/shard_map/ppermute | solution.py:873
  87.0 17.6 %collective-permute-start.35 = (bf16[384,768]{1,0:T(8,128)(2,1)S(1)}, bf16[384,768]{1,0:T(8,128)(2,1)S(1)}, u32[]{:S(2)}, u32[]{:S(2)}) collective-permute-start(bf16[384,768]{1,0:T(8,128)(2,1)S(1)} %get-tuple-element.289), channel_id=1, source_target_pairs={{0,4},{1,5},{2,6},{3,7},{4,0},{5,1},{6,2},{7,3},{8,12},{9,13},{10,... | collective-permute-start | bytes 1769480 | tf_op jit(solution)/shard_map/ppermute | solution.py:881
  89.7 14.8 %collective-permute-start.36 = (bf16[192,768]{1,0:T(8,128)(2,1)S(1)}, bf16[192,768]{1,0:T(8,128)(2,1)S(1)}, u32[]{:S(2)}, u32[]{:S(2)}) collective-permute-start(bf16[192,768]{1,0:T(8,128)(2,1)S(1)} %get-tuple-element.291), channel_id=1, source_target_pairs={{0,8},{1,17},{2,10},{3,19},{4,12},{5,21},{6,14},{7,23},{8,0},{9,25... | collective-permute-start | bytes 884744 | tf_op jit(solution)/shard_map/ppermute | solution.py:881
  109.5 20.4 %collective-permute-start.37 = (bf16[384,768]{1,0:T(8,128)(2,1)}, bf16[384,768]{1,0:T(8,128)(2,1)S(1)}, u32[]{:S(2)}, u32[]{:S(2)}) collective-permute-start(bf16[384,768]{1,0:T(8,128)(2,1)} %get-tuple-element.296), channel_id=1, source_target_pairs={{0,4},{1,9},{2,6},{3,11},{4,0},{5,13},{6,2},{7,15},{8,12},{9,1},{1... | collective-permute-start | bytes 1769480 | tf_op jit(solution)/shard_map/ppermute | solution.py:881
  120.1 14.4 %collective-permute-start.46 = (bf16[192,768]{1,0:T(8,128)(2,1)S(1)}, bf16[192,768]{1,0:T(8,128)(2,1)S(1)}, u32[]{:S(2)}, u32[]{:S(2)}) collective-permute-start(bf16[192,768]{1,0:T(8,128)(2,1)S(1)} %get-tuple-element.320), channel_id=1, source_target_pairs={{0,1},{1,0},{2,3},{3,2},{4,5},{5,4},{6,7},{7,6},{8,9},{9,8},{10,11... | collective-permute-start | bytes 884744 | tf_op jit(solution)/shard_map/ppermute | solution.py:869
  120.2 14.4 %collective-permute-start.45 = (bf16[208,768]{1,0:T(8,128)(2,1)S(1)}, bf16[208,768]{1,0:T(8,128)(2,1)S(1)}, u32[]{:S(2)}, u32[]{:S(2)}) collective-permute-start(bf16[208,768]{1,0:T(8,128)(2,1)S(1)} %get-tuple-element.319), channel_id=1, source_target_pairs={{0,1},{1,0},{2,3},{3,2},{4,5},{5,4},{6,7},{7,6},{8,9},{9,8},{10,11... | collective-permute-start | bytes 958472 | tf_op jit(solution)/shard_map/ppermute | solution.py:869
  134.6 14.6 %collective-permute-start.50 = (bf16[272,768]{1,0:T(8,128)(2,1)S(1)}, bf16[272,768]{1,0:T(8,128)(2,1)S(1)}, u32[]{:S(2)}, u32[]{:S(2)}) collective-permute-start(bf16[272,768]{1,0:T(8,128)(2,1)S(1)} %copy-done.54), channel_id=1, source_target_pairs={{0,2},{1,3},{2,0},{3,1},{4,6},{5,7},{6,4},{7,5},{8,10},{9,11},{10,... | collective-permute-start | bytes 1253384 | tf_op jit(solution)/shard_map/ppermute | solution.py:873
  141.4 18.9 %collective-permute-start.49 = (bf16[400,768]{1,0:T(8,128)(2,1)S(1)}, bf16[400,768]{1,0:T(8,128)(2,1)S(1)}, u32[]{:S(2)}, u32[]{:S(2)}) collective-permute-start(bf16[400,768]{1,0:T(8,128)(2,1)S(1)} %get-tuple-element.331.refs_0_), channel_id=1, source_target_pairs={{0,2},{1,3},{2,0},{3,1},{4,6},{5,7},{6,4},{7,5},{8,10},{9,11},{10,... | collective-permute-start | bytes 1843208 | tf_op jit(solution)/shard_map/ppermute | solution.py:873
  148.3 23.8 %collective-permute-start.47 = (bf16[272,768]{1,0:T(8,128)(2,1)S(1)}, bf16[272,768]{1,0:T(8,128)(2,1)S(1)}, u32[]{:S(2)}, u32[]{:S(2)}) collective-permute-start(bf16[272,768]{1,0:T(8,128)(2,1)S(1)} %get-tuple-element.329), channel_id=1, source_target_pairs={{0,2},{1,3},{2,0},{3,1},{4,6},{5,7},{6,4},{7,5},{8,10},{9,11},{10,... | collective-permute-start | bytes 1253384 | tf_op jit(solution)/shard_map/ppermute | solution.py:873
  153.3 25.4 %collective-permute-start.57 = (bf16[384,768]{1,0:T(8,128)(2,1)S(1)}, bf16[384,768]{1,0:T(8,128)(2,1)S(1)}, u32[]{:S(2)}, u32[]{:S(2)}) collective-permute-start(bf16[384,768]{1,0:T(8,128)(2,1)S(1)} %get-tuple-element.362.refs_0_), channel_id=1, source_target_pairs={{0,4},{1,9},{2,6},{3,11},{4,0},{5,13},{6,2},{7,15},{8,12},{9,1},{1... | collective-permute-start | bytes 1769480 | tf_op jit(solution)/shard_map/ppermute | solution.py:881
  154.6 13.6 %collective-permute-start.48 = (bf16[96,768]{1,0:T(8,128)(2,1)S(1)}, bf16[96,768]{1,0:T(8,128)(2,1)S(1)}, u32[]{:S(2)}, u32[]{:S(2)}) collective-permute-start(bf16[96,768]{1,0:T(8,128)(2,1)S(1)} %get-tuple-element.330.refs_0_), channel_id=1, source_target_pairs={{0,16},{1,17},{2,18},{3,19},{4,20},{5,21},{6,22},{7,23},{8,24},{9,... | collective-permute-start | bytes 442376 | tf_op jit(solution)/shard_map/ppermute | solution.py:881
  158.5 16.3 %collective-permute-start.59 = (bf16[96,768]{1,0:T(8,128)(2,1)S(1)}, bf16[96,768]{1,0:T(8,128)(2,1)S(1)}, u32[]{:S(2)}, u32[]{:S(2)}) collective-permute-start(bf16[96,768]{1,0:T(8,128)(2,1)S(1)} %get-tuple-element.364.refs_0_), channel_id=1, source_target_pairs={{0,16},{1,17},{2,18},{3,19},{4,20},{5,21},{6,22},{7,23},{8,24},{9,... | collective-permute-start | bytes 442376 | tf_op jit(solution)/shard_map/ppermute | solution.py:881
  175.0 19.7 %collective-permute-start.54 = (bf16[400,768]{1,0:T(8,128)(2,1)S(1)}, bf16[400,768]{1,0:T(8,128)(2,1)S(1)}, u32[]{:S(2)}, u32[]{:S(2)}) collective-permute-start(bf16[400,768]{1,0:T(8,128)(2,1)S(1)} %get-tuple-element.354), channel_id=1, source_target_pairs={{0,2},{1,3},{2,0},{3,1},{4,6},{5,7},{6,4},{7,5},{8,10},{9,11},{10,... | collective-permute-start | bytes 1843208 | tf_op jit(solution)/shard_map/ppermute | solution.py:873
  177.5 14.3 %collective-permute-start.61 = (bf16[384,768]{1,0:T(8,128)(2,1)S(1)}, bf16[384,768]{1,0:T(8,128)(2,1)S(1)}, u32[]{:S(2)}, u32[]{:S(2)}) collective-permute-start(bf16[384,768]{1,0:T(8,128)(2,1)S(1)} %get-tuple-element.370.refs_0_), channel_id=1, source_target_pairs={{0,4},{1,5},{2,6},{3,7},{4,0},{5,1},{6,2},{7,3},{8,12},{9,13},{10,... | collective-permute-start | bytes 1769480 | tf_op jit(solution)/shard_map/ppermute | solution.py:881
  181.7 16.4 %collective-permute-start.64 = (bf16[384,768]{1,0:T(8,128)(2,1)S(1)}, bf16[384,768]{1,0:T(8,128)(2,1)S(1)}, u32[]{:S(2)}, u32[]{:S(2)}) collective-permute-start(bf16[384,768]{1,0:T(8,128)(2,1)S(1)} %get-tuple-element.379.refs_0_), channel_id=1, source_target_pairs={{0,4},{1,9},{2,6},{3,11},{4,0},{5,13},{6,2},{7,15},{8,12},{9,1},{1... | collective-permute-start | bytes 1769480 | tf_op jit(solution)/shard_map/ppermute | solution.py:881
  (103 other events, 571.9 us)
Sparse Core Ops, SparseCore 0:
  39.7 42.8 all-gather.1

commit v4 on v3

--- a/solution.py
+++ b/solution.py
@@ -20,7 +20,7 @@
 PLAN = (
     "fc2_weight", "mlp_sum", "mlp_back0", "fc1_weight", "fc2", "attn_back0", "mlp_back1",
     "attn_back1", "fc2", "fc1", "attn_weights", "p_sums", "image_attn", "fc1", "fc2", "qkv",
-    "image_norm", "fc2", "fc1", "qkv", "branch", "input", "qkv", "fc2", "small_near", "image_mlp",
+    "image_norm", "fc2", "fc1", "branch", "qkv", "input", "qkv", "fc2", "small_near", "image_mlp",
     "fc1", "text_out", "small_side", "qkv", "fc1", "fc2", "small_dp", "qkv", "fc1", "small_dp",
     "image_out", "qkv", "small_dp",
 )

time: 208 us -> 217 us (1.043)
  starting transfers between devices: 46.2 us -> 54.1 us
  waiting for transfers between devices: 51.2 us -> 47.9 us
  Pallas kernels: 81.9 us -> 84.8 us
    ppermute x21, starting transfers between devices: 21.9 us -> 31.2 us  [dp_swap(): return lax.ppermute(x, ('dp', 'mp'), pairs)]
    pallas_call x58, Pallas kernels: 81.9 us -> 84.8 us  [__call__(): pl.pallas_call(run, out_shape=(*(pltpu.HBM(o.shape, o.dtype) if isinstanc...]
    ppermute x21, waiting for transfers between devices: 28.6 us -> 26.1 us  [dp_swap(): return lax.ppermute(x, ('dp', 'mp'), pairs)]
    unnamed x122 -> x120, local copies, waits for them, and re-layouts: 12 us -> 13.3 us
where the time goes in v4:
time: 217 us; the launch traced here: 216 us
  Pallas kernels  84.8 us (39%)
  starting transfers between devices  54.1 us (25%)
  waiting for transfers between devices  47.9 us (22%)
  between operations  15.1 us (7%)
  local copies, waits for them, and re-layouts  14 us (6%)
    pallas_call x58, Pallas kernels, __call__(): pl.pallas_call(run, out_shape=(*(pltpu.HBM(o.shape, o.dtype) if isinstanc...  84.8 us
    ppermute x21, starting transfers between devices, dp_swap(): return lax.ppermute(x, ('dp', 'mp'), pairs)  31.2 us
    ppermute x21, waiting for transfers between devices, dp_swap(): return lax.ppermute(x, ('dp', 'mp'), pairs)  26.1 us
    unnamed x120, local copies, waits for them, and re-layouts  13.3 us
    ppermute x11, waiting for transfers between devices, side_swap(): lax.ppermute(x, 'mp', [(i, i ^ 2) for i in range(lax.axis_size('mp'))])  13.1 us
    ppermute x33, starting transfers between devices, core_swap(): lax.ppermute(x, 'mp', [(i, i ^ 1) for i in range(lax.axis_size('mp'))])  11.4 us
    ppermute x11, starting transfers between devices, side_swap(): lax.ppermute(x, 'mp', [(i, i ^ 2) for i in range(lax.axis_size('mp'))])  11.4 us
    ppermute x33, waiting for transfers between devices, core_swap(): lax.ppermute(x, 'mp', [(i, i ^ 1) for i in range(lax.axis_size('mp'))])  8.67 us
  transfers between devices with their start and end apart: 66, of which 19 were waited for; matrix products, arithmetic and copies ran while one was open for 0% of the time, Pallas kernels for 39%

profile of v4, /device:TPU:0, one launch (start us, length us, event | category | flops | bytes accessed | tf_op | source)
XLA Modules:
  0.0 216.4 jit_solution(18092534322373785178)
XLA Ops:
  7.8 2.6 %collective-permute-start = (bf16[272,768]{1,0:T(8,128)(2,1)}, bf16[272,768]{1,0:T(8,128)(2,1)S(1)}, u32[]{:S(2)}, u32[]{:S(2)}) collective-permute-start(bf16[272,768]{1,0:T(8,128)(2,1)} %refs_0_.19), channel_id=1, source_target_pairs={{0,2},{1,3},{2,0},{3,1},{4,6},{5,7},{6,4},{7,5},{8,10},{9,11},{10,... | collective-permute-start | bytes 1253384 | tf_op jit(solution)/shard_map/ppermute | solution.py:873
  10.9 2.5 %collective-permute-done.2.refs_14_ = bf16[768]{0:T(1024)(128)(2,1)S(1)} collective-permute-done((bf16[768]{0:T(1024)(128)(2,1)}, bf16[768]{0:T(1024)(128)(2,1)S(1)}, u32[]{:S(2)}, u32[]{:S(2)}) %collective-permute-start.2) | collective-permute-done | bytes 1568 | tf_op jit(solution)/shard_map/ppermute | solution.py:869
  24.1 5.2 %shard_map.394 = (bf16[544,768]{1,0:T(8,128)(2,1)}, bf16[3,1088,192]{2,1,0:T(8,128)(2,1)}, bf16[1088,192]{1,0:T(8,128)(2,1)}, bf16[2,272,768]{2,1,0:T(8,128)(2,1...) custom-call(bf16[272,768]{1,0:T(8,128)(2,1)S(1)} %copy-done.12, ...), custom_call_target="tpu_custom_call" | custom-call | flops 1 | bytes 1 | tf_op jit(solution)/shard_map/pallas_call | solution.py:129
  30.6 7.5 %collective-permute-done.5.refs_2_.refs_0_ = bf16[384,768]{1,0:T(8,128)(2,1)S(1)} collective-permute-done((bf16[384,768]{1,0:T(8,128)(2,1)S(1)}, bf16[384,768]{1,0:T(8,128)(2,1)S(1)}, u32[]{:S(2)}, u32[]{:S(2)}) %collective-permute-start.5) | collective-permute-done | bytes 589856 | tf_op jit(solution)/shard_map/ppermute | solution.py:873
  40.9 7.2 %shard_map.397 = (f32[400,768]{1,0:T(8,128)}, bf16[400,768]{1,0:T(8,128)(2,1)}, f32[8,128]{1,0:T(8,128)S(1)}) custom-call(bf16[400,768]{1,0:T(8,128)(2,1)} %refs_0_.18, bf16[400,768]{1,0:T(8,128)(2,1)} %collective-permute-done.8.refs_1_, f32[8,768]{1,0:T(8,128)S(1)} %get-tuple-element.220.refs_2_.refs_3_, bf16[896,768]{1,0:T(8,128)(2,1)} %copy-done.8, ...), custom_call_target="tpu_custom_call" | custom-call | flops 1 | bytes 1 | tf_op jit(solution)/shard_map/pallas_call | solution.py:129
  48.2 3.9 %collective-permute-done.6.refs_2_ = bf16[272,768]{1,0:T(8,128)(2,1)S(1)} collective-permute-done((bf16[272,768]{1,0:T(8,128)(2,1)}, bf16[272,768]{1,0:T(8,128)(2,1)S(1)}, u32[]{:S(2)}, u32[]{:S(2)}) %collective-permute-start.6) | collective-permute-done | bytes 417824 | tf_op jit(solution)/shard_map/ppermute | solution.py:873
  54.9 2.4 %shard_map.400 = (bf16[544,768]{1,0:T(8,128)(2,1)}, bf16[544,768]{1,0:T(8,128)(2,1)}, f32[8,128]{1,0:T(8,128)S(1)}) custom-call(bf16[272,768]{1,0:T(8,128)(2,1)S(1)} %copy-done.23, bf16[272,768]{1,0:T(8,128)(2,1)S(1)} %collective-permute-done.13.refs_1_, bf16[384,768]{1,0:T(8,128)(2,1)S(1)} %collective-permute-done.5.refs_2_.refs_0_, ...), custom_call_target="tpu_custom_call" | custom-call | flops 1 | bytes 1 | tf_op jit(solution)/shard_map/pallas_call | solution.py:129
  58.4 5.1 %shard_map.401 = (bf16[544,768]{1,0:T(8,128)(2,1)}, bf16[544,768]{1,0:T(8,128)(2,1)}, bf16[544,768]{1,0:T(8,128)(2,1)}, bf16[272,768]{1,0:T(8,128)(2,1)}, bf16[2...) custom-call(bf16[272,768]{1,0:T(8,128)(2,1)S(1)} %get-tuple-element., ...), custom_call_target="tpu_custom_call" | custom-call | flops 1 | bytes 1 | tf_op jit(solution)/shard_map/pallas_call | solution.py:129
  69.2 5.1 %shard_map.404 = (bf16[544,768]{1,0:T(8,128)(2,1)}, bf16[544,768]{1,0:T(8,128)(2,1)}, bf16[544,768]{1,0:T(8,128)(2,1)}, bf16[272,768]{1,0:T(8,128)(2,1)}, bf16[2...) custom-call(bf16[272,768]{1,0:T(8,128)(2,1)S(1)} %get-tuple-element., ...), custom_call_target="tpu_custom_call" | custom-call | flops 1 | bytes 1 | tf_op jit(solution)/shard_map/pallas_call | solution.py:129
  75.5 3.2 %shard_map.405 = (bf16[384,768]{1,0:T(8,128)(2,1)S(1)}, bf16[384,768]{1,0:T(8,128)(2,1)S(1)}, f32[1,768]{1,0:T(1,128)S(1)}, f32[8,128]{1,0:T(8,128)S(1)}) custom-call(bf16[544,768]{1,0:T(8,128)(2,1)S(1)} %copy-done.32, bf16[544,768]{1,0:T(8,128)(2,1)S(1)} %copy-done.35, bf16[544,768]{1,0:T(8,128)(2,1)S(1)} %copy-done.4, bf16[544,768]{1,0:T(8,128)(2,1)S(1)} %copy-done.2, ...), custom_call_target="tpu_custom_call" | custom-call | flops 1 | bytes 1 | tf_op jit(solution)/shard_map/pallas_call | solution.py:129
  84.9 3.1 %shard_map.408 = (bf16[384,768]{1,0:T(8,128)(2,1)S(1)}, bf16[384,768]{1,0:T(8,128)(2,1)S(1)}, f32[1,768]{1,0:T(1,128)S(1)}, f32[8,128]{1,0:T(8,128)S(1)}) custom-call(bf16[544,768]{1,0:T(8,128)(2,1)S(1)} %copy-done.30, bf16[544,768]{1,0:T(8,128)(2,1)S(1)} %copy-done.33, bf16[544,768]{1,0:T(8,128)(2,1)S(1)} %copy-done.31, bf16[544,768]{1,0:T(8,128)(2,1)S(1)} %copy-done.34, ...), custom_call_target="tpu_custom_call" | custom-call | flops 1 | bytes 1 | tf_op jit(solution)/shard_map/pallas_call | solution.py:129
  91.3 3.5 %shard_map.410 = (bf16[544,768]{1,0:T(8,128)(2,1)S(1)}, bf16[544,192]{1,0:T(8,128)(2,1)S(1)}, bf16[3,512,192]{2,1,0:T(8,128)(2,1)S(1)}, f32[8,128]{1,0:T(8,128)S(1)}) custom-call(bf16[272,768]{1,0:T(8,128)(2,1)S(1)} %get-tuple-element.272.refs_0_, bf16[96,768]{1,0:T(8,128)(2,1)S(1)} %collective-permute-done.31.refs_1_, ...), custom_call_target="tpu_custom_call" | custom-call | flops 1 | bytes 1 | tf_op jit(solution)/shard_map/pallas_call | solution.py:129
  98.4 5.0 %shard_map.412 = (bf16[544,768]{1,0:T(8,128)(2,1)S(1)}, bf16[3,1088,192]{2,1,0:T(8,128)(2,1)S(1)}, bf16[272,768]{1,0:T(8,128)(2,1)S(1)}, bf16[272,768]{1,0:T(8,1...) custom-call(bf16[272,768]{1,0:T(8,128)(2,1)S(1)} %get-tuple-element.279.refs_0_, ...), custom_call_target="tpu_custom_call" | custom-call | flops 1 | bytes 1 | tf_op jit(solution)/shard_map/pallas_call | solution.py:129
  107.2 4.0 %shard_map.415 = (bf16[384,768]{1,0:T(8,128)(2,1)S(1)}, bf16[384,768]{1,0:T(8,128)(2,1)}, f32[1,768]{1,0:T(1,128)S(1)}, f32[2,192]{1,0:T(2,128)S(1)}, f32[8,128]{1,0:T(8,128)S(1)}) custom-call(bf16[1088,192]{1,0:T(8,128)(2,1)S(1)} %copy-done.36, bf16[544,768]{1,0:T(8,128)(2,1)S(1)} %get-tuple-element.298.refs_1_, ...), custom_call_target="tpu_custom_call" | custom-call | flops 1 | bytes 1 | tf_op jit(solution)/shard_map/pallas_call | solution.py:129
  119.1 6.6 %shard_map.417 = (f32[400,768]{1,0:T(8,128)S(1)}, bf16[208,768]{1,0:T(8,128)(2,1)S(1)}, bf16[192,768]{1,0:T(8,128)(2,1)S(1)}, f32[8,128]{1,0:T(8,128)S(1)}) custom-call(bf16[400,768]{1,0:T(8,128)(2,1)} %refs_0_.18, bf16[400,768]{1,0:T(8,128)(2,1)} %collective-permute-done.8.refs_1_, f32[8,768]{1,0:T(8,128)S(1)} %get-tuple-element.220.refs_2_.refs_3_, ...), custom_call_target="tpu_custom_call" | custom-call | flops 1 | bytes 1 | tf_op jit(solution)/shard_map/pallas_call | solution.py:129
  126.9 2.8 %collective-permute-start.23 = (bf16[272,768]{1,0:T(8,128)(2,1)S(1)}, bf16[272,768]{1,0:T(8,128)(2,1)S(1)}, u32[]{:S(2)}, u32[]{:S(2)}) collective-permute-start(bf16[272,768]{1,0:T(8,128)(2,1)S(1)} %copy-done.59), channel_id=1, source_target_pairs={{0,1},{1,0},{2,3},{3,2},{4,5},{5,4},{6,7},{7,6},{8,9},{9,8},{10,11... | collective-permute-start | bytes 1253384 | tf_op jit(solution)/shard_map/ppermute | solution.py:869
  137.8 4.7 %collective-permute-done.42.refs_1_ = bf16[96,768]{1,0:T(8,128)(2,1)S(1)} collective-permute-done((bf16[96,768]{1,0:T(8,128)(2,1)S(1)}, bf16[96,768]{1,0:T(8,128)(2,1)S(1)}, u32[]{:S(2)}, u32[]{:S(2)}) %collective-permute-start.42) | collective-permute-done | bytes 147488 | tf_op jit(solution)/shard_map/ppermute | solution.py:881
  143.1 2.6 %collective-permute-done.40.refs_1_ = bf16[96,768]{1,0:T(8,128)(2,1)S(1)} collective-permute-done((bf16[96,768]{1,0:T(8,128)(2,1)S(1)}, bf16[96,768]{1,0:T(8,128)(2,1)S(1)}, u32[]{:S(2)}, u32[]{:S(2)}) %collective-permute-start.40) | collective-permute-done | bytes 147488 | tf_op jit(solution)/shard_map/ppermute | solution.py:881
  145.7 3.7 %collective-permute-start.52 = (bf16[192,768]{1,0:T(8,128)(2,1)S(1)}, bf16[192,768]{1,0:T(8,128)(2,1)S(1)}, u32[]{:S(2)}, u32[]{:S(2)}) collective-permute-start(bf16[192,768]{1,0:T(8,128)(2,1)S(1)} %get-tuple-element.342.refs_0_), channel_id=1, source_target_pairs={{0,8},{1,17},{2,10},{3,19},{4,12},{5,21},{6,14},{7,23},{8,0},{9,25... | collective-permute-start | bytes 884744 | tf_op jit(solution)/shard_map/ppermute | solution.py:881
  153.7 3.4 %collective-permute-start.53 = (bf16[96,768]{1,0:T(8,128)(2,1)S(1)}, bf16[96,768]{1,0:T(8,128)(2,1)S(1)}, u32[]{:S(2)}, u32[]{:S(2)}) collective-permute-start(bf16[96,768]{1,0:T(8,128)(2,1)S(1)} %get-tuple-element.344), channel_id=1, source_target_pairs={{0,16},{1,17},{2,18},{3,19},{4,20},{5,21},{6,22},{7,23},{8,24},{9,... | collective-permute-start | bytes 442376 | tf_op jit(solution)/shard_map/ppermute | solution.py:881
  159.7 3.0 %collective-permute-done.53.refs_1_ = bf16[96,768]{1,0:T(8,128)(2,1)S(1)} collective-permute-done((bf16[96,768]{1,0:T(8,128)(2,1)S(1)}, bf16[96,768]{1,0:T(8,128)(2,1)S(1)}, u32[]{:S(2)}, u32[]{:S(2)}) %collective-permute-start.53) | collective-permute-done | bytes 147488 | tf_op jit(solution)/shard_map/ppermute | solution.py:881
  162.8 2.2 %collective-permute-start.57 = (bf16[384,768]{1,0:T(8,128)(2,1)S(1)}, bf16[384,768]{1,0:T(8,128)(2,1)S(1)}, u32[]{:S(2)}, u32[]{:S(2)}) collective-permute-start(bf16[384,768]{1,0:T(8,128)(2,1)S(1)} %get-tuple-element.362.refs_0_), channel_id=1, source_target_pairs={{0,4},{1,9},{2,6},{3,11},{4,0},{5,13},{6,2},{7,15},{8,12},{9,1},{1... | collective-permute-start | bytes 1769480 | tf_op jit(solution)/shard_map/ppermute | solution.py:881
  169.1 8.0 %shard_map.432 = (bf16[400,768]{1,0:T(8,128)(2,1)S(1)}, bf16[400,768]{1,0:T(8,128)(2,1)S(1)}, f32[8,128]{1,0:T(8,128)S(1)}) custom-call(bf16[400,768]{1,0:T(8,128)(2,1)S(1)} %get-tuple-element.328.refs_0_, bf16[400,768]{1,0:T(8,128)(2,1)S(1)} %collective-permute-done.48.refs_1_, f32[8,768]{1,0:T(8,128)S(1)} %get-tuple-element.220.refs_2_.refs_3_, ...), custom_call_target="tpu_custom_call" | custom-call | flops 1 | bytes 1 | tf_op jit(solution)/shard_map/pallas_call | solution.py:129
  190.5 9.9 %collective-permute-done.61.refs_1_ = bf16[384,768]{1,0:T(8,128)(2,1)S(1)} collective-permute-done((bf16[384,768]{1,0:T(8,128)(2,1)S(1)}, bf16[384,768]{1,0:T(8,128)(2,1)S(1)}, u32[]{:S(2)}, u32[]{:S(2)}) %collective-permute-start.61) | collective-permute-done | bytes 589856 | tf_op jit(solution)/shard_map/ppermute | solution.py:881
  (290 shorter events, 94.3 us)
Async XLA Ops:
  7.2 111.9 %all-gather.2.cloned.1.call-start = ((), (), s32[]{:S(2)}) async-start(), calls=%async_computation | async-start | bytes 1548288 | tf_op jit(solution)/shard_map/all_gather | solution.py:1037
  7.8 13.5 %collective-permute-start = (bf16[272,768]{1,0:T(8,128)(2,1)}, bf16[272,768]{1,0:T(8,128)(2,1)S(1)}, u32[]{:S(2)}, u32[]{:S(2)}) collective-permute-start(bf16[272,768]{1,0:T(8,128)(2,1)} %refs_0_.19), channel_id=1, source_target_pairs={{0,2},{1,3},{2,0},{3,1},{4,6},{5,7},{6,4},{7,5},{8,10},{9,11},{10,... | collective-permute-start | bytes 1253384 | tf_op jit(solution)/shard_map/ppermute | solution.py:873
  10.4 30.5 %collective-permute-start.9 = (bf16[768,768]{1,0:T(8,128)(2,1)}, bf16[768,768]{1,0:T(8,128)(2,1)}, u32[]{:S(2)}, u32[]{:S(2)}) collective-permute-start(bf16[768,768]{1,0:T(8,128)(2,1)} %refs_3_.3), channel_id=1, source_target_pairs={{0,1},{1,0},{2,3},{3,2},{4,5},{5,4},{6,7},{7,6},{8,9},{9,8},{10,11... | collective-permute-start | bytes 3538952 | tf_op jit(solution)/shard_map/ppermute | solution.py:869
  22.5 15.5 %collective-permute-start.5 = (bf16[384,768]{1,0:T(8,128)(2,1)S(1)}, bf16[384,768]{1,0:T(8,128)(2,1)S(1)}, u32[]{:S(2)}, u32[]{:S(2)}) collective-permute-start(bf16[384,768]{1,0:T(8,128)(2,1)S(1)} %get-tuple-element.215), channel_id=1, source_target_pairs={{0,2},{1,3},{2,0},{3,1},{4,6},{5,7},{6,4},{7,5},{8,10},{9,11},{10,... | collective-permute-start | bytes 1769480 | tf_op jit(solution)/shard_map/ppermute | solution.py:873
  23.1 17.1 %collective-permute-start.8 = (bf16[400,768]{1,0:T(8,128)(2,1)S(1)}, bf16[400,768]{1,0:T(8,128)(2,1)}, u32[]{:S(2)}, u32[]{:S(2)}) collective-permute-start(bf16[400,768]{1,0:T(8,128)(2,1)S(1)} %copy-done.6), channel_id=1, source_target_pairs={{0,1},{1,0},{2,3},{3,2},{4,5},{5,4},{6,7},{7,6},{8,9},{9,8},{10,11... | collective-permute-start | bytes 1843208 | tf_op jit(solution)/shard_map/ppermute | solution.py:869
  30.3 33.8 %collective-permute-start.19 = (bf16[768,768]{1,0:T(8,128)(2,1)}, bf16[768,768]{1,0:T(8,128)(2,1)}, u32[]{:S(2)}, u32[]{:S(2)}) collective-permute-start(bf16[768,768]{1,0:T(8,128)(2,1)} %refs_4_.5), channel_id=1, source_target_pairs={{0,1},{1,0},{2,3},{3,2},{4,5},{5,4},{6,7},{7,6},{8,9},{9,8},{10,11... | collective-permute-start | bytes 3538952 | tf_op jit(solution)/shard_map/ppermute | solution.py:869
  38.1 16.7 %collective-permute-start.14 = (bf16[384,768]{1,0:T(8,128)(2,1)S(1)}, bf16[384,768]{1,0:T(8,128)(2,1)}, u32[]{:S(2)}, u32[]{:S(2)}) collective-permute-start(bf16[384,768]{1,0:T(8,128)(2,1)S(1)} %collective-permute-done.5.refs_2_.refs_0_), channel_id=1, source_target_pairs={{0,1},{1,0},{2,3},{3,2},{4,5},{5,4},{6,7},{7,6},{8,9},{9,8},{10,11... | collective-permute-start | bytes 1769480 | tf_op jit(solution)/shard_map/ppermute | solution.py:869
  40.9 13.4 %collective-permute-start.13 = (bf16[272,768]{1,0:T(8,128)(2,1)S(1)}, bf16[272,768]{1,0:T(8,128)(2,1)S(1)}, u32[]{:S(2)}, u32[]{:S(2)}) collective-permute-start(bf16[272,768]{1,0:T(8,128)(2,1)S(1)} %copy-done.23), channel_id=1, source_target_pairs={{0,1},{1,0},{2,3},{3,2},{4,5},{5,4},{6,7},{7,6},{8,9},{9,8},{10,11... | collective-permute-start | bytes 1253384 | tf_op jit(solution)/shard_map/ppermute | solution.py:869
  67.8 14.2 %collective-permute-start.24 = (bf16[272,768]{1,0:T(8,128)(2,1)S(1)}, bf16[272,768]{1,0:T(8,128)(2,1)S(1)}, u32[]{:S(2)}, u32[]{:S(2)}) collective-permute-start(bf16[272,768]{1,0:T(8,128)(2,1)S(1)} %get-tuple-element.253.refs_1_), channel_id=1, source_target_pairs={{0,2},{1,3},{2,0},{3,1},{4,6},{5,7},{6,4},{7,5},{8,10},{9,11},{10,... | collective-permute-start | bytes 1253384 | tf_op jit(solution)/shard_map/ppermute | solution.py:873
  88.1 18.3 %collective-permute-start.27 = (bf16[384,768]{1,0:T(8,128)(2,1)S(1)}, bf16[384,768]{1,0:T(8,128)(2,1)S(1)}, u32[]{:S(2)}, u32[]{:S(2)}) collective-permute-start(bf16[384,768]{1,0:T(8,128)(2,1)S(1)} %get-tuple-element.264), channel_id=1, source_target_pairs={{0,4},{1,5},{2,6},{3,7},{4,0},{5,1},{6,2},{7,3},{8,12},{9,13},{10,... | collective-permute-start | bytes 1769480 | tf_op jit(solution)/shard_map/ppermute | solution.py:881
  103.4 14.0 %collective-permute-start.38 = (bf16[272,768]{1,0:T(8,128)(2,1)S(1)}, bf16[272,768]{1,0:T(8,128)(2,1)S(1)}, u32[]{:S(2)}, u32[]{:S(2)}) collective-permute-start(bf16[272,768]{1,0:T(8,128)(2,1)S(1)} %get-tuple-element.294), channel_id=1, source_target_pairs={{0,1},{1,0},{2,3},{3,2},{4,5},{5,4},{6,7},{7,6},{8,9},{9,8},{10,11... | collective-permute-start | bytes 1253384 | tf_op jit(solution)/shard_map/ppermute | solution.py:869
  111.2 20.5 %collective-permute-start.45 = (bf16[384,768]{1,0:T(8,128)(2,1)}, bf16[384,768]{1,0:T(8,128)(2,1)S(1)}, u32[]{:S(2)}, u32[]{:S(2)}) collective-permute-start(bf16[384,768]{1,0:T(8,128)(2,1)} %get-tuple-element.317), channel_id=1, source_target_pairs={{0,4},{1,9},{2,6},{3,11},{4,0},{5,13},{6,2},{7,15},{8,12},{9,1},{1... | collective-permute-start | bytes 1769480 | tf_op jit(solution)/shard_map/ppermute | solution.py:881
  117.3 16.2 %collective-permute-start.15 = (bf16[272,768]{1,0:T(8,128)(2,1)}, bf16[272,768]{1,0:T(8,128)(2,1)}, u32[]{:S(2)}, u32[]{:S(2)}) collective-permute-start(bf16[272,768]{1,0:T(8,128)(2,1)} %get-tuple-element.233), channel_id=1, source_target_pairs={{0,1},{1,0},{2,3},{3,2},{4,5},{5,4},{6,7},{7,6},{8,9},{9,8},{10,11... | collective-permute-start | bytes 1253384 | tf_op jit(solution)/shard_map/ppermute | solution.py:869
  126.9 22.4 %collective-permute-start.23 = (bf16[272,768]{1,0:T(8,128)(2,1)S(1)}, bf16[272,768]{1,0:T(8,128)(2,1)S(1)}, u32[]{:S(2)}, u32[]{:S(2)}) collective-permute-start(bf16[272,768]{1,0:T(8,128)(2,1)S(1)} %copy-done.59), channel_id=1, source_target_pairs={{0,1},{1,0},{2,3},{3,2},{4,5},{5,4},{6,7},{7,6},{8,9},{9,8},{10,11... | collective-permute-start | bytes 1253384 | tf_op jit(solution)/shard_map/ppermute | solution.py:869
  133.6 20.1 %collective-permute-start.50 = (bf16[192,768]{1,0:T(8,128)(2,1)S(1)}, bf16[192,768]{1,0:T(8,128)(2,1)S(1)}, u32[]{:S(2)}, u32[]{:S(2)}) collective-permute-start(bf16[192,768]{1,0:T(8,128)(2,1)S(1)} %get-tuple-element.336), channel_id=1, source_target_pairs={{0,8},{1,5},{2,10},{3,7},{4,12},{5,1},{6,14},{7,3},{8,0},{9,13},{1... | collective-permute-start | bytes 884744 | tf_op jit(solution)/shard_map/ppermute | solution.py:881
  135.4 22.7 %collective-permute-start.49 = (bf16[272,768]{1,0:T(8,128)(2,1)S(1)}, bf16[272,768]{1,0:T(8,128)(2,1)S(1)}, u32[]{:S(2)}, u32[]{:S(2)}) collective-permute-start(bf16[272,768]{1,0:T(8,128)(2,1)S(1)} %copy-done.56), channel_id=1, source_target_pairs={{0,2},{1,3},{2,0},{3,1},{4,6},{5,7},{6,4},{7,5},{8,10},{9,11},{10,... | collective-permute-start | bytes 1253384 | tf_op jit(solution)/shard_map/ppermute | solution.py:873
  142.5 26.6 %collective-permute-start.48 = (bf16[400,768]{1,0:T(8,128)(2,1)S(1)}, bf16[400,768]{1,0:T(8,128)(2,1)S(1)}, u32[]{:S(2)}, u32[]{:S(2)}) collective-permute-start(bf16[400,768]{1,0:T(8,128)(2,1)S(1)} %get-tuple-element.328.refs_0_), channel_id=1, source_target_pairs={{0,2},{1,3},{2,0},{3,1},{4,6},{5,7},{6,4},{7,5},{8,10},{9,11},{10,... | collective-permute-start | bytes 1843208 | tf_op jit(solution)/shard_map/ppermute | solution.py:873
  145.7 17.0 %collective-permute-start.52 = (bf16[192,768]{1,0:T(8,128)(2,1)S(1)}, bf16[192,768]{1,0:T(8,128)(2,1)S(1)}, u32[]{:S(2)}, u32[]{:S(2)}) collective-permute-start(bf16[192,768]{1,0:T(8,128)(2,1)S(1)} %get-tuple-element.342.refs_0_), channel_id=1, source_target_pairs={{0,8},{1,17},{2,10},{3,19},{4,12},{5,21},{6,14},{7,23},{8,0},{9,25... | collective-permute-start | bytes 884744 | tf_op jit(solution)/shard_map/ppermute | solution.py:881
  157.2 21.4 %collective-permute-start.46 = (bf16[272,768]{1,0:T(8,128)(2,1)S(1)}, bf16[272,768]{1,0:T(8,128)(2,1)S(1)}, u32[]{:S(2)}, u32[]{:S(2)}) collective-permute-start(bf16[272,768]{1,0:T(8,128)(2,1)S(1)} %get-tuple-element.326), channel_id=1, source_target_pairs={{0,2},{1,3},{2,0},{3,1},{4,6},{5,7},{6,4},{7,5},{8,10},{9,11},{10,... | collective-permute-start | bytes 1253384 | tf_op jit(solution)/shard_map/ppermute | solution.py:873
  162.8 23.4 %collective-permute-start.57 = (bf16[384,768]{1,0:T(8,128)(2,1)S(1)}, bf16[384,768]{1,0:T(8,128)(2,1)S(1)}, u32[]{:S(2)}, u32[]{:S(2)}) collective-permute-start(bf16[384,768]{1,0:T(8,128)(2,1)S(1)} %get-tuple-element.362.refs_0_), channel_id=1, source_target_pairs={{0,4},{1,9},{2,6},{3,11},{4,0},{5,13},{6,2},{7,15},{8,12},{9,1},{1... | collective-permute-start | bytes 1769480 | tf_op jit(solution)/shard_map/ppermute | solution.py:881
  167.9 13.4 %collective-permute-start.59 = (bf16[96,768]{1,0:T(8,128)(2,1)S(1)}, bf16[96,768]{1,0:T(8,128)(2,1)S(1)}, u32[]{:S(2)}, u32[]{:S(2)}) collective-permute-start(bf16[96,768]{1,0:T(8,128)(2,1)S(1)} %get-tuple-element.364.refs_0_), channel_id=1, source_target_pairs={{0,16},{1,17},{2,18},{3,19},{4,20},{5,21},{6,22},{7,23},{8,24},{9,... | collective-permute-start | bytes 442376 | tf_op jit(solution)/shard_map/ppermute | solution.py:881
  183.1 20.8 %collective-permute-start.54 = (bf16[400,768]{1,0:T(8,128)(2,1)S(1)}, bf16[400,768]{1,0:T(8,128)(2,1)S(1)}, u32[]{:S(2)}, u32[]{:S(2)}) collective-permute-start(bf16[400,768]{1,0:T(8,128)(2,1)S(1)} %get-tuple-element.354), channel_id=1, source_target_pairs={{0,2},{1,3},{2,0},{3,1},{4,6},{5,7},{6,4},{7,5},{8,10},{9,11},{10,... | collective-permute-start | bytes 1843208 | tf_op jit(solution)/shard_map/ppermute | solution.py:873
  186.1 14.4 %collective-permute-start.61 = (bf16[384,768]{1,0:T(8,128)(2,1)S(1)}, bf16[384,768]{1,0:T(8,128)(2,1)S(1)}, u32[]{:S(2)}, u32[]{:S(2)}) collective-permute-start(bf16[384,768]{1,0:T(8,128)(2,1)S(1)} %get-tuple-element.370.refs_0_), channel_id=1, source_target_pairs={{0,4},{1,5},{2,6},{3,7},{4,0},{5,1},{6,2},{7,3},{8,12},{9,13},{10,... | collective-permute-start | bytes 1769480 | tf_op jit(solution)/shard_map/ppermute | solution.py:881
  189.2 17.5 %collective-permute-start.64 = (bf16[384,768]{1,0:T(8,128)(2,1)S(1)}, bf16[384,768]{1,0:T(8,128)(2,1)S(1)}, u32[]{:S(2)}, u32[]{:S(2)}) collective-permute-start(bf16[384,768]{1,0:T(8,128)(2,1)S(1)} %get-tuple-element.379.refs_0_), channel_id=1, source_target_pairs={{0,4},{1,9},{2,6},{3,11},{4,0},{5,13},{6,2},{7,15},{8,12},{9,1},{1... | collective-permute-start | bytes 1769480 | tf_op jit(solution)/shard_map/ppermute | solution.py:881
  (102 other events, 575.8 us)
Sparse Core Ops, SparseCore 0:
  39.8 42.9 all-gather.1
